TPU v7x, 32 devices: a whole 2x2x4 slice. The times are simulated.
32 devices in a mesh: layers: 2 (over y), expert: 16 (over z, x, core).
Axes of the slice: x: 2, y: 2, z: 4, core: 2. Of those that a mesh axis runs over, the one named last changes fastest.
Arguments:
- gate_codes: bfloat16 [32, 2048, 768], P(('layers', 'expert')), parts along dimension 0, may hold values from -4 to 4
- up_codes: bfloat16 [32, 2048, 768], P(('layers', 'expert')), parts along dimension 0, may hold values from -4 to 4
- gate_scale: bfloat16 [32, 16, 6], P(('layers', 'expert')), parts along dimension 0, may hold values from 0.25 to 4
- up_scale: bfloat16 [32, 16, 6], P(('layers', 'expert')), parts along dimension 0, may hold values from 0.25 to 4
- pairs: int32 [16, 2], P('layers'), parts along dimension 0, may hold values from 0 to 15, as said below
- counts: int32 [32], P('layers'), parts along dimension 0, may hold values from 64 to 1023
- unit_order: int32 [16, 768], P('layers'), parts along dimension 0, may hold values from 0 to 767, each once within a row
- owners: int32 [96, 1], P('layers'), parts along dimension 0, may hold values from 0 to 15; in each aligned block of 48 rows (0 to 47, 48 to 95, ...) at most 6 rows name the same one
Outputs:
- merged: bfloat16 [192, 256, 2048], P(('layers', 'expert')), parts along dimension 0
- similarity: float32 [16, 768], P('layers'), parts along dimension 0
There are 2 independent parts, one for each index of `layers`. A program takes and returns all parts, laid end to end along the dimension named above; each array names one. Nothing has to cross between parts.
Inputs may be any that keep to these rules, and one draw needn't show every extreme that they name: `pairs`: every expert appears in exactly one pair. `owners`: at most 6 pieces have the same owner, and some owner has exactly 6.
All inputs are finite; a program needn't handle non-finite values.
Results may differ from a plain program's by a relative error of at most 0.005.
Values may be sent and summed in bfloat16 or wider, within the bound.
No kernel may reach another device: no remote copies, remote signals or barrier semaphores. Data moves between devices by JAX's collectives and lax.ppermute only.
A program may use at most 128 MiB of HBM per device.

v0:
```python
import math

import jax
import jax.numpy as jnp
from jax import lax
from jax.sharding import PartitionSpec as P

D = 2048
FF = 768
BLK = 128
U = 128
CAP = 6


epsilon = 1e-06


def dequantize(codes, scale):
    spread = jnp.repeat(jnp.repeat(scale.astype(jnp.float32), BLK, axis=1), BLK, axis=2)
    return (codes.astype(jnp.float32) * spread).astype(jnp.bfloat16)


def slot_rows(owners):
    owner_ids = owners[:, 0]
    count = owner_ids.shape[0]
    matches = owner_ids[:, None] == owner_ids[None, :]
    earlier = jnp.arange(count)[None, :] < jnp.arange(count)[:, None]
    slot_rank = jnp.sum(jnp.where(matches & earlier, 1, 0), axis=1).astype(jnp.int32)
    return owner_ids * CAP + slot_rank


def own_order(pairs, unit_order, width):
    device_id = lax.axis_index("expert")
    is_right = pairs[:, 1] == device_id
    picked = jnp.sum(jnp.where(is_right[:, None], unit_order, 0), axis=0)
    identity = jnp.arange(width, dtype=jnp.int32)
    return jnp.where(jnp.any(is_right), picked, identity)


def body(gate_codes, up_codes, gate_scale, up_scale, pairs, counts, unit_order, owners):
    devices = lax.axis_size("expert")
    width_units = gate_codes.shape[2]
    order = own_order(pairs, unit_order, width_units)
    gate_values = jnp.take(dequantize(gate_codes, gate_scale), order, axis=2)
    up_values = jnp.take(dequantize(up_codes, up_scale), order, axis=2)
    gate_rows, up_rows = (
        lax.all_to_all(gate_values, "expert", split_axis=1, concat_axis=0, tiled=True),
        lax.all_to_all(up_values, "expert", split_axis=1, concat_axis=0, tiled=True),
    )
    left_ids = pairs[:, 0]
    right_ids = pairs[:, 1]
    left_gate = jnp.take(gate_rows, left_ids, axis=0).astype(jnp.float32)
    left_up = jnp.take(up_rows, left_ids, axis=0).astype(jnp.float32)
    right_gate = jnp.take(gate_rows, right_ids, axis=0).astype(jnp.float32)
    right_up = jnp.take(up_rows, right_ids, axis=0).astype(jnp.float32)
    intersection_part = jnp.sum(left_gate * right_gate + left_up * right_up, axis=1)
    own_gate = gate_values.astype(jnp.float32)
    own_up = up_values.astype(jnp.float32)
    own_norms = jnp.sum(own_gate * own_gate + own_up * own_up, axis=1)
    all_norms = lax.all_gather(own_norms, "expert", axis=0, tiled=True)
    intersection = lax.psum(intersection_part, "expert")
    left_norm = jnp.take(all_norms, left_ids, axis=0)
    right_norm = jnp.take(all_norms, right_ids, axis=0)
    similarity = (
        intersection * math.sqrt(2.0 * D) / jnp.sqrt((left_norm + epsilon) * (right_norm + epsilon))
    )
    left_freq = jnp.take(counts, left_ids, axis=0).astype(jnp.float32)[:, None]
    right_freq = jnp.take(counts, right_ids, axis=0).astype(jnp.float32)[:, None]
    share = (right_freq * jax.nn.sigmoid(similarity))[:, None, :]
    total = left_freq[:, :, None] + share
    merged_gate = ((left_freq[:, :, None] * left_gate + share * right_gate) / total).astype(
        jnp.bfloat16
    )
    merged_up = ((left_freq[:, :, None] * left_up + share * right_up) / total).astype(jnp.bfloat16)
    pair_count = merged_gate.shape[0]
    width_rows = merged_gate.shape[1]
    joined = jnp.stack((merged_gate, merged_up), axis=-1)
    joined = joined.reshape(pair_count, width_rows, FF // U, 2 * U).transpose(0, 2, 1, 3)
    joined = joined.reshape(pair_count * (FF // U), width_rows, 2 * U)
    outgoing = (
        jnp.zeros((devices * CAP, width_rows, 2 * U), jnp.bfloat16)
        .at[slot_rows(owners)]
        .set(joined)
    )
    outgoing = outgoing.reshape(devices, CAP, width_rows, 2 * U)
    arrived = lax.all_to_all(outgoing, "expert", split_axis=0, concat_axis=2, tiled=True)
    return (arrived[0].transpose(0, 2, 1), similarity)


def solution(mesh):
    in_specs = (
        P(("layers", "expert"), None, None),
        P(("layers", "expert"), None, None),
        P(("layers", "expert"), None, None),
        P(("layers", "expert"), None, None),
        P("layers", None),
        P("layers"),
        P("layers", None),
        P("layers", None),
    )
    out_specs = (P(("layers", "expert"), None, None), P("layers", None))
    return jax.shard_map(body, mesh=mesh, in_specs=in_specs, out_specs=out_specs, check_vma=False)
```

profile of v0, /device:TPU:0, one launch (start us, length us, event | category | flops | bytes accessed | tf_op | source)
XLA Modules:
  0.0 523.4 jit_solution(12695638725712984197)
XLA Ops:
  0.6 0.0 copy-start
  0.7 0.7 compare_bitcast_fusion
  1.3 1.4 compare_and_fusion.1
  2.7 0.8 select_reduce_fusion
  3.6 0.7 compare_and_fusion
  4.2 0.7 bitcast_convert_fusion.1
  4.9 0.7 bitcast_convert_fusion
  5.6 0.1 broadcast_bitcast_fusion
  5.7 0.1 broadcast_bitcast_fusion.1
  5.8 0.0 copy-start.2
  5.8 4.8 copy.47
  10.6 0.0 copy-done.2
  10.6 3.0 copy.49
  13.6 2.7 fusion.1
  16.3 4.2 gather_fusion.1
  20.5 2.7 fusion
  23.2 4.3 gather_fusion.5
  27.5 5.2 add_reduce_fusion
  32.7 10.8 %copy.48 = bf16[1,2048,768]{2,0,1:T(2,128)(2,1)} copy(bf16[1,2048,768]{1,2,0:T(8,128)(2,1)S(1)} %get-tuple-element.22) | data formatting | bytes 6291456 | tf_op jit(solution)/shard_map/jit(_take)/select_n | solution.py:44
  43.5 0.5 broadcast.199
  44.0 31.6 %reduce.1 = bf16[2048,768]{1,0:T(8,128)(2,1)S(1)} reduce(bf16[2048,1,768]{2,1,0:T(2,128)(2,1)} %bitcast.84, bf16[]{:T(256)} %broadcast.199), dimensions={1}, to_apply=%bitcast.69.reduce_sub_computation | reduce | bytes 6291458
  75.6 3.6 reshape.233
  79.2 7.4 %all-to-all-start = ((bf16[16,2,49152]{2,1,0:T(2,128)(2,1)}), bf16[16,2,49152]{2,1,0:T(2,128)(2,1)S(1)}, u32[]{:S(2)}, u32[]{:S(2)}) async-start(bf16[16,2,49152]{2,1,0:T(2,128)(2,1)} %reshape.233), calls=%async_computation | async-start | bytes 6291456 | tf_op jit(solution)/shard_map/all_to_all | solution.py:47
  86.6 15.5 %copy.50 = bf16[1,2048,768]{2,0,1:T(2,128)(2,1)} copy(bf16[1,2048,768]{1,2,0:T(8,128)(2,1)} %get-tuple-element.23) | data formatting | bytes 6291456 | tf_op jit(solution)/shard_map/jit(_take)/select_n | solution.py:45
  102.1 33.3 %reduce.2 = bf16[2048,768]{1,0:T(8,128)(2,1)} reduce(bf16[2048,1,768]{2,1,0:T(2,128)(2,1)} %bitcast.85, bf16[]{:T(256)} %broadcast.199), dimensions={1}, to_apply=%bitcast.71.reduce_sub_computation | reduce | bytes 6291458
  135.4 6.3 %reshape.235 = bf16[16,2,49152]{2,1,0:T(2,128)(2,1)} reshape(bf16[2048,768]{1,0:T(8,128)(2,1)} %reduce.2) | data formatting | bytes 6291456
  141.7 0.0 copy-start.3
  141.7 4.2 all-to-all-done
  145.9 15.5 %all-to-all-start.1 = ((bf16[16,2,49152]{2,1,0:T(2,128)(2,1)}), bf16[16,2,49152]{2,1,0:T(2,128)(2,1)}, u32[]{:S(2)}, u32[]{:S(2)}) async-start(bf16[16,2,49152]{2,1,0:T(2,128)(2,1)} %reshape.235), calls=%async_computation.1 | async-start | bytes 6291456 | tf_op jit(solution)/shard_map/all_to_all | solution.py:48
  161.4 0.0 copy-done
  161.5 0.6 gather_fusion.3
  162.1 0.6 gather_fusion
  162.8 66.2 %all-gather.1 = f32[16,1,768]{2,1,0:T(1,128)S(1)} all-gather(f32[1,1,768]{2,1,0:T(1,128)S(1)} %reshape.206), channel_id=2, replica_groups=mesh['layers'=2,'expert'=16] {'expert'}, dimensions={0}, use_global_device_ids=true | all-gather | bytes 52224 | tf_op jit(solution)/shard_map/all_gather | solution.py:60
  229.0 0.6 gather_fusion.9
  229.6 0.6 gather_fusion.8
  230.1 0.0 copy-done.3
  230.1 0.2 select_reduce_fusion.1
  230.4 7.6 %reshape.234 = bf16[2048,1,768]{2,1,0:T(2,128)(2,1)} reshape(bf16[16,2,49152]{2,1,0:T(2,128)(2,1)S(1)} %all-to-all-done) | data formatting | bytes 6291456
  237.9 5.0 copy.55
  242.9 2.5 gather_fusion.4
  245.5 2.5 gather_fusion.2
  248.0 0.0 all-to-all-done.1
  248.0 11.5 %reshape.236 = bf16[2048,1,768]{2,1,0:T(2,128)(2,1)} reshape(bf16[16,2,49152]{2,1,0:T(2,128)(2,1)} %all-to-all-done.1) | data formatting | bytes 6291456
  259.5 5.0 copy.56
  264.5 3.7 gather_fusion.7
  268.1 3.7 gather_fusion.6
  271.8 3.2 fusion.6
  275.0 72.9 %psum.7 = f32[8,768]{1,0:T(8,128)S(1)} all-reduce(f32[8,768]{1,0:T(8,128)S(1)} %fusion.6), channel_id=1, replica_groups=mesh['layers'=2,'expert'=16] {'expert'}, use_global_device_ids=true, to_apply=%region_4.8 | all-reduce | flops 6144 | bytes 49152 | tf_op jit(solution)/shard_map/psum | solution.py:61
  347.9 0.7 broadcast_add_fusion
  348.6 3.4 fusion.11
  352.0 0.3 pad_maximum_fusion
  352.3 3.4 copy.51
  355.6 3.9 copy.52
  359.5 3.5 broadcast_in_dim.81
  363.0 7.7 %scatter_fusion = bf16[96,128,256]{2,1,0:T(8,128)(2,1)} fusion(bf16[96,128,256]{2,1,0:T(8,128)(2,1)} %broadcast_in_dim.81, s32[48]{0:T(128)S(1)} %fusion.16, bf16[48,128,256]{2,1,0:T(8,128)(2,1)S(1)} %bitcast.91), kind=kCustom, calls=%fused_computation.10 | custom fusion | bytes 9437376 | tf_op jit(solution)/shard_map/scatter | solution.py:83
  370.7 140.9 %all_to_all.39 = bf16[16,6,128,256]{3,2,1,0:T(8,128)(2,1)S(1)} all-to-all(bf16[16,6,128,256]{3,2,1,0:T(8,128)(2,1)} %bitcast.83), channel_id=1, replica_groups=mesh['layers'=2,'expert'=16] {'expert'}, dimensions={0} | all-to-all | bytes 12582912 | tf_op jit(solution)/shard_map/all_to_all | solution.py:86
  511.6 3.1 copy.53
  514.7 0.0 copy-start.1
  514.7 8.6 %copy.54 = bf16[6,256,2048]{2,1,0:T(8,128)(2,1)} copy(bf16[6,256,2048]{1,2,0:T(8,128)(2,1)} %bitcast.89) | data formatting | bytes 12582912
  523.4 0.0 copy-done.1
  (9 shorter events, 0.1 us)
Async XLA Ops:
  0.6 160.8 %copy-start = (s32[16]{0:T(128)S(1)}, s32[16]{0:T(128)}, u32[]{:S(2)}) copy-start(s32[16]{0:T(128)} %param.21) | copy-start | bytes 196
  5.8 4.8 copy-start.2
  79.2 66.7 %all-to-all-start = ((bf16[16,2,49152]{2,1,0:T(2,128)(2,1)}), bf16[16,2,49152]{2,1,0:T(2,128)(2,1)S(1)}, u32[]{:S(2)}, u32[]{:S(2)}) async-start(bf16[16,2,49152]{2,1,0:T(2,128)(2,1)} %reshape.233), calls=%async_computation | async-start | bytes 6291456 | tf_op jit(solution)/shard_map/all_to_all | solution.py:47
  141.7 88.4 %copy-start.3 = (s32[48,1]{0,1:T(1,128)S(1)}, s32[48,1]{0,1:T(1,128)}, u32[]{:S(2)}) copy-start(s32[48,1]{0,1:T(1,128)} %param.23) | copy-start | bytes 580
  145.9 102.1 %all-to-all-start.1 = ((bf16[16,2,49152]{2,1,0:T(2,128)(2,1)}), bf16[16,2,49152]{2,1,0:T(2,128)(2,1)}, u32[]{:S(2)}, u32[]{:S(2)}) async-start(bf16[16,2,49152]{2,1,0:T(2,128)(2,1)} %reshape.235), calls=%async_computation.1 | async-start | bytes 6291456 | tf_op jit(solution)/shard_map/all_to_all | solution.py:48
  514.7 8.6 %copy-start.1 = (s32[16]{0:T(128)S(1)}, s32[16]{0:T(128)}, u32[]{:S(2)}) copy-start(s32[16]{0:T(128)} %param.21) | copy-start | bytes 196
where the time goes:
time: 526 us; the launch traced here: 523 us
  blocking collectives  280 us (53%)
  local copies, waits for them, and re-layouts  127 us (24%)
  other arithmetic  88.2 us (17%)
  starting transfers between devices  22.8 us (4%)
    all_to_all x1, blocking collectives, body(): lax.all_to_all(outgoing, 'expert', split_axis=0, concat_axis=2, tiled=True)  141 us
    psum x1, blocking collectives, body(): intersection = lax.psum(intersection_part, 'expert')  72.9 us
    all_gather x1, blocking collectives, body(): all_norms = lax.all_gather(own_norms, 'expert', axis=0, tiled=True)  66.2 us
    unnamed x2, other arithmetic  64.9 us
    unnamed x24, local copies, waits for them, and re-layouts  56.1 us
    all_to_all x1, starting transfers between devices, body(): lax.all_to_all(up_values, 'expert', split_axis=1, concat_axis=0, tiled=True)  15.5 us
    select_n x1, local copies, waits for them, and re-layouts, body(): up_values = jnp.take(dequantize(up_codes, up_scale), order, axis=2)  15.5 us
    select_n x1, local copies, waits for them, and re-layouts, body(): gate_values = jnp.take(dequantize(gate_codes, gate_scale), order, axis=2)  10.8 us
  transfers between devices with their start and end apart: 2, of which 1 were waited for; matrix products, arithmetic and copies ran while one was open for 14% of the time, Pallas kernels for 0%

commit v1 on v0

v1 whole, which is shorter than its diff:
```python
import functools
import math

import jax
import jax.numpy as jnp
from jax import lax
from jax.experimental import pallas as pl
from jax.experimental.pallas import tpu as pltpu
from jax.sharding import PartitionSpec as P

BLK = 128
U = 128
CAP = 6
EPSILON = 1e-06
VMEM = 48 * 1024 * 1024


def slot_rows(owners):
    owner_ids = owners[:, 0]
    count = owner_ids.shape[0]
    matches = owner_ids[:, None] == owner_ids[None, :]
    earlier = jnp.arange(count)[None, :] < jnp.arange(count)[:, None]
    slot_rank = jnp.sum(jnp.where(matches & earlier, 1, 0), axis=1).astype(jnp.int32)
    return owner_ids * CAP + slot_rank


def own_order(pairs, unit_order, width):
    device_id = lax.axis_index("expert")
    is_right = pairs[:, 1] == device_id
    picked = jnp.sum(jnp.where(is_right[:, None], unit_order, 0), axis=0)
    identity = jnp.arange(width, dtype=jnp.int32)
    return jnp.where(jnp.any(is_right), picked, identity)


def prepare_kernel(source_ref, gate_ref, up_ref, gate_scale_ref, up_scale_ref, out_ref, select_ref):
    units = select_ref.shape[1]
    rows = gate_ref.shape[0]

    @pl.when(pl.program_id(0) == 0)
    def _():
        columns = lax.broadcasted_iota(jnp.int32, select_ref.shape, 1)
        select_ref[...] = (source_ref[...] == columns).astype(jnp.float32).astype(jnp.bfloat16)

    for kind, (codes_ref, scale_ref) in enumerate(
        ((gate_ref, gate_scale_ref), (up_ref, up_scale_ref))
    ):
        parts = []
        for block in range(rows // BLK):
            scale = scale_ref[0, block : block + 1, :]
            codes = codes_ref[block * BLK : (block + 1) * BLK, :].astype(jnp.float32)
            parts.append((codes * scale).astype(jnp.bfloat16))
        values = jnp.concatenate(parts, axis=0)
        chosen = lax.dot_general(
            select_ref[...], values, (((1,), (1,)), ((), ())), preferred_element_type=jnp.float32
        ).astype(jnp.bfloat16)
        out_ref[:, kind] = chosen.reshape(out_ref.shape[0], out_ref.shape[2], rows)


def prepare(source, gate_codes, up_codes, gate_scale, up_scale, devices):
    depth, units = gate_codes.shape
    per_device = units // devices
    tile = 256
    blocks = tile // BLK
    spread = lambda scale: jnp.repeat(scale.astype(jnp.float32), BLK, axis=1).reshape(
        depth // tile, blocks, units
    )
    return pl.pallas_call(
        prepare_kernel,
        grid=(depth // tile,),
        in_specs=[
            pl.BlockSpec((units, 1), lambda d: (0, 0)),
            pl.BlockSpec((tile, units), lambda d: (d, 0)),
            pl.BlockSpec((tile, units), lambda d: (d, 0)),
            pl.BlockSpec((1, blocks, units), lambda d: (d, 0, 0)),
            pl.BlockSpec((1, blocks, units), lambda d: (d, 0, 0)),
        ],
        out_specs=pl.BlockSpec((devices, 2, per_device, tile), lambda d: (0, 0, 0, d)),
        out_shape=jax.ShapeDtypeStruct((devices, 2, per_device, depth), jnp.bfloat16),
        scratch_shapes=[pltpu.VMEM((units, units), jnp.bfloat16)],
        compiler_params=pltpu.CompilerParams(vmem_limit_bytes=VMEM),
        name="prepare",
    )(source[:, None], gate_codes, up_codes, spread(gate_scale), spread(up_scale))


def merge_kernel(
    pairs_ref, counts_ref, slots_ref, left_ref, right_ref, similarity_ref, out_ref, ready, sems
):
    pair = pl.program_id(0)
    pair_count = pl.num_programs(0)
    per_device, depth = left_ref.shape[2], left_ref.shape[3]
    pieces, piece_rows = ready.shape[1], ready.shape[2]
    left_gate = left_ref[0, 0].astype(jnp.float32)
    left_up = left_ref[0, 1].astype(jnp.float32)
    right_gate = right_ref[0, 0].astype(jnp.float32)
    right_up = right_ref[0, 1].astype(jnp.float32)
    total_of = lambda value: jnp.sum(value, axis=1, keepdims=True)
    intersection = total_of(left_gate * right_gate + left_up * right_up)
    left_norm = total_of(left_gate * left_gate + left_up * left_up)
    right_norm = total_of(right_gate * right_gate + right_up * right_up)
    similarity = (
        intersection
        * math.sqrt(2.0 * depth)
        / jnp.sqrt((left_norm + EPSILON) * (right_norm + EPSILON))
    )
    similarity_ref[0] = similarity
    left_freq = counts_ref[pairs_ref[2 * pair]].astype(jnp.float32)
    right_freq = counts_ref[pairs_ref[2 * pair + 1]].astype(jnp.float32)
    share = right_freq * jax.nn.sigmoid(similarity)
    total = left_freq + share
    left_weight = left_freq / total
    right_weight = share / total
    merged = jnp.concatenate(
        (
            left_weight * left_gate + right_weight * right_gate,
            left_weight * left_up + right_weight * right_up,
        ),
        axis=0,
    ).astype(jnp.bfloat16)
    to_row = lax.broadcasted_iota(jnp.int32, (2 * per_device, 2 * per_device), 0)
    from_row = lax.broadcasted_iota(jnp.int32, (2 * per_device, 2 * per_device), 1)
    weave = from_row == jnp.right_shift(to_row, 1) + per_device * jnp.bitwise_and(to_row, 1)
    woven = jnp.dot(
        weave.astype(jnp.float32).astype(jnp.bfloat16), merged, preferred_element_type=jnp.float32
    )
    slot = lax.rem(pair, 2)

    def copies(which_pair, which_slot):
        return [
            pltpu.make_async_copy(
                ready.at[which_slot, piece],
                out_ref.at[slots_ref[which_pair * pieces + piece]],
                sems.at[which_slot, piece],
            )
            for piece in range(pieces)
        ]

    @pl.when(pair >= 2)
    def _():
        for copy in copies(pair - 2, slot):
            copy.wait()

    ready[slot] = woven.astype(jnp.bfloat16).reshape(pieces, piece_rows, depth)
    for copy in copies(pair, slot):
        copy.start()

    @pl.when(pair == pair_count - 1)
    def _():
        for copy in copies(pair - 1, 1 - slot):
            copy.wait()
        for copy in copies(pair, slot):
            copy.wait()


def merge(pairs, counts, slots, rows, devices):
    _, _, per_device, depth = rows.shape
    pair_count = pairs.shape[0]
    pieces = slots.shape[0] // pair_count
    piece_rows = 2 * per_device // pieces
    grid_spec = pltpu.PrefetchScalarGridSpec(
        num_scalar_prefetch=3,
        grid=(pair_count,),
        in_specs=[
            pl.BlockSpec((1, 2, per_device, depth), lambda p, pairs, *_: (pairs[2 * p], 0, 0, 0)),
            pl.BlockSpec(
                (1, 2, per_device, depth), lambda p, pairs, *_: (pairs[2 * p + 1], 0, 0, 0)
            ),
        ],
        out_specs=[
            pl.BlockSpec((1, per_device, 1), lambda p, *_: (p, 0, 0)),
            pl.BlockSpec(memory_space=pl.ANY),
        ],
        scratch_shapes=[
            pltpu.VMEM((2, pieces, piece_rows, depth), jnp.bfloat16),
            pltpu.SemaphoreType.DMA((2, pieces)),
        ],
    )
    return pl.pallas_call(
        merge_kernel,
        grid_spec=grid_spec,
        out_shape=[
            jax.ShapeDtypeStruct((pair_count, per_device, 1), jnp.float32),
            jax.ShapeDtypeStruct((devices * CAP, piece_rows, depth), jnp.bfloat16),
        ],
        compiler_params=pltpu.CompilerParams(vmem_limit_bytes=VMEM),
        name="merge",
    )(pairs.reshape(-1), counts, slots, rows, rows)


def place_kernel(filled_ref, in_ref, out_ref):
    value = in_ref[:, 0].reshape(out_ref.shape[1], out_ref.shape[2])
    keep = pl.program_id(0) < filled_ref[0]
    out_ref[0] = jnp.where(keep, value, jnp.zeros_like(value))


def place(filled, arrived):
    devices, cap, piece_rows, depth = arrived.shape
    grid_spec = pltpu.PrefetchScalarGridSpec(
        num_scalar_prefetch=1,
        grid=(cap,),
        in_specs=[pl.BlockSpec((devices, 1, piece_rows, depth), lambda s, *_: (0, s, 0, 0))],
        out_specs=pl.BlockSpec((1, devices * piece_rows, depth), lambda s, *_: (s, 0, 0)),
    )
    return pl.pallas_call(
        place_kernel,
        grid_spec=grid_spec,
        out_shape=jax.ShapeDtypeStruct((cap, devices * piece_rows, depth), arrived.dtype),
        compiler_params=pltpu.CompilerParams(vmem_limit_bytes=VMEM),
        name="place",
    )(filled, arrived)


def body(gate_codes, up_codes, gate_scale, up_scale, pairs, counts, unit_order, owners):
    devices = lax.axis_size("expert")
    units = gate_codes.shape[2]
    pieces = units // U
    share_units = U // devices
    per_device = pieces * share_units
    order = own_order(pairs, unit_order, units)
    source = order.reshape(pieces, devices, share_units).transpose(1, 0, 2).reshape(units)
    outgoing = prepare(
        source, gate_codes[0], up_codes[0], gate_scale[0], up_scale[0], devices
    )
    rows = lax.all_to_all(outgoing, "expert", split_axis=0, concat_axis=0, tiled=True)
    similarity_part, merged = merge(pairs, counts, slot_rows(owners), rows, devices)
    pair_count = pairs.shape[0]
    merged = merged.reshape(devices, CAP, merged.shape[1], merged.shape[2])
    arrived = lax.all_to_all(merged, "expert", split_axis=0, concat_axis=0, tiled=True)
    similarity = lax.all_gather(similarity_part.reshape(1, -1), "expert", axis=0, tiled=True)
    similarity = similarity.reshape(devices, pair_count, pieces, share_units)
    similarity = similarity.transpose(1, 2, 0, 3).reshape(pair_count, units)
    filled = jnp.sum((owners[:, 0] == lax.axis_index("expert")).astype(jnp.int32))[None]
    return place(filled, arrived), similarity


def solution(mesh):
    in_specs = (
        P(("layers", "expert"), None, None),
        P(("layers", "expert"), None, None),
        P(("layers", "expert"), None, None),
        P(("layers", "expert"), None, None),
        P("layers", None),
        P("layers"),
        P("layers", None),
        P("layers", None),
    )
    out_specs = (P(("layers", "expert"), None, None), P("layers", None))
    return jax.shard_map(body, mesh=mesh, in_specs=in_specs, out_specs=out_specs, check_vma=False)
```

time: 526 us -> 334 us (0.63)
  the two profiles are of different devices: /device:TPU:0 before, /device:TPU:9 now
where the time goes in v1:
time: 334 us; the launch traced here: 333 us
  blocking collectives  148 us (44%)
  waiting for transfers between devices  134 us (40%)
  Pallas kernels  27.4 us (8%)
  starting transfers between devices  13.8 us (4%)
  other arithmetic  5.1 us (2%)
  local copies, waits for them, and re-layouts  3.94 us (1%)
    all_gather x1, blocking collectives, body(): lax.all_gather(similarity_part.reshape(1, -1), 'expert', axis=0, tiled=True)  148 us
    all_to_all x1, waiting for transfers between devices, body(): lax.all_to_all(outgoing, 'expert', split_axis=0, concat_axis=0, tiled=True)  134 us
    pallas_call x1, Pallas kernels, prepare(): pl.pallas_call(prepare_kernel, grid=(depth // tile,), in_specs=[pl.BlockS...  10.2 us
    pallas_call x1, Pallas kernels, merge(): pl.pallas_call(merge_kernel, grid_spec=grid_spec, out_shape=[jax.ShapeDty...  9.63 us
    pallas_call x1, Pallas kernels, place(): pl.pallas_call(place_kernel, grid_spec=grid_spec, out_shape=jax.ShapeDtyp...  7.61 us
    all_to_all x1, starting transfers between devices, body(): lax.all_to_all(merged, 'expert', split_axis=0, concat_axis=0, tiled=True)  7.07 us
    all_to_all x1, starting transfers between devices, body(): lax.all_to_all(outgoing, 'expert', split_axis=0, concat_axis=0, tiled=True)  6.72 us
  transfers between devices with their start and end apart: 2, of which 1 were waited for; matrix products, arithmetic and copies ran while one was open for 1% of the time, Pallas kernels for 0%

profile of v1, /device:TPU:9, one launch (start us, length us, event | category | flops | bytes accessed | tf_op | source)
XLA Modules:
  0.0 332.8 jit_solution(10772180191578409174)
XLA Ops:
  0.6 0.7 bitcast_convert_fusion.1
  1.3 0.1 copy.30
  1.4 0.7 bitcast_convert_fusion
  2.1 0.1 copy.31
  2.2 1.3 compare_reduce_fusion
  3.5 0.8 select_reduce_fusion
  4.3 0.1 reduce_sum.32
  4.4 0.7 select_bitcast_fusion
  5.1 0.1 broadcast_in_dim.41
  5.2 0.1 broadcast_in_dim.40
  5.3 0.2 broadcast_in_dim_reshape.4.source_ref
  5.5 0.0 copy-start
  5.5 1.9 copy-done
  7.4 10.2 %prepare.1 = bf16[16,2,48,2048]{3,2,1,0:T(8,128)(2,1)} custom-call(s32[768,1]{1,0:T(8,128)S(1)} %broadcast_in_dim_reshape.4.source_ref, bf16[2048,768]{1,0:T(8,128)(2,1)S(1)} %bitcast.22, bf16[2048,768]{1,0:T(8,128)(2,1)} %bitcast.24, f32[8,2,768]{2,1,0:T(2,128)S(1)} %reshape_reshape.6.gate_scale_ref, f32[8,2,768]{2,1,0:T(2,128)S(1)} %reshape_reshape.7.up_scale_ref), custom_call_target="tpu_custom_call" | custom-call | tf_op jit(solution)/shard_map/prepare/pallas_call | solution.py:67
  17.6 0.0 copy-start.2
  17.6 0.0 copy-start.3
  17.6 0.0 copy-start.1
  17.6 6.7 %all-to-all-start = ((bf16[16,2,48,2048]{3,2,1,0:T(8,128)(2,1)}), bf16[16,2,48,2048]{3,2,1,0:T(8,128)(2,1)}, u32[]{:S(2)}, u32[]{:S(2)}) async-start(bf16[16,2,48,2048]{3,2,1,0:T(8,128)(2,1)} %prepare.1), calls=%async_computation | async-start | bytes 12582912 | tf_op jit(solution)/shard_map/all_to_all | solution.py:223
  24.3 0.0 copy-done.2
  24.3 0.1 copy.28
  24.4 0.1 reshape.29.pairs_ref
  24.5 0.0 copy-done.3
  24.5 0.2 select_reduce_fusion.1
  24.7 0.6 multiply_add_fusion
  25.3 134.3 %all-to-all-done.left_ref.right_ref = bf16[16,2,48,2048]{3,2,1,0:T(8,128)(2,1)} async-done(((bf16[16,2,48,2048]{3,2,1,0:T(8,128)(2,1)}), bf16[16,2,48,2048]{3,2,1,0:T(8,128)(2,1)}, u32[]{:S(2)}, u32[]{:S(2)}) %all-to-all-start) | async-done | bytes 6291488 | tf_op jit(solution)/shard_map/all_to_all | solution.py:223
  159.6 0.0 copy-done.1
  159.6 9.6 %merge.1 = (f32[8,48,1]{2,1,0:T(8,128)S(1)}, bf16[96,16,2048]{2,1,0:T(8,128)(2,1)}) custom-call(s32[16]{0:T(128)S(1)} %reshape.29.pairs_ref, s32[16]{0:T(128)S(1)} %copy-done.1, s32[48]{0:T(128)S(1)} %get-tuple-element.8.slots_ref, bf16[16,2,48,2048]{3,2,1,0:T(8,128)(2,1)} %all-to-all-done.left_ref.right_ref, ...), custom_call_target="tpu_custom_call" | custom-call | tf_op jit(solution)/shard_map/merge/pallas_call | solution.py:177
  169.2 7.1 %all-to-all-start.1 = ((bf16[16,6,16,2048]{3,2,1,0:T(8,128)(2,1)}), bf16[16,6,16,2048]{3,2,1,0:T(8,128)(2,1)}, u32[]{:S(2)}, u32[]{:S(2)}) async-start(bf16[16,6,16,2048]{3,2,1,0:T(8,128)(2,1)} %bitcast.23), calls=%async_computation.1 | async-start | bytes 12582912 | tf_op jit(solution)/shard_map/all_to_all | solution.py:227
  176.3 0.1 reduce.1
  176.4 0.1 reshape.36
  176.5 147.5 %all-gather = f32[16,1,384]{2,1,0:T(1,128)S(1)} all-gather(f32[1,1,384]{2,1,0:T(1,128)S(1)} %reshape.36), channel_id=1, replica_groups=mesh['layers'=2,'expert'=16] {'expert'}, dimensions={0}, use_global_device_ids=true | all-gather | bytes 26112 | tf_op jit(solution)/shard_map/all_gather | solution.py:228
  324.0 0.1 copy.33
  324.1 0.2 copy.34
  324.3 0.8 reshape.33
  325.2 0.0 all-to-all-done.1.in_ref
  325.2 7.6 %place.1 = bf16[6,256,2048]{2,1,0:T(8,128)(2,1)} custom-call(s32[1]{0:T(128)} %bitcast.1.filled_ref, bf16[16,6,16,2048]{3,2,1,0:T(8,128)(2,1)} %all-to-all-done.1.in_ref), custom_call_target="tpu_custom_call" | custom-call | tf_op jit(solution)/shard_map/place/pallas_call | solution.py:203
  (3 shorter events, 0.1 us)
Async XLA Ops:
  5.5 1.9 copy-start
  17.6 6.7 %copy-start.2 = (s32[8,2]{0,1:T(2,128)S(1)}, s32[8,2]{0,1:T(2,128)}, u32[]{:S(2)}) copy-start(s32[8,2]{0,1:T(2,128)} %param.12) | copy-start | bytes 196
  17.6 6.9 %copy-start.3 = (s32[48,1]{0,1:T(1,128)S(1)}, s32[48,1]{0,1:T(1,128)}, u32[]{:S(2)}) copy-start(s32[48,1]{0,1:T(1,128)} %param.15) | copy-start | bytes 580
  17.6 142.0 %copy-start.1 = (s32[16]{0:T(128)S(1)}, s32[16]{0:T(128)}, u32[]{:S(2)}) copy-start(s32[16]{0:T(128)} %counts_ref.1) | copy-start | bytes 196
  17.6 142.0 %all-to-all-start = ((bf16[16,2,48,2048]{3,2,1,0:T(8,128)(2,1)}), bf16[16,2,48,2048]{3,2,1,0:T(8,128)(2,1)}, u32[]{:S(2)}, u32[]{:S(2)}) async-start(bf16[16,2,48,2048]{3,2,1,0:T(8,128)(2,1)} %prepare.1), calls=%async_computation | async-start | bytes 12582912 | tf_op jit(solution)/shard_map/all_to_all | solution.py:223
  169.2 156.0 %all-to-all-start.1 = ((bf16[16,6,16,2048]{3,2,1,0:T(8,128)(2,1)}), bf16[16,6,16,2048]{3,2,1,0:T(8,128)(2,1)}, u32[]{:S(2)}, u32[]{:S(2)}) async-start(bf16[16,6,16,2048]{3,2,1,0:T(8,128)(2,1)} %bitcast.23), calls=%async_computation.1 | async-start | bytes 12582912 | tf_op jit(solution)/shard_map/all_to_all | solution.py:227

commit v2 on v1

--- a/solution.py
+++ b/solution.py
@@ -13,15 +13,6 @@
 CAP = 6
 EPSILON = 1e-06
 VMEM = 48 * 1024 * 1024
-
-
-def slot_rows(owners):
-    owner_ids = owners[:, 0]
-    count = owner_ids.shape[0]
-    matches = owner_ids[:, None] == owner_ids[None, :]
-    earlier = jnp.arange(count)[None, :] < jnp.arange(count)[:, None]
-    slot_rank = jnp.sum(jnp.where(matches & earlier, 1, 0), axis=1).astype(jnp.int32)
-    return owner_ids * CAP + slot_rank
 
 
 def own_order(pairs, unit_order, width):
@@ -83,8 +74,18 @@
 
 
 def merge_kernel(
-    pairs_ref, counts_ref, slots_ref, left_ref, right_ref, similarity_ref, out_ref, ready, sems
+    widths,
+    pairs_ref,
+    counts_ref,
+    near_ref,
+    place_ref,
+    left_ref,
+    right_ref,
+    similarity_ref,
+    near_out,
+    *rest,
 ):
+    far_outs, (ready, sems) = rest[: len(widths)], rest[len(widths) :]
     pair = pl.program_id(0)
     pair_count = pl.num_programs(0)
     per_device, depth = left_ref.shape[2], left_ref.shape[3]
@@ -124,40 +125,54 @@
     )
     slot = lax.rem(pair, 2)
 
-    def copies(which_pair, which_slot):
-        return [
-            pltpu.make_async_copy(
-                ready.at[which_slot, piece],
-                out_ref.at[slots_ref[which_pair * pieces + piece]],
-                sems.at[which_slot, piece],
-            )
-            for piece in range(pieces)
-        ]
+    def each_copy(which_pair, which_slot, act):
+        for piece in range(pieces):
+            index = which_pair * pieces + piece
+            near = near_ref[index] == 1
+
+            @pl.when(near)
+            def _():
+                act(
+                    pltpu.make_async_copy(
+                        ready.at[which_slot, piece],
+                        near_out.at[place_ref[index]],
+                        sems.at[which_slot, piece, 0],
+                    )
+                )
+
+            @pl.when(jnp.logical_not(near))
+            def _():
+                begin = 0
+                for chunk, width in enumerate(widths):
+                    act(
+                        pltpu.make_async_copy(
+                            ready.at[which_slot, piece, :, pl.ds(begin, width)],
+                            far_outs[chunk].at[place_ref[index]],
+                            sems.at[which_slot, piece, chunk],
+                        )
+                    )
+                    begin += width
 
     @pl.when(pair >= 2)
     def _():
-        for copy in copies(pair - 2, slot):
-            copy.wait()
+        each_copy(pair - 2, slot, lambda copy: copy.wait())
 
     ready[slot] = woven.astype(jnp.bfloat16).reshape(pieces, piece_rows, depth)
-    for copy in copies(pair, slot):
-        copy.start()
+    each_copy(pair, slot, lambda copy: copy.start())
 
     @pl.when(pair == pair_count - 1)
     def _():
-        for copy in copies(pair - 1, 1 - slot):
-            copy.wait()
-        for copy in copies(pair, slot):
-            copy.wait()
-
-
-def merge(pairs, counts, slots, rows, devices):
+        each_copy(pair - 1, 1 - slot, lambda copy: copy.wait())
+        each_copy(pair, slot, lambda copy: copy.wait())
+
+
+def merge(pairs, counts, near, places, rows, slots, listed, widths):
     _, _, per_device, depth = rows.shape
     pair_count = pairs.shape[0]
-    pieces = slots.shape[0] // pair_count
+    pieces = near.shape[0] // pair_count
     piece_rows = 2 * per_device // pieces
     grid_spec = pltpu.PrefetchScalarGridSpec(
-        num_scalar_prefetch=3,
+        num_scalar_prefetch=4,
         grid=(pair_count,),
         in_specs=[
             pl.BlockSpec((1, 2, per_device, depth), lambda p, pairs, *_: (pairs[2 * p], 0, 0, 0)),
@@ -165,71 +180,147 @@
                 (1, 2, per_device, depth), lambda p, pairs, *_: (pairs[2 * p + 1], 0, 0, 0)
             ),
         ],
-        out_specs=[
-            pl.BlockSpec((1, per_device, 1), lambda p, *_: (p, 0, 0)),
-            pl.BlockSpec(memory_space=pl.ANY),
-        ],
+        out_specs=[pl.BlockSpec((1, per_device, 1), lambda p, *_: (p, 0, 0))]
+        + [pl.BlockSpec(memory_space=pl.ANY)] * (1 + len(widths)),
         scratch_shapes=[
             pltpu.VMEM((2, pieces, piece_rows, depth), jnp.bfloat16),
-            pltpu.SemaphoreType.DMA((2, pieces)),
+            pltpu.SemaphoreType.DMA((2, pieces, len(widths))),
         ],
     )
     return pl.pallas_call(
-        merge_kernel,
+        functools.partial(merge_kernel, widths),
         grid_spec=grid_spec,
         out_shape=[
             jax.ShapeDtypeStruct((pair_count, per_device, 1), jnp.float32),
-            jax.ShapeDtypeStruct((devices * CAP, piece_rows, depth), jnp.bfloat16),
-        ],
+            jax.ShapeDtypeStruct((slots, piece_rows, depth), jnp.bfloat16),
+        ]
+        + [jax.ShapeDtypeStruct((listed, piece_rows, width), jnp.bfloat16) for width in widths],
         compiler_params=pltpu.CompilerParams(vmem_limit_bytes=VMEM),
         name="merge",
-    )(pairs.reshape(-1), counts, slots, rows, rows)
-
-
-def place_kernel(filled_ref, in_ref, out_ref):
+    )(pairs.reshape(-1), counts, near, places, rows, rows)
+
+
+def place_kernel(offset, filled_ref, in_ref, *rest):
+    out_ref = rest[-1]
     value = in_ref[:, 0].reshape(out_ref.shape[1], out_ref.shape[2])
     keep = pl.program_id(0) < filled_ref[0]
     out_ref[0] = jnp.where(keep, value, jnp.zeros_like(value))
 
 
-def place(filled, arrived):
-    devices, cap, piece_rows, depth = arrived.shape
+def place(filled, half, arrived, begin, depth, base=None):
+    sources, cap, piece_rows, width = arrived.shape
     grid_spec = pltpu.PrefetchScalarGridSpec(
-        num_scalar_prefetch=1,
+        num_scalar_prefetch=2,
         grid=(cap,),
-        in_specs=[pl.BlockSpec((devices, 1, piece_rows, depth), lambda s, *_: (0, s, 0, 0))],
-        out_specs=pl.BlockSpec((1, devices * piece_rows, depth), lambda s, *_: (s, 0, 0)),
+        in_specs=[pl.BlockSpec((sources, 1, piece_rows, width), lambda s, *_: (0, s, 0, 0))]
+        + ([] if base is None else [pl.BlockSpec(memory_space=pl.ANY)]),
+        out_specs=pl.BlockSpec(
+            (1, sources * piece_rows, width),
+            lambda s, filled, half: (s, half[0], begin // width),
+        ),
     )
     return pl.pallas_call(
-        place_kernel,
+        lambda filled_ref, half_ref, *refs: place_kernel(None, filled_ref, *refs),
         grid_spec=grid_spec,
-        out_shape=jax.ShapeDtypeStruct((cap, devices * piece_rows, depth), arrived.dtype),
+        out_shape=jax.ShapeDtypeStruct((cap, 2 * sources * piece_rows, depth), arrived.dtype),
+        input_output_aliases={} if base is None else {3: 0},
         compiler_params=pltpu.CompilerParams(vmem_limit_bytes=VMEM),
         name="place",
-    )(filled, arrived)
+    )(filled, half, arrived, *(() if base is None else (base,)))
 
 
 def body(gate_codes, up_codes, gate_scale, up_scale, pairs, counts, unit_order, owners):
     devices = lax.axis_size("expert")
-    units = gate_codes.shape[2]
+    layers = lax.axis_size("layers")
+    me = lax.axis_index("expert")
+    depth, units = gate_codes.shape[1:]
     pieces = units // U
     share_units = U // devices
     per_device = pieces * share_units
+    half = devices // 2
+    side = me // half
+    pair_count = pairs.shape[0]
+    all_pieces = pair_count * pieces
+    widths = (depth // 2, depth // 2)
+
+    owner_ids = owners[:, 0]
+    owner_side = owner_ids // half
+    earlier = jnp.arange(all_pieces)[None, :] < jnp.arange(all_pieces)[:, None]
+    count_earlier = lambda values: jnp.sum(
+        jnp.where((values[:, None] == values[None, :]) & earlier, 1, 0), axis=1
+    ).astype(jnp.int32)
+    slot = (owner_ids % half) * CAP + count_earlier(owner_ids)
+    position = count_earlier(owner_side)
+    near = (owner_side == side).astype(jnp.int32)
+    places = jnp.where(near == 1, slot, position)
+    filled = jnp.sum((owner_ids == me).astype(jnp.int32))[None]
+    from_list = jnp.sum(
+        jnp.where(
+            (jnp.arange(half * CAP)[:, None] == slot[None, :]) & (near == 1)[None, :],
+            position[None, :],
+            0,
+        ),
+        axis=1,
+    ).astype(jnp.int32)
+    ones = jnp.sum(owner_side).astype(jnp.int32)
+    longest = jnp.maximum(ones, all_pieces - ones)
+    for shift in range(1, layers):
+        other = lax.ppermute(
+            jnp.maximum(ones, all_pieces - ones),
+            "layers",
+            [(layer, (layer + shift) % layers) for layer in range(layers)],
+        )
+        longest = jnp.maximum(longest, other)
+    least = all_pieces // 2
+    sizes = [least + -(-least * part // 12) for part in (1, 2, 3, 6, 12)]
+    level = sum((longest > size).astype(jnp.int32) for size in sizes[:-1])
+
     order = own_order(pairs, unit_order, units)
     source = order.reshape(pieces, devices, share_units).transpose(1, 0, 2).reshape(units)
     outgoing = prepare(
         source, gate_codes[0], up_codes[0], gate_scale[0], up_scale[0], devices
     )
     rows = lax.all_to_all(outgoing, "expert", split_axis=0, concat_axis=0, tiled=True)
-    similarity_part, merged = merge(pairs, counts, slot_rows(owners), rows, devices)
-    pair_count = pairs.shape[0]
-    merged = merged.reshape(devices, CAP, merged.shape[1], merged.shape[2])
-    arrived = lax.all_to_all(merged, "expert", split_axis=0, concat_axis=0, tiled=True)
-    similarity = lax.all_gather(similarity_part.reshape(1, -1), "expert", axis=0, tiled=True)
-    similarity = similarity.reshape(devices, pair_count, pieces, share_units)
-    similarity = similarity.transpose(1, 2, 0, 3).reshape(pair_count, units)
-    filled = jnp.sum((owners[:, 0] == lax.axis_index("expert")).astype(jnp.int32))[None]
-    return place(filled, arrived), similarity
+
+    groups = [list(range(half)), list(range(half, devices))]
+    mirror = [(device, (device + half) % devices) for device in range(devices)]
+
+    def within_half(value):
+        value = value.reshape(half, CAP, value.shape[1], value.shape[2])
+        return lax.all_to_all(
+            value, "expert", split_axis=0, concat_axis=0, tiled=True, axis_index_groups=groups
+        )
+
+    def deal(listed, rows, near, places, from_list):
+        similarity_part, slots, *lists = merge(
+            pairs, counts, near, places, rows, half * CAP, listed, widths
+        )
+        arrived = [within_half(slots)]
+        for chunk in lists:
+            chunk = lax.ppermute(chunk, "expert", mirror)
+            spread = jnp.take(chunk, from_list, axis=0, mode="clip")
+            spread, arrived[-1] = lax.optimization_barrier((spread, arrived[-1]))
+            arrived.append(within_half(spread))
+        similarity_part, _ = lax.optimization_barrier((similarity_part, spread))
+        similarity = lax.all_gather(similarity_part.reshape(1, -1), "expert", axis=0, tiled=True)
+        similarity = similarity.reshape(devices, pair_count, pieces, share_units)
+        similarity = similarity.transpose(1, 2, 0, 3).reshape(pair_count, units)
+        own, others = side.astype(jnp.int32)[None], (1 - side).astype(jnp.int32)[None]
+        merged = place(filled, own, arrived[0], 0, depth)
+        begin = 0
+        for width, value in zip(widths, arrived[1:]):
+            merged = place(filled, others, value, begin, depth, merged)
+            begin += width
+        return merged, similarity
+
+    return lax.switch(
+        level,
+        [functools.partial(deal, size) for size in sizes],
+        rows,
+        near,
+        places,
+        from_list,
+    )
 
 
 def solution(mesh):

time: 334 us -> 341 us (1.021)
  the two profiles are of different devices: /device:TPU:9 before, /device:TPU:0 now
where the time goes in v2:
time: 341 us; the launch traced here: 342 us
  waiting for transfers between devices  203 us (60%)
  starting transfers between devices  52.1 us (15%)
  Pallas kernels  35.5 us (10%)
  blocking collectives  28.9 us (8%)
  local copies, waits for them, and re-layouts  13.8 us (4%)
  other arithmetic  6.09 us (2%)
    all_to_all x1, waiting for transfers between devices, body(): lax.all_to_all(outgoing, 'expert', split_axis=0, concat_axis=0, tiled=True)  108 us
    ppermute x2, waiting for transfers between devices, deal(): chunk = lax.ppermute(chunk, 'expert', mirror)  94.6 us
    all_to_all x3, starting transfers between devices, within_half(): lax.all_to_all(value, 'expert', split_axis=0, concat_axis=0, tiled=True,...  38.1 us
    all_gather x1, blocking collectives, deal(): lax.all_gather(similarity_part.reshape(1, -1), 'expert', axis=0, tiled=True)  28.9 us
    pallas_call x3, Pallas kernels, place(): pl.pallas_call(lambda filled_ref, half_ref, *refs: place_kernel(None, fil...  14 us
    pallas_call x1, Pallas kernels, merge(): pl.pallas_call(functools.partial(merge_kernel, widths), grid_spec=grid_sp...  11.4 us
    pallas_call x1, Pallas kernels, prepare(): pl.pallas_call(prepare_kernel, grid=(depth // tile,), in_specs=[pl.BlockS...  10.2 us
    all_to_all x1, starting transfers between devices, body(): lax.all_to_all(outgoing, 'expert', split_axis=0, concat_axis=0, tiled=True)  7.53 us
  transfers between devices with their start and end apart: 7, of which 4 were waited for; matrix products, arithmetic and copies ran while one was open for 3% of the time, Pallas kernels for 3%

profile of v2, /device:TPU:0, one launch (start us, length us, event | category | flops | bytes accessed | tf_op | source)
XLA Modules:
  0.0 342.1 jit_solution(11152536813371755269)
XLA Ops:
  0.6 0.7 bitcast_convert_fusion.1
  1.3 0.1 copy.77
  1.4 0.7 bitcast_convert_fusion
  2.1 0.1 copy.78
  2.2 1.3 compare_reduce_fusion
  3.5 0.8 select_reduce_fusion.5
  4.3 0.1 reduce_sum.60
  4.4 0.7 select_bitcast_fusion
  5.1 0.1 broadcast_in_dim.113
  5.2 0.1 broadcast_in_dim.112
  5.3 0.2 broadcast_in_dim_reshape.4.source_ref
  5.5 0.0 copy-start.4
  5.5 1.9 copy-done.4
  7.4 10.2 %prepare.1 = bf16[16,2,48,2048]{3,2,1,0:T(8,128)(2,1)} custom-call(s32[768,1]{1,0:T(8,128)S(1)} %broadcast_in_dim_reshape.4.source_ref, bf16[2048,768]{1,0:T(8,128)(2,1)S(1)} %bitcast.82, bf16[2048,768]{1,0:T(8,128)(2,1)} %bitcast.94, f32[8,2,768]{2,1,0:T(2,128)S(1)} %reshape_reshape.6.gate_scale_ref, f32[8,2,768]{2,1,0:T(2,128)S(1)} %reshape_reshape.7.up_scale_ref), custom_call_target="tpu_custom_call" | custom-call | tf_op jit(solution)/shard_map/prepare/pallas_call | solution.py:58
  17.6 0.0 copy-start.17
  17.6 0.0 copy-start.15
  17.6 0.0 copy-start.16
  17.6 7.5 %all-to-all-start.15 = ((bf16[16,2,48,2048]{3,2,1,0:T(8,128)(2,1)}), bf16[16,2,48,2048]{3,2,1,0:T(8,128)(2,1)}, u32[]{:S(2)}, u32[]{:S(2)}) async-start(bf16[16,2,48,2048]{3,2,1,0:T(8,128)(2,1)} %prepare.1), calls=%async_computation.15 | async-start | bytes 12582912 | tf_op jit(solution)/shard_map/all_to_all | solution.py:283
  25.1 0.0 copy-done.17
  25.2 0.6 reduce_sum.56
  27.1 2.9 collective-permute-start.10
  30.0 0.2 select_reduce_fusion.7
  30.2 0.2 select_reduce_fusion.6
  30.4 0.3 collective-permute-done.10
  31.4 108.0 %all-to-all-done.15 = bf16[16,2,48,2048]{3,2,1,0:T(8,128)(2,1)} async-done(((bf16[16,2,48,2048]{3,2,1,0:T(8,128)(2,1)}), bf16[16,2,48,2048]{3,2,1,0:T(8,128)(2,1)}, u32[]{:S(2)}, u32[]{:S(2)}) %all-to-all-start.15) | async-done | bytes 6291488 | tf_op jit(solution)/shard_map/all_to_all | solution.py:283
  139.3 0.0 copy-done.15
  139.3 0.0 copy-done.16
  139.4 202.8 %conditional.1 = (bf16[6,256,2048]{2,1,0:T(8,128)(2,1)}, f32[8,768]{1,0:T(8,128)}) conditional(s32[]{:T(128)} %clamp.3, (s32[]{:T(128)}, s32[8,2]{0,1:T(2,128)S(1)}, s32[16]{0:T(128)S(1)}, s32[48]{0:T(128)S(1)}, pred[48]{0:T(512)(128)(4,1)S(1)}, /*index=5*/bf16[16,2,48,2048]{3,2,1,0:T(8,128)(2,1)}, ...), branch_computations={%region_7.8_spmd, %region_8.9_spmd, %region_9.10_spmd, %region_10.... | conditional | flops 10288 | bytes 56827920 | solution.py:316
  139.4 0.1 copy.81
  139.5 0.1 reshape.157.pairs_ref
  139.5 11.4 %merge.6 = (f32[8,48,1]{2,1,0:T(8,128)S(1)}, bf16[48,16,2048]{2,1,0:T(8,128)(2,1)S(1)}, bf16[28,16,1024]{2,1,0:T(8,128)(2,1)S(1)}, bf16[28,16,1024]{2,1,0:T(8,128)(2,1)S(1)}) custom-call(s32[16]{0:T(128)S(1)} %reshape.157.pairs_ref, s32[16]{0:T(128)S(1)} %get-tuple-element.205.counts_ref, s32[48]{0:T(128)S(1)} %get-tuple-element.101.near_ref, ...), custom_call_target="tpu_custom_call" | custom-call | tf_op jit(solution)/shard_map/cond/branch_1_fun/merge/pallas_call | solution.py:190
  150.9 0.0 copy-start.1
  150.9 1.7 copy-done.1
  152.6 0.0 copy-start.11
  152.6 1.0 copy-done.11
  153.6 0.0 copy-start.12
  153.6 1.0 copy-done.12
  154.6 27.1 %all-to-all-start.3 = ((bf16[8,6,16,2048]{3,2,1,0:T(8,128)(2,1)}), bf16[8,6,16,2048]{3,2,1,0:T(8,128)(2,1)S(1)}, u32[]{:S(2)}, u32[]{:S(2)}) async-start(bf16[8,6,16,2048]{3,2,1,0:T(8,128)(2,1)} %bitcast.79), calls=%async_computation.3 | async-start | bytes 6291456 | tf_op jit(solution)/shard_map/cond/branch_1_fun/all_to_all | solution.py:290
  181.7 2.6 collective-permute-start.3
  184.3 0.1 select_reduce_fusion.1
  184.4 51.9 %collective-permute-done.3 = bf16[28,16,1024]{2,1,0:T(8,128)(2,1)} collective-permute-done((bf16[28,16,1024]{2,1,0:T(8,128)(2,1)}, bf16[28,16,1024]{2,1,0:T(8,128)(2,1)}, u32[]{:S(2)}, u32[]{:S(2)}) %collective-permute-start.3) | collective-permute-done | bytes 917536 | tf_op jit(solution)/shard_map/cond/branch_1_fun/ppermute | solution.py:300
  236.3 3.0 gather_fusion.3
  239.4 0.0 all-to-all-done.3.refs_0_
  239.4 6.7 %all-to-all-start.4 = ((bf16[8,6,16,1024]{3,2,1,0:T(8,128)(2,1)}), bf16[8,6,16,1024]{3,2,1,0:T(8,128)(2,1)}, u32[]{:S(2)}, u32[]{:S(2)}) async-start(bf16[8,6,16,1024]{3,2,1,0:T(8,128)(2,1)} %bitcast.89), calls=%async_computation.4 | async-start | bytes 3145728 | tf_op jit(solution)/shard_map/cond/branch_1_fun/all_to_all | solution.py:290
  246.1 1.0 collective-permute-start.2
  247.1 42.6 %collective-permute-done.2 = bf16[28,16,1024]{2,1,0:T(8,128)(2,1)} collective-permute-done((bf16[28,16,1024]{2,1,0:T(8,128)(2,1)}, bf16[28,16,1024]{2,1,0:T(8,128)(2,1)}, u32[]{:S(2)}, u32[]{:S(2)}) %collective-permute-start.2) | collective-permute-done | bytes 917536 | tf_op jit(solution)/shard_map/cond/branch_1_fun/ppermute | solution.py:300
  289.8 3.1 gather_fusion.2
  292.9 0.0 all-to-all-done.4.refs_0_
  292.9 4.3 %all-to-all-start.5 = ((bf16[8,6,16,1024]{3,2,1,0:T(8,128)(2,1)}), bf16[8,6,16,1024]{3,2,1,0:T(8,128)(2,1)}, u32[]{:S(2)}, u32[]{:S(2)}) async-start(bf16[8,6,16,1024]{3,2,1,0:T(8,128)(2,1)} %bitcast.84), calls=%async_computation.5 | async-start | bytes 3145728 | tf_op jit(solution)/shard_map/cond/branch_1_fun/all_to_all | solution.py:290
  297.2 0.7 reduce_sum.69
  297.9 3.5 %place.18.refs_1_ = bf16[6,256,2048]{2,1,0:T(8,128)(2,1)} custom-call(s32[1]{0:T(128)} %bitcast.9.filled_ref, s32[1]{0:T(128)} %bitcast.14.half_ref, bf16[8,6,16,2048]{3,2,1,0:T(8,128)(2,1)S(1)} %all-to-all-done.3.refs_0_), custom_call_target="tpu_custom_call" | custom-call | tf_op jit(solution)/shard_map/cond/branch_1_fun/place/pallas_call | solution.py:222
  301.4 0.1 reduce.2
  301.5 0.1 reshape.279
  301.6 28.9 %all-gather.1 = f32[16,1,384]{2,1,0:T(1,128)S(1)} all-gather(f32[1,1,384]{2,1,0:T(1,128)S(1)} %reshape.279), channel_id=1, replica_groups=mesh['layers'=2,'expert'=16] {'expert'}, dimensions={0}, use_global_device_ids=true | all-gather | bytes 26112 | tf_op jit(solution)/shard_map/cond/branch_1_fun/all_gather | solution.py:305
  330.5 0.1 copy.68
  330.7 0.2 copy.69
  330.9 0.8 reshape.163
  331.7 5.2 %place.19.refs_1_ = bf16[6,256,2048]{2,1,0:T(8,128)(2,1)} custom-call(s32[1]{0:T(128)} %bitcast.9.filled_ref, s32[1]{0:T(128)} %bitcast.10.half_ref, bf16[8,6,16,1024]{3,2,1,0:T(8,128)(2,1)} %all-to-all-done.4.refs_0_, bf16[6,256,2048]{2,1,0:T(8,128)(2,1)} %place.18.refs_1_), custom_call_target="tpu_custom_call", output_to_operand_aliasing={{}: (3, {})} | custom-call | tf_op jit(solution)/shard_map/cond/branch_1_fun/place/pallas_call | solution.py:222
  336.9 0.0 all-to-all-done.5.refs_0_
  336.9 5.2 %place.20 = bf16[6,256,2048]{2,1,0:T(8,128)(2,1)} custom-call(s32[1]{0:T(128)} %bitcast.9.filled_ref, s32[1]{0:T(128)} %bitcast.10.half_ref, bf16[8,6,16,1024]{3,2,1,0:T(8,128)(2,1)} %all-to-all-done.5.refs_0_, bf16[6,256,2048]{2,1,0:T(8,128)(2,1)} %place.19.refs_1_), custom_call_target="tpu_custom_call", output_to_operand_aliasing={{}: (3, {})} | custom-call | tf_op jit(solution)/shard_map/cond/branch_1_fun/place/pallas_call | solution.py:222
  (10 shorter events, 0.1 us)
Async XLA Ops:
  5.5 1.9 copy-start.4
  17.6 7.6 %copy-start.17 = (s32[48,1]{0,1:T(1,128)S(1)}, s32[48,1]{0,1:T(1,128)}, u32[]{:S(2)}) copy-start(s32[48,1]{0,1:T(1,128)} %param.20) | copy-start | bytes 580
  17.6 121.8 %copy-start.15 = (s32[8,2]{0,1:T(2,128)S(1)}, s32[8,2]{0,1:T(2,128)}, u32[]{:S(2)}) copy-start(s32[8,2]{0,1:T(2,128)} %param.17) | copy-start | bytes 196
  17.6 121.8 %copy-start.16 = (s32[16]{0:T(128)S(1)}, s32[16]{0:T(128)}, u32[]{:S(2)}) copy-start(s32[16]{0:T(128)} %param.18) | copy-start | bytes 196
  17.6 121.7 %all-to-all-start.15 = ((bf16[16,2,48,2048]{3,2,1,0:T(8,128)(2,1)}), bf16[16,2,48,2048]{3,2,1,0:T(8,128)(2,1)}, u32[]{:S(2)}, u32[]{:S(2)}) async-start(bf16[16,2,48,2048]{3,2,1,0:T(8,128)(2,1)} %prepare.1), calls=%async_computation.15 | async-start | bytes 12582912 | tf_op jit(solution)/shard_map/all_to_all | solution.py:283
  27.1 3.6 %collective-permute-start.10 = (s32[]{:T(128)}, s32[]{:T(128)}, u32[]{:S(2)}, u32[]{:S(2)}) collective-permute-start(s32[]{:T(128)} %max.7), channel_id=1, source_target_pairs={{0,16},{16,0},{1,17},{17,1},{2,18},{18,2},{3,19},{19,3},{4,20},{20... | collective-permute-start | bytes 20 | tf_op jit(solution)/shard_map/ppermute | solution.py:268
  150.9 1.7 copy-start.1
  152.6 1.0 copy-start.11
  153.6 1.0 copy-start.12
  154.6 84.8 %all-to-all-start.3 = ((bf16[8,6,16,2048]{3,2,1,0:T(8,128)(2,1)}), bf16[8,6,16,2048]{3,2,1,0:T(8,128)(2,1)S(1)}, u32[]{:S(2)}, u32[]{:S(2)}) async-start(bf16[8,6,16,2048]{3,2,1,0:T(8,128)(2,1)} %bitcast.79), calls=%async_computation.3 | async-start | bytes 6291456 | tf_op jit(solution)/shard_map/cond/branch_1_fun/all_to_all | solution.py:290
  181.7 54.6 %collective-permute-start.3 = (bf16[28,16,1024]{2,1,0:T(8,128)(2,1)}, bf16[28,16,1024]{2,1,0:T(8,128)(2,1)}, u32[]{:S(2)}, u32[]{:S(2)}) collective-permute-start(bf16[28,16,1024]{2,1,0:T(8,128)(2,1)} %copy-done.12), channel_id=1, source_target_pairs={{0,8},{1,9},{2,10},{3,11},{4,12},{5,13},{6,14},{7,15},{8,0},{9,1},... | collective-permute-start | bytes 2752520 | tf_op jit(solution)/shard_map/cond/branch_1_fun/ppermute | solution.py:300
  239.4 53.5 %all-to-all-start.4 = ((bf16[8,6,16,1024]{3,2,1,0:T(8,128)(2,1)}), bf16[8,6,16,1024]{3,2,1,0:T(8,128)(2,1)}, u32[]{:S(2)}, u32[]{:S(2)}) async-start(bf16[8,6,16,1024]{3,2,1,0:T(8,128)(2,1)} %bitcast.89), calls=%async_computation.4 | async-start | bytes 3145728 | tf_op jit(solution)/shard_map/cond/branch_1_fun/all_to_all | solution.py:290
  246.1 43.7 %collective-permute-start.2 = (bf16[28,16,1024]{2,1,0:T(8,128)(2,1)}, bf16[28,16,1024]{2,1,0:T(8,128)(2,1)}, u32[]{:S(2)}, u32[]{:S(2)}) collective-permute-start(bf16[28,16,1024]{2,1,0:T(8,128)(2,1)} %copy-done.11), channel_id=1, source_target_pairs={{0,8},{1,9},{2,10},{3,11},{4,12},{5,13},{6,14},{7,15},{8,0},{9,1},... | collective-permute-start | bytes 2752520 | tf_op jit(solution)/shard_map/cond/branch_1_fun/ppermute | solution.py:300
  292.9 44.0 %all-to-all-start.5 = ((bf16[8,6,16,1024]{3,2,1,0:T(8,128)(2,1)}), bf16[8,6,16,1024]{3,2,1,0:T(8,128)(2,1)}, u32[]{:S(2)}, u32[]{:S(2)}) async-start(bf16[8,6,16,1024]{3,2,1,0:T(8,128)(2,1)} %bitcast.84), calls=%async_computation.5 | async-start | bytes 3145728 | tf_op jit(solution)/shard_map/cond/branch_1_fun/all_to_all | solution.py:290

commit v3 on v2

--- a/solution.py
+++ b/solution.py
@@ -12,7 +12,9 @@
 U = 128
 CAP = 6
 EPSILON = 1e-06
-VMEM = 48 * 1024 * 1024
+VMEM = 60 * 1024 * 1024
+QUARTERS = 4
+LIST_PARTS = (14, 15, 16, 17, 18, 20, 24)
 
 
 def own_order(pairs, unit_order, width):
@@ -74,18 +76,9 @@
 
 
 def merge_kernel(
-    widths,
-    pairs_ref,
-    counts_ref,
-    near_ref,
-    place_ref,
-    left_ref,
-    right_ref,
-    similarity_ref,
-    near_out,
-    *rest,
+    pairs_ref, counts_ref, where_ref, place_ref, left_ref, right_ref, similarity_ref, *rest
 ):
-    far_outs, (ready, sems) = rest[: len(widths)], rest[len(widths) :]
+    outs, (ready, sems) = rest[:-2], rest[-2:]
     pair = pl.program_id(0)
     pair_count = pl.num_programs(0)
     per_device, depth = left_ref.shape[2], left_ref.shape[3]
@@ -128,30 +121,17 @@
     def each_copy(which_pair, which_slot, act):
         for piece in range(pieces):
             index = which_pair * pieces + piece
-            near = near_ref[index] == 1
-
-            @pl.when(near)
-            def _():
-                act(
-                    pltpu.make_async_copy(
-                        ready.at[which_slot, piece],
-                        near_out.at[place_ref[index]],
-                        sems.at[which_slot, piece, 0],
-                    )
-                )
-
-            @pl.when(jnp.logical_not(near))
-            def _():
-                begin = 0
-                for chunk, width in enumerate(widths):
+            for where, out_ref in enumerate(outs):
+
+                @pl.when(where_ref[index] == where)
+                def _():
                     act(
                         pltpu.make_async_copy(
-                            ready.at[which_slot, piece, :, pl.ds(begin, width)],
-                            far_outs[chunk].at[place_ref[index]],
-                            sems.at[which_slot, piece, chunk],
+                            ready.at[which_slot, piece],
+                            out_ref.at[place_ref[index]],
+                            sems.at[which_slot, piece],
                         )
                     )
-                    begin += width
 
     @pl.when(pair >= 2)
     def _():
@@ -166,11 +146,12 @@
         each_copy(pair, slot, lambda copy: copy.wait())
 
 
-def merge(pairs, counts, near, places, rows, slots, listed, widths):
+def merge(pairs, counts, where, places, rows, slots, listed):
     _, _, per_device, depth = rows.shape
     pair_count = pairs.shape[0]
-    pieces = near.shape[0] // pair_count
+    pieces = where.shape[0] // pair_count
     piece_rows = 2 * per_device // pieces
+    lengths = (slots,) + (listed,) * (QUARTERS - 1)
     grid_spec = pltpu.PrefetchScalarGridSpec(
         num_scalar_prefetch=4,
         grid=(pair_count,),
@@ -181,99 +162,90 @@
             ),
         ],
         out_specs=[pl.BlockSpec((1, per_device, 1), lambda p, *_: (p, 0, 0))]
-        + [pl.BlockSpec(memory_space=pl.ANY)] * (1 + len(widths)),
+        + [pl.BlockSpec(memory_space=pltpu.HBM)] * len(lengths),
         scratch_shapes=[
             pltpu.VMEM((2, pieces, piece_rows, depth), jnp.bfloat16),
-            pltpu.SemaphoreType.DMA((2, pieces, len(widths))),
+            pltpu.SemaphoreType.DMA((2, pieces)),
         ],
     )
     return pl.pallas_call(
-        functools.partial(merge_kernel, widths),
+        merge_kernel,
         grid_spec=grid_spec,
-        out_shape=[
-            jax.ShapeDtypeStruct((pair_count, per_device, 1), jnp.float32),
-            jax.ShapeDtypeStruct((slots, piece_rows, depth), jnp.bfloat16),
-        ]
-        + [jax.ShapeDtypeStruct((listed, piece_rows, width), jnp.bfloat16) for width in widths],
+        out_shape=[jax.ShapeDtypeStruct((pair_count, per_device, 1), jnp.float32)]
+        + [jax.ShapeDtypeStruct((length, piece_rows, depth), jnp.bfloat16) for length in lengths],
         compiler_params=pltpu.CompilerParams(vmem_limit_bytes=VMEM),
         name="merge",
-    )(pairs.reshape(-1), counts, near, places, rows, rows)
-
-
-def place_kernel(offset, filled_ref, in_ref, *rest):
+    )(pairs.reshape(-1), counts, where, places, rows, rows)
+
+
+def place_kernel(filled_ref, quarter_ref, in_ref, *rest):
     out_ref = rest[-1]
     value = in_ref[:, 0].reshape(out_ref.shape[1], out_ref.shape[2])
     keep = pl.program_id(0) < filled_ref[0]
     out_ref[0] = jnp.where(keep, value, jnp.zeros_like(value))
 
 
-def place(filled, half, arrived, begin, depth, base=None):
-    sources, cap, piece_rows, width = arrived.shape
+def place(filled, quarter, arrived, base=None):
+    sources, cap, piece_rows, depth = arrived.shape
+    bases = () if base is None else (base,)
     grid_spec = pltpu.PrefetchScalarGridSpec(
         num_scalar_prefetch=2,
         grid=(cap,),
-        in_specs=[pl.BlockSpec((sources, 1, piece_rows, width), lambda s, *_: (0, s, 0, 0))]
-        + ([] if base is None else [pl.BlockSpec(memory_space=pl.ANY)]),
+        in_specs=[pl.BlockSpec((sources, 1, piece_rows, depth), lambda s, *_: (0, s, 0, 0))]
+        + [pl.BlockSpec(memory_space=pltpu.HBM)] * len(bases),
         out_specs=pl.BlockSpec(
-            (1, sources * piece_rows, width),
-            lambda s, filled, half: (s, half[0], begin // width),
+            (1, sources * piece_rows, depth), lambda s, filled, quarter: (s, quarter[0], 0)
         ),
     )
     return pl.pallas_call(
-        lambda filled_ref, half_ref, *refs: place_kernel(None, filled_ref, *refs),
+        place_kernel,
         grid_spec=grid_spec,
-        out_shape=jax.ShapeDtypeStruct((cap, 2 * sources * piece_rows, depth), arrived.dtype),
-        input_output_aliases={} if base is None else {3: 0},
-        compiler_params=pltpu.CompilerParams(vmem_limit_bytes=VMEM),
+        out_shape=jax.ShapeDtypeStruct((cap, QUARTERS * sources * piece_rows, depth), arrived.dtype),
+        input_output_aliases={3: 0} if bases else {},
+        compiler_params=pltpu.CompilerParams(vmem_limit_bytes=VMEM // 4),
         name="place",
-    )(filled, half, arrived, *(() if base is None else (base,)))
+    )(filled, quarter, arrived, *bases)
 
 
 def body(gate_codes, up_codes, gate_scale, up_scale, pairs, counts, unit_order, owners):
     devices = lax.axis_size("expert")
     layers = lax.axis_size("layers")
     me = lax.axis_index("expert")
-    depth, units = gate_codes.shape[1:]
+    units = gate_codes.shape[2]
     pieces = units // U
     share_units = U // devices
-    per_device = pieces * share_units
-    half = devices // 2
-    side = me // half
+    size = devices // QUARTERS
+    quarter = me // size
     pair_count = pairs.shape[0]
     all_pieces = pair_count * pieces
-    widths = (depth // 2, depth // 2)
 
     owner_ids = owners[:, 0]
-    owner_side = owner_ids // half
+    owner_quarter = owner_ids // size
     earlier = jnp.arange(all_pieces)[None, :] < jnp.arange(all_pieces)[:, None]
     count_earlier = lambda values: jnp.sum(
         jnp.where((values[:, None] == values[None, :]) & earlier, 1, 0), axis=1
     ).astype(jnp.int32)
-    slot = (owner_ids % half) * CAP + count_earlier(owner_ids)
-    position = count_earlier(owner_side)
-    near = (owner_side == side).astype(jnp.int32)
-    places = jnp.where(near == 1, slot, position)
+    slot = (owner_ids % size) * CAP + count_earlier(owner_ids)
+    position = count_earlier(owner_quarter)
+    where = (owner_quarter - quarter + QUARTERS) % QUARTERS
+    places = jnp.where(where == 0, slot, position)
     filled = jnp.sum((owner_ids == me).astype(jnp.int32))[None]
     from_list = jnp.sum(
         jnp.where(
-            (jnp.arange(half * CAP)[:, None] == slot[None, :]) & (near == 1)[None, :],
+            (jnp.arange(size * CAP)[:, None] == slot[None, :]) & (where == 0)[None, :],
             position[None, :],
             0,
         ),
         axis=1,
     ).astype(jnp.int32)
-    ones = jnp.sum(owner_side).astype(jnp.int32)
-    longest = jnp.maximum(ones, all_pieces - ones)
+    here = (jnp.max(position) + 1).astype(jnp.int32)
+    longest = here
     for shift in range(1, layers):
-        other = lax.ppermute(
-            jnp.maximum(ones, all_pieces - ones),
-            "layers",
-            [(layer, (layer + shift) % layers) for layer in range(layers)],
-        )
-        longest = jnp.maximum(longest, other)
-    least = all_pieces // 2
-    sizes = [least + -(-least * part // 12) for part in (1, 2, 3, 6, 12)]
-    level = sum((longest > size).astype(jnp.int32) for size in sizes[:-1])
+        ring = [(layer, (layer + shift) % layers) for layer in range(layers)]
+        longest = jnp.maximum(longest, lax.ppermute(here, "layers", ring))
+    least = all_pieces // QUARTERS
+    lengths = sorted({min(size * CAP, -(-least * part // 12)) for part in LIST_PARTS})
+    level = sum((longest > length).astype(jnp.int32) for length in lengths[:-1])
 
     order = own_order(pairs, unit_order, units)
     source = order.reshape(pieces, devices, share_units).transpose(1, 0, 2).reshape(units)
@@ -282,42 +254,43 @@
     )
     rows = lax.all_to_all(outgoing, "expert", split_axis=0, concat_axis=0, tiled=True)
 
-    groups = [list(range(half)), list(range(half, devices))]
-    mirror = [(device, (device + half) % devices) for device in range(devices)]
-
-    def within_half(value):
-        value = value.reshape(half, CAP, value.shape[1], value.shape[2])
+    groups = [list(range(first, first + size)) for first in range(0, devices, size)]
+
+    def within_quarter(value):
+        value = value.reshape(size, CAP, value.shape[1], value.shape[2])
         return lax.all_to_all(
             value, "expert", split_axis=0, concat_axis=0, tiled=True, axis_index_groups=groups
         )
 
-    def deal(listed, rows, near, places, from_list):
+    def deal(listed, rows, where, places, from_list):
         similarity_part, slots, *lists = merge(
-            pairs, counts, near, places, rows, half * CAP, listed, widths
+            pairs, counts, where, places, rows, size * CAP, listed
         )
-        arrived = [within_half(slots)]
-        for chunk in lists:
-            chunk = lax.ppermute(chunk, "expert", mirror)
+        arrived = [within_quarter(slots)]
+        shifts = (2, 1, 3)
+        for step, shift in enumerate(shifts):
+            chunk = lists[shift - 1]
+            ring = [(device, (device + shift * size) % devices) for device in range(devices)]
+            chunk = lax.ppermute(chunk, "expert", ring)
             spread = jnp.take(chunk, from_list, axis=0, mode="clip")
             spread, arrived[-1] = lax.optimization_barrier((spread, arrived[-1]))
-            arrived.append(within_half(spread))
-        similarity_part, _ = lax.optimization_barrier((similarity_part, spread))
-        similarity = lax.all_gather(similarity_part.reshape(1, -1), "expert", axis=0, tiled=True)
+            arrived.append(within_quarter(spread))
+        merged, part = None, similarity_part.reshape(1, -1)
+        for step, (shift, value) in enumerate(zip((0,) + shifts, arrived)):
+            if step == len(shifts):
+                merged, part = lax.optimization_barrier((merged, part))
+            origin = ((quarter - shift + QUARTERS) % QUARTERS).astype(jnp.int32)[None]
+            merged = place(filled, origin, value, merged)
+        similarity = lax.all_gather(part, "expert", axis=0, tiled=True)
         similarity = similarity.reshape(devices, pair_count, pieces, share_units)
         similarity = similarity.transpose(1, 2, 0, 3).reshape(pair_count, units)
-        own, others = side.astype(jnp.int32)[None], (1 - side).astype(jnp.int32)[None]
-        merged = place(filled, own, arrived[0], 0, depth)
-        begin = 0
-        for width, value in zip(widths, arrived[1:]):
-            merged = place(filled, others, value, begin, depth, merged)
-            begin += width
         return merged, similarity
 
     return lax.switch(
         level,
-        [functools.partial(deal, size) for size in sizes],
+        [functools.partial(deal, length) for length in lengths],
         rows,
-        near,
+        where,
         places,
         from_list,
     )

time: 341 us -> 345 us (1.012); the launches traced: 342 us -> 340 us
  waiting for transfers between devices: 203 us -> 209 us
  Pallas kernels: 35.5 us -> 30.4 us
  blocking collectives: 28.9 us -> 23.9 us
    all_to_all x3 -> x4, starting transfers between devices: 38.1 us -> 22.2 us  [within_quarter(): lax.all_to_all(value, 'expert', split_axis=0, concat_axis=0, tiled=True,...]
    ppermute x3 -> x4, starting transfers between devices: 6.5 us -> 22.2 us  [the longest x3 19.3 us: deal(): chunk = lax.ppermute(chunk, 'expert', ring)]
    pallas_call x4 -> x5, Pallas kernels: 25.3 us -> 19.3 us  [the longest x1 10.8 us: merge(): pl.pallas_call(merge_kernel, grid_spec=grid_spec, out_shape=[jax.ShapeDty...]
    ppermute x3 -> x4, waiting for transfers between devices: 94.8 us -> 100 us  [the longest x3 99.6 us: deal(): chunk = lax.ppermute(chunk, 'expert', ring)]
    all_gather x1, blocking collectives: 28.9 us -> 23.9 us  [deal(): similarity = lax.all_gather(part, 'expert', axis=0, tiled=True)]
  transfers between devices with their start and end apart: 7 -> 9, of which waited for: 4 -> 5; matrix products, arithmetic and copies ran while one was open for 3% -> 3% of each run, Pallas kernels for 3% -> 1%
where the time goes in v3:
time: 345 us; the launch traced here: 340 us
  waiting for transfers between devices  209 us (61%)
  starting transfers between devices  52 us (15%)
  Pallas kernels  30.4 us (9%)
  blocking collectives  23.9 us (7%)
  local copies, waits for them, and re-layouts  16.7 us (5%)
  other arithmetic  6.69 us (2%)
    all_to_all x1, waiting for transfers between devices, body(): lax.all_to_all(outgoing, 'expert', split_axis=0, concat_axis=0, tiled=True)  108 us
    ppermute x3, waiting for transfers between devices, deal(): chunk = lax.ppermute(chunk, 'expert', ring)  99.6 us
    all_gather x1, blocking collectives, deal(): similarity = lax.all_gather(part, 'expert', axis=0, tiled=True)  23.9 us
    all_to_all x4, starting transfers between devices, within_quarter(): lax.all_to_all(value, 'expert', split_axis=0, concat_axis=0, tiled=True,...  22.2 us
    ppermute x3, starting transfers between devices, deal(): chunk = lax.ppermute(chunk, 'expert', ring)  19.3 us
    pallas_call x1, Pallas kernels, prepare(): pl.pallas_call(prepare_kernel, grid=(depth // tile,), in_specs=[pl.BlockS...  11.1 us
    pallas_call x1, Pallas kernels, merge(): pl.pallas_call(merge_kernel, grid_spec=grid_spec, out_shape=[jax.ShapeDty...  10.8 us
    pallas_call x4, Pallas kernels, place(): pl.pallas_call(place_kernel, grid_spec=grid_spec, out_shape=jax.ShapeDtyp...  8.53 us
  transfers between devices with their start and end apart: 9, of which 5 were waited for; matrix products, arithmetic and copies ran while one was open for 3% of the time, Pallas kernels for 1%

profile of v3, /device:TPU:0, one launch (start us, length us, event | category | flops | bytes accessed | tf_op | source)
XLA Modules:
  0.0 340.4 jit_solution(17536992638909485440)
XLA Ops:
  0.6 0.7 bitcast_convert_fusion.1
  1.3 0.1 copy.144
  1.4 0.7 bitcast_convert_fusion
  2.1 0.1 copy.145
  2.2 1.3 compare_reduce_fusion
  3.5 0.8 select_reduce_fusion.7
  4.3 0.1 reduce_sum.50
  4.4 0.7 select_bitcast_fusion
  5.1 0.1 broadcast_in_dim.186
  5.2 0.7 reshape_reshape.7.up_scale_ref
  5.8 0.1 broadcast_in_dim.185
  5.9 0.7 reshape_reshape.6.gate_scale_ref
  6.6 0.9 broadcast_in_dim_reshape.4.source_ref
  7.4 11.1 %prepare.1 = bf16[16,2,48,2048]{3,2,1,0:T(8,128)(2,1)} custom-call(s32[768,1]{1,0:T(8,128)} %broadcast_in_dim_reshape.4.source_ref, bf16[2048,768]{1,0:T(8,128)(2,1)} %bitcast.142, bf16[2048,768]{1,0:T(8,128)(2,1)} %bitcast.143, f32[8,2,768]{2,1,0:T(2,128)} %reshape_reshape.6.gate_scale_ref, f32[8,2,768]{2,1,0:T(2,128)} %reshape_reshape.7.up_scale_ref), custom_call_target="tpu_custom_call" | custom-call | tf_op jit(solution)/shard_map/prepare/pallas_call | solution.py:60
  18.5 0.0 copy-start.29
  18.5 7.5 %all-to-all-start.28 = ((bf16[16,2,48,2048]{3,2,1,0:T(8,128)(2,1)}), bf16[16,2,48,2048]{3,2,1,0:T(8,128)(2,1)}, u32[]{:S(2)}, u32[]{:S(2)}) async-start(bf16[16,2,48,2048]{3,2,1,0:T(8,128)(2,1)} %prepare.1), calls=%async_computation.28 | async-start | bytes 12582912 | tf_op jit(solution)/shard_map/all_to_all | solution.py:255
  26.1 0.0 copy-done.30
  26.1 0.2 select_reduce_fusion.9
  26.3 0.6 reduce_max.9
  27.6 2.9 collective-permute-start.21
  30.5 0.2 select_reduce_fusion.8
  30.7 0.6 collective-permute-done.21
  31.9 108.4 %all-to-all-done.28 = bf16[16,2,48,2048]{3,2,1,0:T(8,128)(2,1)} async-done(((bf16[16,2,48,2048]{3,2,1,0:T(8,128)(2,1)}), bf16[16,2,48,2048]{3,2,1,0:T(8,128)(2,1)}, u32[]{:S(2)}, u32[]{:S(2)}) %all-to-all-start.28) | async-done | bytes 6291488 | tf_op jit(solution)/shard_map/all_to_all | solution.py:255
  140.3 0.0 copy-done.28
  140.3 0.0 copy-done.29
  140.3 200.1 %conditional.1 = (bf16[6,256,2048]{2,1,0:T(8,128)(2,1)}, f32[8,768]{1,0:T(8,128)}) conditional(s32[]{:T(128)} %clamp.3, (s32[]{:T(128)}, s32[8,2]{0,1:T(2,128)S(1)}, s32[16]{0:T(128)S(1)}, s32[48]{0:T(128)S(1)}, pred[48]{0:T(512)(128)(4,1)S(1)}, /*index=5*/bf16[16,2,48,2048]{3,2,1,0:T(8,128)(2,1)}, ...), branch_computations={%region_7.8_spmd, %region_8.9_spmd, %region_9.10_spmd, %region_10.... | conditional | flops 5751 | bytes 85132080 | solution.py:289
  140.3 0.1 copy.149
  140.4 0.6 reshape.219.pairs_ref
  141.0 0.6 select_n.193.place_ref
  141.6 10.8 %merge.9 = (f32[8,48,1]{2,1,0:T(8,128)}, bf16[24,16,2048]{2,1,0:T(8,128)(2,1)}, bf16[16,16,2048]{2,1,0:T(8,128)(2,1)}, bf16[16,16,2048]{2,1,0:T(8,128)(2,1)}, bf16[16,16,2048]{2,1,0:T(8,128)(2,1)}) custom-call(s32[16]{0:T(128)} %reshape.219.pairs_ref, s32[16]{0:T(128)S(1)} %get-tuple-element.314.counts_ref, s32[48]{0:T(128)S(1)} %get-tuple-element.158.where_ref, ...), custom_call_target="tpu_custom_call" | custom-call | tf_op jit(solution)/shard_map/cond/branch_2_fun/merge/pallas_call | solution.py:171
  152.4 10.6 %all-to-all-start.8 = ((bf16[4,6,16,2048]{3,2,1,0:T(8,128)(2,1)}), bf16[4,6,16,2048]{3,2,1,0:T(8,128)(2,1)S(1)}, u32[]{:S(2)}, u32[]{:S(2)}) async-start(bf16[4,6,16,2048]{3,2,1,0:T(8,128)(2,1)} %bitcast.149), calls=%async_computation.8 | async-start | bytes 3145728 | tf_op jit(solution)/shard_map/cond/branch_2_fun/all_to_all | solution.py:261
  163.0 19.2 %collective-permute-start.8 = (bf16[16,16,2048]{2,1,0:T(8,128)(2,1)}, bf16[16,16,2048]{2,1,0:T(8,128)(2,1)S(1)}, u32[]{:S(2)}, u32[]{:S(2)}) collective-permute-start(bf16[16,16,2048]{2,1,0:T(8,128)(2,1)} %get-tuple-element.164), channel_id=1, source_target_pairs={{0,8},{1,9},{2,10},{3,11},{4,12},{5,13},{6,14},{7,15},{8,0},{9,1},... | collective-permute-start | bytes 3145736 | tf_op jit(solution)/shard_map/cond/branch_2_fun/ppermute | solution.py:274
  182.2 0.1 select_reduce_fusion.2
  182.3 46.3 %collective-permute-done.8 = bf16[16,16,2048]{2,1,0:T(8,128)(2,1)S(1)} collective-permute-done((bf16[16,16,2048]{2,1,0:T(8,128)(2,1)}, bf16[16,16,2048]{2,1,0:T(8,128)(2,1)S(1)}, u32[]{:S(2)}, u32[]{:S(2)}) %collective-permute-start.8) | collective-permute-done | bytes 1048608 | tf_op jit(solution)/shard_map/cond/branch_2_fun/ppermute | solution.py:274
  228.6 1.9 gather_fusion.8
  230.5 0.0 all-to-all-done.8.in_ref
  230.5 1.2 copy-done.4
  231.7 3.6 %all-to-all-start.9 = ((bf16[4,6,16,2048]{3,2,1,0:T(8,128)(2,1)}), bf16[4,6,16,2048]{3,2,1,0:T(8,128)(2,1)S(1)}, u32[]{:S(2)}, u32[]{:S(2)}) async-start(bf16[4,6,16,2048]{3,2,1,0:T(8,128)(2,1)} %bitcast.29), calls=%async_computation.9 | async-start | bytes 3145728 | tf_op jit(solution)/shard_map/cond/branch_2_fun/all_to_all | solution.py:261
  235.3 0.1 collective-permute-start.7
  235.4 27.5 %collective-permute-done.7 = bf16[16,16,2048]{2,1,0:T(8,128)(2,1)S(1)} collective-permute-done((bf16[16,16,2048]{2,1,0:T(8,128)(2,1)}, bf16[16,16,2048]{2,1,0:T(8,128)(2,1)S(1)}, u32[]{:S(2)}, u32[]{:S(2)}) %collective-permute-start.7) | collective-permute-done | bytes 1048608 | tf_op jit(solution)/shard_map/cond/branch_2_fun/ppermute | solution.py:274
  262.8 1.8 gather_fusion.7
  264.7 0.0 all-to-all-done.9.in_ref
  264.7 3.6 %all-to-all-start.10 = ((bf16[4,6,16,2048]{3,2,1,0:T(8,128)(2,1)}), bf16[4,6,16,2048]{3,2,1,0:T(8,128)(2,1)S(1)}, u32[]{:S(2)}, u32[]{:S(2)}) async-start(bf16[4,6,16,2048]{3,2,1,0:T(8,128)(2,1)} %bitcast.137), calls=%async_computation.10 | async-start | bytes 3145728 | tf_op jit(solution)/shard_map/cond/branch_2_fun/all_to_all | solution.py:261
  268.3 0.1 collective-permute-start.6
  268.3 25.8 %collective-permute-done.6 = bf16[16,16,2048]{2,1,0:T(8,128)(2,1)} collective-permute-done((bf16[16,16,2048]{2,1,0:T(8,128)(2,1)}, bf16[16,16,2048]{2,1,0:T(8,128)(2,1)}, u32[]{:S(2)}, u32[]{:S(2)}) %collective-permute-start.6) | collective-permute-done | bytes 1048608 | tf_op jit(solution)/shard_map/cond/branch_2_fun/ppermute | solution.py:274
  294.1 3.1 gather_fusion.6
  297.3 0.0 all-to-all-done.10.in_ref
  297.3 4.5 %all-to-all-start.11 = ((bf16[4,6,16,2048]{3,2,1,0:T(8,128)(2,1)}), bf16[4,6,16,2048]{3,2,1,0:T(8,128)(2,1)}, u32[]{:S(2)}, u32[]{:S(2)}) async-start(bf16[4,6,16,2048]{3,2,1,0:T(8,128)(2,1)} %bitcast.130), calls=%async_computation.11 | async-start | bytes 3145728 | tf_op jit(solution)/shard_map/cond/branch_2_fun/all_to_all | solution.py:261
  301.8 0.7 reduce_sum.62
  302.5 0.1 reduce.3
  302.6 0.1 reshape.224
  302.7 0.0 copy-start.5
  302.7 1.4 copy-done.5
  304.1 1.1 place.36.rest_0_
  305.2 1.1 place.37.rest_0_
  306.3 1.1 place.38.rest_0_
  307.4 0.0 copy-start.16
  307.4 2.7 copy-done.16
  310.1 23.9 %all-gather.2 = f32[16,1,384]{2,1,0:T(1,128)S(1)} all-gather(f32[1,1,384]{2,1,0:T(1,128)S(1)} %bitcast.160), channel_id=1, replica_groups=mesh['layers'=2,'expert'=16] {'expert'}, dimensions={0}, use_global_device_ids=true | all-gather | bytes 26112 | tf_op jit(solution)/shard_map/cond/branch_2_fun/all_gather | solution.py:284
  334.0 0.1 copy.133
  334.2 0.2 copy.134
  334.4 0.8 reshape.226
  335.2 0.0 all-to-all-done.11.in_ref
  335.2 5.2 %place.39 = bf16[6,256,2048]{2,1,0:T(8,128)(2,1)} custom-call(s32[1]{0:T(128)} %bitcast.26.filled_ref, s32[1]{0:T(128)} %bitcast.27.quarter_ref, bf16[4,6,16,2048]{3,2,1,0:T(8,128)(2,1)} %all-to-all-done.11.in_ref, bf16[6,256,2048]{2,1,0:T(8,128)(2,1)} %copy-done.16), custom_call_target="tpu_custom_call", output_to_operand_aliasing={{}: (3, {})} | custom-call | tf_op jit(solution)/shard_map/cond/branch_2_fun/place/pallas_call | solution.py:200
  (11 shorter events, 0.1 us)
Async XLA Ops:
  18.5 7.6 %copy-start.30 = (s32[48,1]{0,1:T(1,128)S(1)}, s32[48,1]{0,1:T(1,128)}, u32[]{:S(2)}) copy-start(s32[48,1]{0,1:T(1,128)} %param.22) | copy-start | bytes 580
  18.5 121.8 %copy-start.28 = (s32[8,2]{0,1:T(2,128)S(1)}, s32[8,2]{0,1:T(2,128)}, u32[]{:S(2)}) copy-start(s32[8,2]{0,1:T(2,128)} %param.19) | copy-start | bytes 196
  18.5 121.8 %copy-start.29 = (s32[16]{0:T(128)S(1)}, s32[16]{0:T(128)}, u32[]{:S(2)}) copy-start(s32[16]{0:T(128)} %param.20) | copy-start | bytes 196
  18.5 121.8 %all-to-all-start.28 = ((bf16[16,2,48,2048]{3,2,1,0:T(8,128)(2,1)}), bf16[16,2,48,2048]{3,2,1,0:T(8,128)(2,1)}, u32[]{:S(2)}, u32[]{:S(2)}) async-start(bf16[16,2,48,2048]{3,2,1,0:T(8,128)(2,1)} %prepare.1), calls=%async_computation.28 | async-start | bytes 12582912 | tf_op jit(solution)/shard_map/all_to_all | solution.py:255
  27.6 3.7 %collective-permute-start.21 = (s32[]{:T(128)}, s32[]{:T(128)}, u32[]{:S(2)}, u32[]{:S(2)}) collective-permute-start(s32[]{:T(128)} %add.295), channel_id=1, source_target_pairs={{0,16},{16,0},{1,17},{17,1},{2,18},{18,2},{3,19},{19,3},{4,20},{20... | collective-permute-start | bytes 20 | tf_op jit(solution)/shard_map/ppermute | solution.py:245
  152.4 78.2 %all-to-all-start.8 = ((bf16[4,6,16,2048]{3,2,1,0:T(8,128)(2,1)}), bf16[4,6,16,2048]{3,2,1,0:T(8,128)(2,1)S(1)}, u32[]{:S(2)}, u32[]{:S(2)}) async-start(bf16[4,6,16,2048]{3,2,1,0:T(8,128)(2,1)} %bitcast.149), calls=%async_computation.8 | async-start | bytes 3145728 | tf_op jit(solution)/shard_map/cond/branch_2_fun/all_to_all | solution.py:261
  163.0 65.6 %collective-permute-start.8 = (bf16[16,16,2048]{2,1,0:T(8,128)(2,1)}, bf16[16,16,2048]{2,1,0:T(8,128)(2,1)S(1)}, u32[]{:S(2)}, u32[]{:S(2)}) collective-permute-start(bf16[16,16,2048]{2,1,0:T(8,128)(2,1)} %get-tuple-element.164), channel_id=1, source_target_pairs={{0,8},{1,9},{2,10},{3,11},{4,12},{5,13},{6,14},{7,15},{8,0},{9,1},... | collective-permute-start | bytes 3145736 | tf_op jit(solution)/shard_map/cond/branch_2_fun/ppermute | solution.py:274
  230.5 1.2 copy-start.4
  231.7 33.0 %all-to-all-start.9 = ((bf16[4,6,16,2048]{3,2,1,0:T(8,128)(2,1)}), bf16[4,6,16,2048]{3,2,1,0:T(8,128)(2,1)S(1)}, u32[]{:S(2)}, u32[]{:S(2)}) async-start(bf16[4,6,16,2048]{3,2,1,0:T(8,128)(2,1)} %bitcast.29), calls=%async_computation.9 | async-start | bytes 3145728 | tf_op jit(solution)/shard_map/cond/branch_2_fun/all_to_all | solution.py:261
  235.3 27.6 %collective-permute-start.7 = (bf16[16,16,2048]{2,1,0:T(8,128)(2,1)}, bf16[16,16,2048]{2,1,0:T(8,128)(2,1)S(1)}, u32[]{:S(2)}, u32[]{:S(2)}) collective-permute-start(bf16[16,16,2048]{2,1,0:T(8,128)(2,1)} %get-tuple-element.163), channel_id=1, source_target_pairs={{0,4},{1,5},{2,6},{3,7},{4,8},{5,9},{6,10},{7,11},{8,12},{9,13},{1... | collective-permute-start | bytes 3145736 | tf_op jit(solution)/shard_map/cond/branch_2_fun/ppermute | solution.py:274
  264.7 32.6 %all-to-all-start.10 = ((bf16[4,6,16,2048]{3,2,1,0:T(8,128)(2,1)}), bf16[4,6,16,2048]{3,2,1,0:T(8,128)(2,1)S(1)}, u32[]{:S(2)}, u32[]{:S(2)}) async-start(bf16[4,6,16,2048]{3,2,1,0:T(8,128)(2,1)} %bitcast.137), calls=%async_computation.10 | async-start | bytes 3145728 | tf_op jit(solution)/shard_map/cond/branch_2_fun/all_to_all | solution.py:261
  268.3 25.9 %collective-permute-start.6 = (bf16[16,16,2048]{2,1,0:T(8,128)(2,1)}, bf16[16,16,2048]{2,1,0:T(8,128)(2,1)}, u32[]{:S(2)}, u32[]{:S(2)}) collective-permute-start(bf16[16,16,2048]{2,1,0:T(8,128)(2,1)} %get-tuple-element.161), channel_id=1, source_target_pairs={{0,12},{1,13},{2,14},{3,15},{4,0},{5,1},{6,2},{7,3},{8,4},{9,5},{1... | collective-permute-start | bytes 3145736 | tf_op jit(solution)/shard_map/cond/branch_2_fun/ppermute | solution.py:274
  297.3 5.2 %copy-start.23 = (f32[8,48,1]{2,1,0:T(8,128)S(1)}, f32[8,48,1]{2,1,0:T(8,128)}, u32[]{:S(2)}) copy-start(f32[8,48,1]{2,1,0:T(8,128)} %get-tuple-element.172) | copy-start | bytes 4612 | tf_op jit(solution)/shard_map/cond
  297.3 37.9 %all-to-all-start.11 = ((bf16[4,6,16,2048]{3,2,1,0:T(8,128)(2,1)}), bf16[4,6,16,2048]{3,2,1,0:T(8,128)(2,1)}, u32[]{:S(2)}, u32[]{:S(2)}) async-start(bf16[4,6,16,2048]{3,2,1,0:T(8,128)(2,1)} %bitcast.130), calls=%async_computation.11 | async-start | bytes 3145728 | tf_op jit(solution)/shard_map/cond/branch_2_fun/all_to_all | solution.py:261
  302.7 1.4 copy-start.5
  307.4 2.7 copy-start.16

commit v4 on v3

--- a/solution.py
+++ b/solution.py
@@ -10,6 +10,7 @@
 
 BLK = 128
 U = 128
+LANES = 128
 CAP = 6
 EPSILON = 1e-06
 VMEM = 60 * 1024 * 1024
@@ -78,7 +79,7 @@
 def merge_kernel(
     pairs_ref, counts_ref, where_ref, place_ref, left_ref, right_ref, similarity_ref, *rest
 ):
-    outs, (ready, sems) = rest[:-2], rest[-2:]
+    outs, (woven, ready, sems) = rest[:-3], rest[-3:]
     pair = pl.program_id(0)
     pair_count = pl.num_programs(0)
     per_device, depth = left_ref.shape[2], left_ref.shape[3]
@@ -103,19 +104,12 @@
     total = left_freq + share
     left_weight = left_freq / total
     right_weight = share / total
-    merged = jnp.concatenate(
-        (
-            left_weight * left_gate + right_weight * right_gate,
-            left_weight * left_up + right_weight * right_up,
-        ),
-        axis=0,
-    ).astype(jnp.bfloat16)
-    to_row = lax.broadcasted_iota(jnp.int32, (2 * per_device, 2 * per_device), 0)
-    from_row = lax.broadcasted_iota(jnp.int32, (2 * per_device, 2 * per_device), 1)
-    weave = from_row == jnp.right_shift(to_row, 1) + per_device * jnp.bitwise_and(to_row, 1)
-    woven = jnp.dot(
-        weave.astype(jnp.float32).astype(jnp.bfloat16), merged, preferred_element_type=jnp.float32
-    )
+    for kind, (left, right) in enumerate(((left_gate, right_gate), (left_up, right_up))):
+        merged = left_weight * left + right_weight * right
+        for block in range(depth // LANES):
+            woven[block, pl.ds(kind, per_device, stride=2), :] = merged[
+                :, block * LANES : (block + 1) * LANES
+            ]
     slot = lax.rem(pair, 2)
 
     def each_copy(which_pair, which_slot, act):
@@ -137,7 +131,10 @@
     def _():
         each_copy(pair - 2, slot, lambda copy: copy.wait())
 
-    ready[slot] = woven.astype(jnp.bfloat16).reshape(pieces, piece_rows, depth)
+    for block in range(depth // LANES):
+        ready[slot, :, :, block * LANES : (block + 1) * LANES] = (
+            woven[block].reshape(pieces, piece_rows, LANES).astype(jnp.bfloat16)
+        )
     each_copy(pair, slot, lambda copy: copy.start())
 
     @pl.when(pair == pair_count - 1)
@@ -164,6 +161,7 @@
         out_specs=[pl.BlockSpec((1, per_device, 1), lambda p, *_: (p, 0, 0))]
         + [pl.BlockSpec(memory_space=pltpu.HBM)] * len(lengths),
         scratch_shapes=[
+            pltpu.VMEM((depth // LANES, 2 * per_device, LANES), jnp.float32),
             pltpu.VMEM((2, pieces, piece_rows, depth), jnp.bfloat16),
             pltpu.SemaphoreType.DMA((2, pieces)),
         ],
@@ -180,21 +178,24 @@
 
 def place_kernel(filled_ref, quarter_ref, in_ref, *rest):
     out_ref = rest[-1]
-    value = in_ref[:, 0].reshape(out_ref.shape[1], out_ref.shape[2])
-    keep = pl.program_id(0) < filled_ref[0]
-    out_ref[0] = jnp.where(keep, value, jnp.zeros_like(value))
+    slots = out_ref.shape[0]
+    for slot in range(slots):
+        value = in_ref[:, slot].reshape(out_ref.shape[1:])
+        keep = pl.program_id(0) * slots + slot < filled_ref[0]
+        out_ref[slot] = jnp.where(keep, value, jnp.zeros_like(value))
 
 
 def place(filled, quarter, arrived, base=None):
     sources, cap, piece_rows, depth = arrived.shape
+    slots = 2
     bases = () if base is None else (base,)
     grid_spec = pltpu.PrefetchScalarGridSpec(
         num_scalar_prefetch=2,
-        grid=(cap,),
-        in_specs=[pl.BlockSpec((sources, 1, piece_rows, depth), lambda s, *_: (0, s, 0, 0))]
+        grid=(cap // slots,),
+        in_specs=[pl.BlockSpec((sources, slots, piece_rows, depth), lambda s, *_: (0, s, 0, 0))]
         + [pl.BlockSpec(memory_space=pltpu.HBM)] * len(bases),
         out_specs=pl.BlockSpec(
-            (1, sources * piece_rows, depth), lambda s, filled, quarter: (s, quarter[0], 0)
+            (slots, sources * piece_rows, depth), lambda s, filled, quarter: (s, quarter[0], 0)
         ),
     )
     return pl.pallas_call(
@@ -269,19 +270,24 @@
         arrived = [within_quarter(slots)]
         shifts = (2, 1, 3)
         for step, shift in enumerate(shifts):
-            chunk = lists[shift - 1]
             ring = [(device, (device + shift * size) % devices) for device in range(devices)]
-            chunk = lax.ppermute(chunk, "expert", ring)
+            chunk = lax.ppermute(lists[shift - 1], "expert", ring)
             spread = jnp.take(chunk, from_list, axis=0, mode="clip")
-            spread, arrived[-1] = lax.optimization_barrier((spread, arrived[-1]))
+            if step == 0:
+                part, arrived[0] = lax.optimization_barrier(
+                    (similarity_part.reshape(1, -1), arrived[0])
+                )
+                similarity = lax.all_to_all(
+                    jnp.broadcast_to(part, (devices, part.shape[1])), "expert", 0, 0, tiled=True
+                )
+                spread, similarity = lax.optimization_barrier((spread, similarity))
+            else:
+                spread, arrived[-1] = lax.optimization_barrier((spread, arrived[-1]))
             arrived.append(within_quarter(spread))
-        merged, part = None, similarity_part.reshape(1, -1)
-        for step, (shift, value) in enumerate(zip((0,) + shifts, arrived)):
-            if step == len(shifts):
-                merged, part = lax.optimization_barrier((merged, part))
+        merged = None
+        for shift, value in zip((0,) + shifts, arrived):
             origin = ((quarter - shift + QUARTERS) % QUARTERS).astype(jnp.int32)[None]
             merged = place(filled, origin, value, merged)
-        similarity = lax.all_gather(part, "expert", axis=0, tiled=True)
         similarity = similarity.reshape(devices, pair_count, pieces, share_units)
         similarity = similarity.transpose(1, 2, 0, 3).reshape(pair_count, units)
         return merged, similarity

time: 345 us -> 327 us (0.948); the launches traced: 340 us -> 332 us
  blocking collectives: 23.9 us -> 0 us
  starting transfers between devices: 52 us -> 72.1 us
  waiting for transfers between devices: 209 us -> 202 us
    all_gather x1 -> x0, blocking collectives: 23.9 us -> none  [deal(): similarity = lax.all_gather(part, 'expert', axis=0, tiled=True)]
    all_to_all x0 -> x1, starting transfers between devices: none -> 20 us  [deal(): lax.all_to_all(jnp.broadcast_to(part, (devices, part.shape[1])), 'expert'...]
    ppermute x3, waiting for transfers between devices: 99.6 us -> 83.6 us  [deal(): chunk = lax.ppermute(lists[shift - 1], 'expert', ring)]
    all_to_all x4, waiting for transfers between devices: 0.01 us -> 9.42 us  [within_quarter(): lax.all_to_all(value, 'expert', split_axis=0, concat_axis=0, tiled=True,...]
    cond x8 -> x14, local copies, waits for them, and re-layouts: 5.3 us -> 1.43 us
  transfers between devices with their start and end apart: 9 -> 10, of which waited for: 5 -> 7; matrix products, arithmetic and copies ran while one was open for 3% -> 3% of each run, Pallas kernels for 1% -> 2%
where the time goes in v4:
time: 327 us; the launch traced here: 332 us
  waiting for transfers between devices  202 us (62%)
  starting transfers between devices  72.1 us (22%)
  Pallas kernels  33.1 us (10%)
  local copies, waits for them, and re-layouts  15.1 us (5%)
  other arithmetic  6.76 us (2%)
    all_to_all x1, waiting for transfers between devices, body(): lax.all_to_all(outgoing, 'expert', split_axis=0, concat_axis=0, tiled=True)  108 us
    ppermute x3, waiting for transfers between devices, deal(): chunk = lax.ppermute(lists[shift - 1], 'expert', ring)  83.6 us
    all_to_all x4, starting transfers between devices, within_quarter(): lax.all_to_all(value, 'expert', split_axis=0, concat_axis=0, tiled=True,...  22.3 us
    all_to_all x1, starting transfers between devices, deal(): lax.all_to_all(jnp.broadcast_to(part, (devices, part.shape[1])), 'expert'...  20 us
    ppermute x3, starting transfers between devices, deal(): chunk = lax.ppermute(lists[shift - 1], 'expert', ring)  19.4 us
    pallas_call x4, Pallas kernels, place(): pl.pallas_call(place_kernel, grid_spec=grid_spec, out_shape=jax.ShapeDtyp...  11.7 us
    pallas_call x1, Pallas kernels, prepare(): pl.pallas_call(prepare_kernel, grid=(depth // tile,), in_specs=[pl.BlockS...  11.1 us
    pallas_call x1, Pallas kernels, merge(): pl.pallas_call(merge_kernel, grid_spec=grid_spec, out_shape=[jax.ShapeDty...  10.4 us
  transfers between devices with their start and end apart: 10, of which 7 were waited for; matrix products, arithmetic and copies ran while one was open for 3% of the time, Pallas kernels for 2%

profile of v4, /device:TPU:0, one launch (start us, length us, event | category | flops | bytes accessed | tf_op | source)
XLA Modules:
  0.0 331.6 jit_solution(722241326501454259)
XLA Ops:
  0.6 0.7 bitcast_convert_fusion.1
  1.3 0.1 copy.119
  1.4 0.7 bitcast_convert_fusion
  2.1 0.1 copy.120
  2.2 1.3 compare_reduce_fusion
  3.5 0.8 select_reduce_fusion.7
  4.3 0.1 reduce_sum.50
  4.4 0.7 select_bitcast_fusion
  5.1 0.1 broadcast_in_dim.221
  5.2 0.7 reshape_reshape.7.up_scale_ref
  5.8 0.1 broadcast_in_dim.220
  5.9 0.7 reshape_reshape.6.gate_scale_ref
  6.5 0.9 broadcast_in_dim_reshape.4.source_ref
  7.5 11.1 %prepare.1 = bf16[16,2,48,2048]{3,2,1,0:T(8,128)(2,1)} custom-call(s32[768,1]{1,0:T(8,128)} %broadcast_in_dim_reshape.4.source_ref, bf16[2048,768]{1,0:T(8,128)(2,1)} %bitcast.142, bf16[2048,768]{1,0:T(8,128)(2,1)} %bitcast.143, f32[8,2,768]{2,1,0:T(2,128)} %reshape_reshape.6.gate_scale_ref, f32[8,2,768]{2,1,0:T(2,128)} %reshape_reshape.7.up_scale_ref), custom_call_target="tpu_custom_call" | custom-call | tf_op jit(solution)/shard_map/prepare/pallas_call | solution.py:61
  18.5 0.0 copy-start.46
  18.5 7.5 %all-to-all-start.35 = ((bf16[16,2,48,2048]{3,2,1,0:T(8,128)(2,1)}), bf16[16,2,48,2048]{3,2,1,0:T(8,128)(2,1)}, u32[]{:S(2)}, u32[]{:S(2)}) async-start(bf16[16,2,48,2048]{3,2,1,0:T(8,128)(2,1)} %prepare.1), calls=%async_computation.35 | async-start | bytes 12582912 | tf_op jit(solution)/shard_map/all_to_all | solution.py:256
  26.1 0.0 copy-done.47
  26.1 0.2 select_reduce_fusion.9
  26.3 0.6 reduce_max.9
  27.6 2.9 collective-permute-start.21
  30.5 0.2 select_reduce_fusion.8
  30.7 0.6 collective-permute-done.21
  32.0 108.3 %all-to-all-done.35 = bf16[16,2,48,2048]{3,2,1,0:T(8,128)(2,1)} async-done(((bf16[16,2,48,2048]{3,2,1,0:T(8,128)(2,1)}), bf16[16,2,48,2048]{3,2,1,0:T(8,128)(2,1)}, u32[]{:S(2)}, u32[]{:S(2)}) %all-to-all-start.35) | async-done | bytes 6291488 | tf_op jit(solution)/shard_map/all_to_all | solution.py:256
  140.3 0.0 copy-done.45
  140.3 0.0 copy-done.46
  140.3 191.3 %conditional.1 = (bf16[6,256,2048]{2,1,0:T(8,128)(2,1)}, f32[8,768]{1,0:T(8,128)}) conditional(s32[]{:T(128)} %clamp.3, (s32[]{:T(128)}, s32[8,2]{0,1:T(2,128)S(1)}, s32[16]{0:T(128)S(1)}, s32[48]{0:T(128)S(1)}, pred[48]{0:T(512)(128)(4,1)S(1)}, /*index=5*/bf16[16,2,48,2048]{3,2,1,0:T(8,128)(2,1)}, ...), branch_computations={%region_7.8_spmd, %region_8.9_spmd, %region_9.10_spmd, %region_10.... | conditional | flops 5751 | bytes 60047832 | solution.py:295
  140.5 0.1 copy.125
  140.6 0.6 reshape.269.pairs_ref
  141.2 0.6 select_n.194.place_ref
  141.8 10.4 %merge.10 = (f32[8,48,1]{2,1,0:T(8,128)}, bf16[24,16,2048]{2,1,0:T(8,128)(2,1)}, bf16[17,16,2048]{2,1,0:T(8,128)(2,1)}, bf16[17,16,2048]{2,1,0:T(8,128)(2,1)}, bf16[17,16,2048]{2,1,0:T(8,128)(2,1)}) custom-call(s32[16]{0:T(128)} %reshape.269.pairs_ref, s32[16]{0:T(128)S(1)} %get-tuple-element.315.counts_ref, s32[48]{0:T(128)S(1)} %get-tuple-element.179.where_ref, ...), custom_call_target="tpu_custom_call" | custom-call | tf_op jit(solution)/shard_map/cond/branch_3_fun/merge/pallas_call | solution.py:169
  152.2 10.8 %all-to-all-start.15 = ((bf16[4,6,16,2048]{3,2,1,0:T(8,128)(2,1)}), bf16[4,6,16,2048]{3,2,1,0:T(8,128)(2,1)S(1)}, u32[]{:S(2)}, u32[]{:S(2)}) async-start(bf16[4,6,16,2048]{3,2,1,0:T(8,128)(2,1)} %bitcast.150), calls=%async_computation.15 | async-start | bytes 3145728 | tf_op jit(solution)/shard_map/cond/branch_3_fun/all_to_all | solution.py:262
  163.0 19.2 %collective-permute-start.11 = (bf16[17,16,2048]{2,1,0:T(8,128)(2,1)}, bf16[17,16,2048]{2,1,0:T(8,128)(2,1)S(1)}, u32[]{:S(2)}, u32[]{:S(2)}) collective-permute-start(bf16[17,16,2048]{2,1,0:T(8,128)(2,1)} %get-tuple-element.185), channel_id=1, source_target_pairs={{0,8},{1,9},{2,10},{3,11},{4,12},{5,13},{6,14},{7,15},{8,0},{9,1},... | collective-permute-start | bytes 3342344 | tf_op jit(solution)/shard_map/cond/branch_3_fun/ppermute | solution.py:274
  182.3 0.1 reduce.7
  182.4 0.1 reshape.270
  182.5 0.0 copy-done.26
  182.5 0.0 copy-done.38
  182.5 0.1 select_reduce_fusion.3
  182.6 1.0 all-to-all-done.15.in_ref
  183.6 0.7 broadcast_in_dim.183
  184.3 20.0 %all-to-all-start.16 = ((f32[16,1,384]{2,1,0:T(1,128)}), f32[16,1,384]{2,1,0:T(1,128)S(1)}, u32[]{:S(2)}, u32[]{:S(2)}) async-start(f32[16,1,384]{2,1,0:T(1,128)} %broadcast_in_dim.183), calls=%async_computation.16 | async-start | bytes 49152 | tf_op jit(solution)/shard_map/cond/branch_3_fun/all_to_all | solution.py:280
  204.3 27.5 %collective-permute-done.11 = bf16[17,16,2048]{2,1,0:T(8,128)(2,1)S(1)} collective-permute-done((bf16[17,16,2048]{2,1,0:T(8,128)(2,1)}, bf16[17,16,2048]{2,1,0:T(8,128)(2,1)S(1)}, u32[]{:S(2)}, u32[]{:S(2)}) %collective-permute-start.11) | collective-permute-done | bytes 1114144 | tf_op jit(solution)/shard_map/cond/branch_3_fun/ppermute | solution.py:274
  231.8 1.9 gather_fusion.11
  233.7 0.0 all-to-all-done.16
  233.7 0.8 copy.110
  234.5 3.6 %all-to-all-start.17 = ((bf16[4,6,16,2048]{3,2,1,0:T(8,128)(2,1)}), bf16[4,6,16,2048]{3,2,1,0:T(8,128)(2,1)S(1)}, u32[]{:S(2)}, u32[]{:S(2)}) async-start(bf16[4,6,16,2048]{3,2,1,0:T(8,128)(2,1)} %bitcast.43), calls=%async_computation.17 | async-start | bytes 3145728 | tf_op jit(solution)/shard_map/cond/branch_3_fun/all_to_all | solution.py:262
  238.1 0.1 collective-permute-start.10
  238.2 28.9 %collective-permute-done.10 = bf16[17,16,2048]{2,1,0:T(8,128)(2,1)S(1)} collective-permute-done((bf16[17,16,2048]{2,1,0:T(8,128)(2,1)}, bf16[17,16,2048]{2,1,0:T(8,128)(2,1)S(1)}, u32[]{:S(2)}, u32[]{:S(2)}) %collective-permute-start.10) | collective-permute-done | bytes 1114144 | tf_op jit(solution)/shard_map/cond/branch_3_fun/ppermute | solution.py:274
  267.1 1.8 gather_fusion.10
  268.9 0.0 all-to-all-done.17.in_ref
  268.9 3.6 %all-to-all-start.18 = ((bf16[4,6,16,2048]{3,2,1,0:T(8,128)(2,1)}), bf16[4,6,16,2048]{3,2,1,0:T(8,128)(2,1)S(1)}, u32[]{:S(2)}, u32[]{:S(2)}) async-start(bf16[4,6,16,2048]{3,2,1,0:T(8,128)(2,1)} %bitcast.138), calls=%async_computation.18 | async-start | bytes 3145728 | tf_op jit(solution)/shard_map/cond/branch_3_fun/all_to_all | solution.py:262
  272.5 0.1 collective-permute-start.9
  272.6 27.2 %collective-permute-done.9 = bf16[17,16,2048]{2,1,0:T(8,128)(2,1)} collective-permute-done((bf16[17,16,2048]{2,1,0:T(8,128)(2,1)}, bf16[17,16,2048]{2,1,0:T(8,128)(2,1)}, u32[]{:S(2)}, u32[]{:S(2)}) %collective-permute-start.9) | collective-permute-done | bytes 1114144 | tf_op jit(solution)/shard_map/cond/branch_3_fun/ppermute | solution.py:274
  299.8 3.1 gather_fusion.9
  302.9 0.0 all-to-all-done.18.in_ref
  302.9 4.4 %all-to-all-start.19 = ((bf16[4,6,16,2048]{3,2,1,0:T(8,128)(2,1)}), bf16[4,6,16,2048]{3,2,1,0:T(8,128)(2,1)}, u32[]{:S(2)}, u32[]{:S(2)}) async-start(bf16[4,6,16,2048]{3,2,1,0:T(8,128)(2,1)} %bitcast.131), calls=%async_computation.19 | async-start | bytes 3145728 | tf_op jit(solution)/shard_map/cond/branch_3_fun/all_to_all | solution.py:262
  307.3 0.7 reduce_sum.63
  308.1 1.4 copy-done.7
  309.5 2.5 place.40.rest_0_
  312.0 1.1 copy.111
  313.1 0.8 reshape.276
  313.9 2.5 place.41.rest_0_
  316.5 2.5 place.42.rest_0_
  319.0 8.4 %all-to-all-done.19.in_ref = bf16[4,6,16,2048]{3,2,1,0:T(8,128)(2,1)} async-done(((bf16[4,6,16,2048]{3,2,1,0:T(8,128)(2,1)}), bf16[4,6,16,2048]{3,2,1,0:T(8,128)(2,1)}, u32[]{:S(2)}, u32[]{:S(2)}) %all-to-all-start.19) | async-done | bytes 1572896 | tf_op jit(solution)/shard_map/cond/branch_3_fun/all_to_all | solution.py:262
  327.4 4.1 %place.43 = bf16[6,256,2048]{2,1,0:T(8,128)(2,1)} custom-call(s32[1]{0:T(128)} %bitcast.39.filled_ref, s32[1]{0:T(128)} %bitcast.40.quarter_ref, bf16[4,6,16,2048]{3,2,1,0:T(8,128)(2,1)} %all-to-all-done.19.in_ref, bf16[6,256,2048]{2,1,0:T(8,128)(2,1)} %place.42.rest_0_), custom_call_target="tpu_custom_call", output_to_operand_aliasing={{}: (3, {})} | custom-call | tf_op jit(solution)/shard_map/cond/branch_3_fun/place/pallas_call | solution.py:201
  (20 shorter events, 0.1 us)
Async XLA Ops:
  18.5 7.6 %copy-start.47 = (s32[48,1]{0,1:T(1,128)S(1)}, s32[48,1]{0,1:T(1,128)}, u32[]{:S(2)}) copy-start(s32[48,1]{0,1:T(1,128)} %param.22) | copy-start | bytes 580
  18.5 121.8 %copy-start.45 = (s32[8,2]{0,1:T(2,128)S(1)}, s32[8,2]{0,1:T(2,128)}, u32[]{:S(2)}) copy-start(s32[8,2]{0,1:T(2,128)} %param.19) | copy-start | bytes 196
  18.5 121.8 %copy-start.46 = (s32[16]{0:T(128)S(1)}, s32[16]{0:T(128)}, u32[]{:S(2)}) copy-start(s32[16]{0:T(128)} %param.20) | copy-start | bytes 196
  18.5 121.7 %all-to-all-start.35 = ((bf16[16,2,48,2048]{3,2,1,0:T(8,128)(2,1)}), bf16[16,2,48,2048]{3,2,1,0:T(8,128)(2,1)}, u32[]{:S(2)}, u32[]{:S(2)}) async-start(bf16[16,2,48,2048]{3,2,1,0:T(8,128)(2,1)} %prepare.1), calls=%async_computation.35 | async-start | bytes 12582912 | tf_op jit(solution)/shard_map/all_to_all | solution.py:256
  27.6 3.7 %collective-permute-start.21 = (s32[]{:T(128)}, s32[]{:T(128)}, u32[]{:S(2)}, u32[]{:S(2)}) collective-permute-start(s32[]{:T(128)} %add.295), channel_id=1, source_target_pairs={{0,16},{16,0},{1,17},{17,1},{2,18},{18,2},{3,19},{19,3},{4,20},{20... | collective-permute-start | bytes 20 | tf_op jit(solution)/shard_map/ppermute | solution.py:246
  140.5 11.7 %copy-start.25 = (s32[48]{0:T(128)}, s32[48]{0:T(128)S(1)}, u32[]{:S(2)}) copy-start(s32[48]{0:T(128)S(1)} %get-tuple-element.371) | copy-start | bytes 580 | tf_op jit(solution)/shard_map/cond
  140.5 11.7 %copy-start.37 = (s32[48]{0:T(128)}, s32[48]{0:T(128)S(1)}, u32[]{:S(2)}) copy-start(s32[48]{0:T(128)S(1)} %get-tuple-element.406) | copy-start | bytes 580 | tf_op jit(solution)/shard_map/cond
  152.2 30.1 %copy-start.20 = (f32[8,48,1]{2,1,0:T(8,128)S(1)}, f32[8,48,1]{2,1,0:T(8,128)}, u32[]{:S(2)}) copy-start(f32[8,48,1]{2,1,0:T(8,128)} %get-tuple-element.186) | copy-start | bytes 4612 | tf_op jit(solution)/shard_map/cond
  152.2 30.3 %copy-start.26 = (s32[48]{0:T(128)S(1)}, s32[48]{0:T(128)}, u32[]{:S(2)}) copy-start(s32[48]{0:T(128)} %copy-done.25) | copy-start | bytes 580 | tf_op jit(solution)/shard_map/cond
  152.2 30.3 %copy-start.38 = (s32[48]{0:T(128)S(1)}, s32[48]{0:T(128)}, u32[]{:S(2)}) copy-start(s32[48]{0:T(128)} %copy-done.37) | copy-start | bytes 580 | tf_op jit(solution)/shard_map/cond
  152.2 31.4 %all-to-all-start.15 = ((bf16[4,6,16,2048]{3,2,1,0:T(8,128)(2,1)}), bf16[4,6,16,2048]{3,2,1,0:T(8,128)(2,1)S(1)}, u32[]{:S(2)}, u32[]{:S(2)}) async-start(bf16[4,6,16,2048]{3,2,1,0:T(8,128)(2,1)} %bitcast.150), calls=%async_computation.15 | async-start | bytes 3145728 | tf_op jit(solution)/shard_map/cond/branch_3_fun/all_to_all | solution.py:262
  163.0 68.8 %collective-permute-start.11 = (bf16[17,16,2048]{2,1,0:T(8,128)(2,1)}, bf16[17,16,2048]{2,1,0:T(8,128)(2,1)S(1)}, u32[]{:S(2)}, u32[]{:S(2)}) collective-permute-start(bf16[17,16,2048]{2,1,0:T(8,128)(2,1)} %get-tuple-element.185), channel_id=1, source_target_pairs={{0,8},{1,9},{2,10},{3,11},{4,12},{5,13},{6,14},{7,15},{8,0},{9,1},... | collective-permute-start | bytes 3342344 | tf_op jit(solution)/shard_map/cond/branch_3_fun/ppermute | solution.py:274
  183.6 50.2 %copy-start.6 = (bf16[4,6,16,2048]{3,2,1,0:T(8,128)(2,1)}, bf16[4,6,16,2048]{3,2,1,0:T(8,128)(2,1)S(1)}, u32[]{:S(2)}) copy-start(bf16[4,6,16,2048]{3,2,1,0:T(8,128)(2,1)S(1)} %all-to-all-done.15.in_ref) | copy-start | bytes 4718596 | tf_op jit(solution)/shard_map/cond
  184.3 49.4 %all-to-all-start.16 = ((f32[16,1,384]{2,1,0:T(1,128)}), f32[16,1,384]{2,1,0:T(1,128)S(1)}, u32[]{:S(2)}, u32[]{:S(2)}) async-start(f32[16,1,384]{2,1,0:T(1,128)} %broadcast_in_dim.183), calls=%async_computation.16 | async-start | bytes 49152 | tf_op jit(solution)/shard_map/cond/branch_3_fun/all_to_all | solution.py:280
  234.5 34.4 %all-to-all-start.17 = ((bf16[4,6,16,2048]{3,2,1,0:T(8,128)(2,1)}), bf16[4,6,16,2048]{3,2,1,0:T(8,128)(2,1)S(1)}, u32[]{:S(2)}, u32[]{:S(2)}) async-start(bf16[4,6,16,2048]{3,2,1,0:T(8,128)(2,1)} %bitcast.43), calls=%async_computation.17 | async-start | bytes 3145728 | tf_op jit(solution)/shard_map/cond/branch_3_fun/all_to_all | solution.py:262
  238.1 29.0 %collective-permute-start.10 = (bf16[17,16,2048]{2,1,0:T(8,128)(2,1)}, bf16[17,16,2048]{2,1,0:T(8,128)(2,1)S(1)}, u32[]{:S(2)}, u32[]{:S(2)}) collective-permute-start(bf16[17,16,2048]{2,1,0:T(8,128)(2,1)} %get-tuple-element.184), channel_id=1, source_target_pairs={{0,4},{1,5},{2,6},{3,7},{4,8},{5,9},{6,10},{7,11},{8,12},{9,13},{1... | collective-permute-start | bytes 3342344 | tf_op jit(solution)/shard_map/cond/branch_3_fun/ppermute | solution.py:274
  268.9 34.0 %all-to-all-start.18 = ((bf16[4,6,16,2048]{3,2,1,0:T(8,128)(2,1)}), bf16[4,6,16,2048]{3,2,1,0:T(8,128)(2,1)S(1)}, u32[]{:S(2)}, u32[]{:S(2)}) async-start(bf16[4,6,16,2048]{3,2,1,0:T(8,128)(2,1)} %bitcast.138), calls=%async_computation.18 | async-start | bytes 3145728 | tf_op jit(solution)/shard_map/cond/branch_3_fun/all_to_all | solution.py:262
  272.5 27.3 %collective-permute-start.9 = (bf16[17,16,2048]{2,1,0:T(8,128)(2,1)}, bf16[17,16,2048]{2,1,0:T(8,128)(2,1)}, u32[]{:S(2)}, u32[]{:S(2)}) collective-permute-start(bf16[17,16,2048]{2,1,0:T(8,128)(2,1)} %get-tuple-element.182), channel_id=1, source_target_pairs={{0,12},{1,13},{2,14},{3,15},{4,0},{5,1},{6,2},{7,3},{8,4},{9,5},{1... | collective-permute-start | bytes 3342344 | tf_op jit(solution)/shard_map/cond/branch_3_fun/ppermute | solution.py:274
  302.9 24.5 %all-to-all-start.19 = ((bf16[4,6,16,2048]{3,2,1,0:T(8,128)(2,1)}), bf16[4,6,16,2048]{3,2,1,0:T(8,128)(2,1)}, u32[]{:S(2)}, u32[]{:S(2)}) async-start(bf16[4,6,16,2048]{3,2,1,0:T(8,128)(2,1)} %bitcast.131), calls=%async_computation.19 | async-start | bytes 3145728 | tf_op jit(solution)/shard_map/cond/branch_3_fun/all_to_all | solution.py:262
  308.1 1.4 copy-start.7

commit v5 on v4

--- a/solution.py
+++ b/solution.py
@@ -18,62 +18,80 @@
 LIST_PARTS = (14, 15, 16, 17, 18, 20, 24)
 
 
-def own_order(pairs, unit_order, width):
-    device_id = lax.axis_index("expert")
-    is_right = pairs[:, 1] == device_id
-    picked = jnp.sum(jnp.where(is_right[:, None], unit_order, 0), axis=0)
-    identity = jnp.arange(width, dtype=jnp.int32)
-    return jnp.where(jnp.any(is_right), picked, identity)
-
-
-def prepare_kernel(source_ref, gate_ref, up_ref, gate_scale_ref, up_scale_ref, out_ref, select_ref):
+def prepare_kernel(
+    pairs_ref, me_ref, order_ref, gate_ref, up_ref, gate_scale_ref, up_scale_ref, out_ref, select_ref, scale_ref
+):
     units = select_ref.shape[1]
-    rows = gate_ref.shape[0]
-
-    @pl.when(pl.program_id(0) == 0)
+    tile = gate_ref.shape[0]
+    devices, _, per_device, _ = out_ref.shape
+    step = pl.program_id(0)
+
+    @pl.when(step == 0)
     def _():
-        columns = lax.broadcasted_iota(jnp.int32, select_ref.shape, 1)
-        select_ref[...] = (source_ref[...] == columns).astype(jnp.float32).astype(jnp.bfloat16)
-
-    for kind, (codes_ref, scale_ref) in enumerate(
-        ((gate_ref, gate_scale_ref), (up_ref, up_scale_ref))
-    ):
+        order = lax.broadcasted_iota(jnp.int32, (1, units), 1)
+        for pair in range(order_ref.shape[0]):
+            order = jnp.where(
+                pairs_ref[2 * pair + 1] == me_ref[0], order_ref[pair : pair + 1, :], order
+            )
+        share = U // devices
+        row = lax.broadcasted_iota(jnp.int32, (units, 1), 0)
+        device = lax.div(row, per_device)
+        within = row - device * per_device
+        piece = lax.div(within, share)
+        unit = piece * U + device * share + within - piece * share
+        columns = lax.broadcasted_iota(jnp.int32, (units, units), 1)
+        source = jnp.sum(
+            jnp.where(unit == columns, order.astype(jnp.float32), 0.0), axis=1, keepdims=True
+        ).astype(jnp.int32)
+        select_ref[...] = (source == columns).astype(jnp.float32).astype(jnp.bfloat16)
+        for kind, scales in enumerate((gate_scale_ref, up_scale_ref)):
+            value = scales[...].astype(jnp.float32)
+            block = lax.div(lax.broadcasted_iota(jnp.int32, (value.shape[0], units), 1), BLK)
+            spread = jnp.zeros((value.shape[0], units), jnp.float32)
+            for index in range(value.shape[1]):
+                spread = jnp.where(block == index, value[:, index : index + 1], spread)
+            scale_ref[kind] = spread
+
+    for kind, codes_ref in enumerate((gate_ref, up_ref)):
         parts = []
-        for block in range(rows // BLK):
-            scale = scale_ref[0, block : block + 1, :]
-            codes = codes_ref[block * BLK : (block + 1) * BLK, :].astype(jnp.float32)
-            parts.append((codes * scale).astype(jnp.bfloat16))
+        for block in range(tile // BLK):
+            scale = scale_ref[kind, pl.ds(step * (tile // BLK) + block, 1), :].astype(jnp.bfloat16)
+            parts.append(codes_ref[block * BLK : (block + 1) * BLK, :] * scale)
         values = jnp.concatenate(parts, axis=0)
         chosen = lax.dot_general(
             select_ref[...], values, (((1,), (1,)), ((), ())), preferred_element_type=jnp.float32
         ).astype(jnp.bfloat16)
-        out_ref[:, kind] = chosen.reshape(out_ref.shape[0], out_ref.shape[2], rows)
-
-
-def prepare(source, gate_codes, up_codes, gate_scale, up_scale, devices):
+        out_ref[:, kind] = chosen.reshape(devices, per_device, tile)
+
+
+def prepare(pairs, me, unit_order, gate_codes, up_codes, gate_scale, up_scale, devices):
     depth, units = gate_codes.shape
     per_device = units // devices
-    tile = 256
-    blocks = tile // BLK
-    spread = lambda scale: jnp.repeat(scale.astype(jnp.float32), BLK, axis=1).reshape(
-        depth // tile, blocks, units
+    tile = 512
+    whole = lambda array: pl.BlockSpec(array.shape, lambda d, *_: (0, 0))
+    grid_spec = pltpu.PrefetchScalarGridSpec(
+        num_scalar_prefetch=2,
+        grid=(depth // tile,),
+        in_specs=[
+            whole(unit_order),
+            pl.BlockSpec((tile, units), lambda d, *_: (d, 0)),
+            pl.BlockSpec((tile, units), lambda d, *_: (d, 0)),
+            whole(gate_scale),
+            whole(up_scale),
+        ],
+        out_specs=pl.BlockSpec((devices, 2, per_device, tile), lambda d, *_: (0, 0, 0, d)),
+        scratch_shapes=[
+            pltpu.VMEM((units, units), jnp.bfloat16),
+            pltpu.VMEM((2, depth // BLK, units), jnp.float32),
+        ],
     )
     return pl.pallas_call(
         prepare_kernel,
-        grid=(depth // tile,),
-        in_specs=[
-            pl.BlockSpec((units, 1), lambda d: (0, 0)),
-            pl.BlockSpec((tile, units), lambda d: (d, 0)),
-            pl.BlockSpec((tile, units), lambda d: (d, 0)),
-            pl.BlockSpec((1, blocks, units), lambda d: (d, 0, 0)),
-            pl.BlockSpec((1, blocks, units), lambda d: (d, 0, 0)),
-        ],
-        out_specs=pl.BlockSpec((devices, 2, per_device, tile), lambda d: (0, 0, 0, d)),
+        grid_spec=grid_spec,
         out_shape=jax.ShapeDtypeStruct((devices, 2, per_device, depth), jnp.bfloat16),
-        scratch_shapes=[pltpu.VMEM((units, units), jnp.bfloat16)],
         compiler_params=pltpu.CompilerParams(vmem_limit_bytes=VMEM),
         name="prepare",
-    )(source[:, None], gate_codes, up_codes, spread(gate_scale), spread(up_scale))
+    )(pairs.reshape(-1), me[None], unit_order, gate_codes, up_codes, gate_scale, up_scale)
 
 
 def merge_kernel(
@@ -84,32 +102,46 @@
     pair_count = pl.num_programs(0)
     per_device, depth = left_ref.shape[2], left_ref.shape[3]
     pieces, piece_rows = ready.shape[1], ready.shape[2]
-    left_gate = left_ref[0, 0].astype(jnp.float32)
-    left_up = left_ref[0, 1].astype(jnp.float32)
-    right_gate = right_ref[0, 0].astype(jnp.float32)
-    right_up = right_ref[0, 1].astype(jnp.float32)
-    total_of = lambda value: jnp.sum(value, axis=1, keepdims=True)
-    intersection = total_of(left_gate * right_gate + left_up * right_up)
-    left_norm = total_of(left_gate * left_gate + left_up * left_up)
-    right_norm = total_of(right_gate * right_gate + right_up * right_up)
-    similarity = (
-        intersection
-        * math.sqrt(2.0 * depth)
-        / jnp.sqrt((left_norm + EPSILON) * (right_norm + EPSILON))
-    )
-    similarity_ref[0] = similarity
     left_freq = counts_ref[pairs_ref[2 * pair]].astype(jnp.float32)
     right_freq = counts_ref[pairs_ref[2 * pair + 1]].astype(jnp.float32)
-    share = right_freq * jax.nn.sigmoid(similarity)
-    total = left_freq + share
-    left_weight = left_freq / total
-    right_weight = share / total
-    for kind, (left, right) in enumerate(((left_gate, right_gate), (left_up, right_up))):
-        merged = left_weight * left + right_weight * right
+    group = 16 if per_device % 16 == 0 else per_device
+
+    def values_of(first, block):
+        rows, columns = slice(first, first + group), slice(block * LANES, (block + 1) * LANES)
+        return [
+            ref[0, kind, rows, columns].astype(jnp.float32)
+            for ref in (left_ref, right_ref)
+            for kind in (0, 1)
+        ]
+
+    for first in range(0, per_device, group):
+        intersection = left_norm = right_norm = jnp.zeros((group, LANES), jnp.float32)
         for block in range(depth // LANES):
-            woven[block, pl.ds(kind, per_device, stride=2), :] = merged[
-                :, block * LANES : (block + 1) * LANES
-            ]
+            left_gate, left_up, right_gate, right_up = values_of(first, block)
+            intersection += left_gate * right_gate + left_up * right_up
+            left_norm += left_gate * left_gate + left_up * left_up
+            right_norm += right_gate * right_gate + right_up * right_up
+        intersection, left_norm, right_norm = (
+            jnp.sum(value, axis=1, keepdims=True) for value in (intersection, left_norm, right_norm)
+        )
+        similarity = (
+            intersection
+            * math.sqrt(2.0 * depth)
+            / jnp.sqrt((left_norm + EPSILON) * (right_norm + EPSILON))
+        )
+        similarity_ref[0, first : first + group] = similarity
+        share = right_freq * jax.nn.sigmoid(similarity)
+        total = left_freq + share
+        left_weight = jnp.broadcast_to(left_freq / total, (group, LANES))
+        right_weight = jnp.broadcast_to(share / total, (group, LANES))
+        for block in range(depth // LANES):
+            left_gate, left_up, right_gate, right_up = values_of(first, block)
+            woven[block, pl.ds(2 * first, group, stride=2), :] = (
+                left_weight * left_gate + right_weight * right_gate
+            )
+            woven[block, pl.ds(2 * first + 1, group, stride=2), :] = (
+                left_weight * left_up + right_weight * right_up
+            )
     slot = lax.rem(pair, 2)
 
     def each_copy(which_pair, which_slot, act):
@@ -248,10 +280,8 @@
     lengths = sorted({min(size * CAP, -(-least * part // 12)) for part in LIST_PARTS})
     level = sum((longest > length).astype(jnp.int32) for length in lengths[:-1])
 
-    order = own_order(pairs, unit_order, units)
-    source = order.reshape(pieces, devices, share_units).transpose(1, 0, 2).reshape(units)
     outgoing = prepare(
-        source, gate_codes[0], up_codes[0], gate_scale[0], up_scale[0], devices
+        pairs, me, unit_order, gate_codes[0], up_codes[0], gate_scale[0], up_scale[0], devices
     )
     rows = lax.all_to_all(outgoing, "expert", split_axis=0, concat_axis=0, tiled=True)
 

time: 327 us -> 326 us (level); the launches traced: 332 us -> 322 us
  waiting for transfers between devices: 202 us -> 197 us
  other arithmetic: 6.76 us -> 2.5 us
    ppermute x3, waiting for transfers between devices: 83.6 us -> 77.9 us  [deal(): chunk = lax.ppermute(lists[shift - 1], 'expert', ring)]
  transfers between devices with their start and end apart: 10 -> 10, of which waited for: 7 -> 7; matrix products, arithmetic and copies ran while one was open for 3% -> 4% of each run, Pallas kernels for 2% -> 2%
where the time goes in v5:
time: 326 us; the launch traced here: 322 us
  waiting for transfers between devices  197 us (60%)
  starting transfers between devices  72.1 us (22%)
  Pallas kernels  32 us (10%)
  local copies, waits for them, and re-layouts  16.5 us (5%)
    all_to_all x1, waiting for transfers between devices, body(): lax.all_to_all(outgoing, 'expert', split_axis=0, concat_axis=0, tiled=True)  108 us
    ppermute x3, waiting for transfers between devices, deal(): chunk = lax.ppermute(lists[shift - 1], 'expert', ring)  77.9 us
    all_to_all x4, starting transfers between devices, within_quarter(): lax.all_to_all(value, 'expert', split_axis=0, concat_axis=0, tiled=True,...  22.3 us
    all_to_all x1, starting transfers between devices, deal(): lax.all_to_all(jnp.broadcast_to(part, (devices, part.shape[1])), 'expert'...  20 us
    ppermute x3, starting transfers between devices, deal(): chunk = lax.ppermute(lists[shift - 1], 'expert', ring)  19.3 us
    pallas_call x4, Pallas kernels, place(): pl.pallas_call(place_kernel, grid_spec=grid_spec, out_shape=jax.ShapeDtyp...  11.4 us
    pallas_call x1, Pallas kernels, merge(): pl.pallas_call(merge_kernel, grid_spec=grid_spec, out_shape=[jax.ShapeDty...  10.3 us
    pallas_call x1, Pallas kernels, prepare(): pl.pallas_call(prepare_kernel, grid_spec=grid_spec, out_shape=jax.ShapeDt...  10.3 us
  transfers between devices with their start and end apart: 10, of which 7 were waited for; matrix products, arithmetic and copies ran while one was open for 4% of the time, Pallas kernels for 2%

profile of v5, /device:TPU:0, one launch (start us, length us, event | category | flops | bytes accessed | tf_op | source)
XLA Modules:
  0.0 321.9 jit_solution(8626778807427309696)
XLA Ops:
  0.6 1.4 copy.118.gate_scale_ref
  2.0 1.4 copy.119.up_scale_ref
  3.3 0.8 copy.117
  4.1 0.6 reshape.295.pairs_ref
  4.7 10.3 %prepare.1 = bf16[16,2,48,2048]{3,2,1,0:T(8,128)(2,1)} custom-call(s32[16]{0:T(128)} %reshape.295.pairs_ref, s32[1]{0:T(128)} %bitcast.93.me_ref, s32[8,768]{1,0:T(8,128)} %order_ref.1, bf16[2048,768]{1,0:T(8,128)(2,1)} %bitcast.135, bf16[2048,768]{1,0:T(8,128)(2,1)} %bitcast.136, bf16[16,6]{1,0:T(8,128)(2,1)} %copy.118.gate_scale_ref, ...), custom_call_target="tpu_custom_call" | custom-call | tf_op jit(solution)/shard_map/prepare/pallas_call | solution.py:88
  15.0 0.0 copy-start.47
  15.0 7.5 %all-to-all-start.35 = ((bf16[16,2,48,2048]{3,2,1,0:T(8,128)(2,1)}), bf16[16,2,48,2048]{3,2,1,0:T(8,128)(2,1)}, u32[]{:S(2)}, u32[]{:S(2)}) async-start(bf16[16,2,48,2048]{3,2,1,0:T(8,128)(2,1)} %prepare.1), calls=%async_computation.35 | async-start | bytes 12582912 | tf_op jit(solution)/shard_map/all_to_all | solution.py:286
  22.5 0.0 copy-done.47
  22.6 0.2 select_reduce_fusion.8
  22.8 0.6 reduce_max.9
  24.1 2.9 collective-permute-start.21
  26.9 0.2 select_reduce_fusion.7
  27.1 0.5 collective-permute-done.21
  28.3 108.4 %all-to-all-done.35 = bf16[16,2,48,2048]{3,2,1,0:T(8,128)(2,1)} async-done(((bf16[16,2,48,2048]{3,2,1,0:T(8,128)(2,1)}), bf16[16,2,48,2048]{3,2,1,0:T(8,128)(2,1)}, u32[]{:S(2)}, u32[]{:S(2)}) %all-to-all-start.35) | async-done | bytes 6291488 | tf_op jit(solution)/shard_map/all_to_all | solution.py:286
  136.7 0.0 copy-done.45
  136.7 0.0 copy-done.46
  136.7 185.2 %conditional.1 = (bf16[6,256,2048]{2,1,0:T(8,128)(2,1)}, f32[8,768]{1,0:T(8,128)}) conditional(s32[]{:T(128)} %clamp.3, (s32[]{:T(128)}, s32[8,2]{0,1:T(2,128)S(1)}, s32[16]{0:T(128)S(1)}, s32[48]{0:T(128)S(1)}, pred[48]{0:T(512)(128)(4,1)S(1)}, /*index=5*/bf16[16,2,48,2048]{3,2,1,0:T(8,128)(2,1)}, ...), branch_computations={%region_5.6_spmd, %region_6.7_spmd, %region_7.8_spmd, %region_8.9_... | conditional | flops 5751 | bytes 60047832 | solution.py:325
  136.8 0.0 copy-start.23
  136.8 0.0 copy-start.35
  136.8 0.1 copy.122
  136.9 0.6 reshape.254.pairs_ref
  137.5 0.5 select_n.177.place_ref
  138.0 10.3 %merge.9 = (f32[8,48,1]{2,1,0:T(8,128)}, bf16[24,16,2048]{2,1,0:T(8,128)(2,1)}, bf16[16,16,2048]{2,1,0:T(8,128)(2,1)}, bf16[16,16,2048]{2,1,0:T(8,128)(2,1)}, bf16[16,16,2048]{2,1,0:T(8,128)(2,1)}) custom-call(s32[16]{0:T(128)} %reshape.254.pairs_ref, s32[16]{0:T(128)S(1)} %get-tuple-element.314.counts_ref, s32[48]{0:T(128)S(1)} %get-tuple-element.158.where_ref, ...), custom_call_target="tpu_custom_call" | custom-call | tf_op jit(solution)/shard_map/cond/branch_2_fun/merge/pallas_call | solution.py:201
  148.3 0.0 copy-done.23
  148.3 0.0 copy-done.35
  148.3 0.0 copy-start.19
  148.4 0.0 copy-start.24
  148.4 0.0 copy-start.36
  148.4 10.8 %all-to-all-start.10 = ((bf16[4,6,16,2048]{3,2,1,0:T(8,128)(2,1)}), bf16[4,6,16,2048]{3,2,1,0:T(8,128)(2,1)S(1)}, u32[]{:S(2)}, u32[]{:S(2)}) async-start(bf16[4,6,16,2048]{3,2,1,0:T(8,128)(2,1)} %bitcast.142), calls=%async_computation.10 | async-start | bytes 3145728 | tf_op jit(solution)/shard_map/cond/branch_2_fun/all_to_all | solution.py:292
  159.1 19.2 %collective-permute-start.8 = (bf16[16,16,2048]{2,1,0:T(8,128)(2,1)}, bf16[16,16,2048]{2,1,0:T(8,128)(2,1)S(1)}, u32[]{:S(2)}, u32[]{:S(2)}) collective-permute-start(bf16[16,16,2048]{2,1,0:T(8,128)(2,1)} %get-tuple-element.164), channel_id=1, source_target_pairs={{0,8},{1,9},{2,10},{3,11},{4,12},{5,13},{6,14},{7,15},{8,0},{9,1},... | collective-permute-start | bytes 3145736 | tf_op jit(solution)/shard_map/cond/branch_2_fun/ppermute | solution.py:304
  178.4 0.0 copy-done.19
  178.4 0.1 reduce.4
  178.5 0.1 reshape.255
  178.6 0.0 copy-done.24
  178.6 0.0 copy-done.36
  178.6 0.1 select_reduce_fusion.2
  178.7 1.0 all-to-all-done.10.in_ref
  179.7 0.7 broadcast_in_dim.163
  180.4 20.0 %all-to-all-start.11 = ((f32[16,1,384]{2,1,0:T(1,128)}), f32[16,1,384]{2,1,0:T(1,128)S(1)}, u32[]{:S(2)}, u32[]{:S(2)}) async-start(f32[16,1,384]{2,1,0:T(1,128)} %broadcast_in_dim.163), calls=%async_computation.11 | async-start | bytes 49152 | tf_op jit(solution)/shard_map/cond/branch_2_fun/all_to_all | solution.py:310
  200.5 24.6 %collective-permute-done.8 = bf16[16,16,2048]{2,1,0:T(8,128)(2,1)S(1)} collective-permute-done((bf16[16,16,2048]{2,1,0:T(8,128)(2,1)}, bf16[16,16,2048]{2,1,0:T(8,128)(2,1)S(1)}, u32[]{:S(2)}, u32[]{:S(2)}) %collective-permute-start.8) | collective-permute-done | bytes 1048608 | tf_op jit(solution)/shard_map/cond/branch_2_fun/ppermute | solution.py:304
  225.1 1.9 gather_fusion.8
  227.0 0.0 copy-done.4
  227.0 0.0 all-to-all-done.11
  227.0 0.8 copy.107
  227.8 3.6 %all-to-all-start.12 = ((bf16[4,6,16,2048]{3,2,1,0:T(8,128)(2,1)}), bf16[4,6,16,2048]{3,2,1,0:T(8,128)(2,1)S(1)}, u32[]{:S(2)}, u32[]{:S(2)}) async-start(bf16[4,6,16,2048]{3,2,1,0:T(8,128)(2,1)} %bitcast.30), calls=%async_computation.12 | async-start | bytes 3145728 | tf_op jit(solution)/shard_map/cond/branch_2_fun/all_to_all | solution.py:292
  231.4 0.1 collective-permute-start.7
  231.4 27.5 %collective-permute-done.7 = bf16[16,16,2048]{2,1,0:T(8,128)(2,1)S(1)} collective-permute-done((bf16[16,16,2048]{2,1,0:T(8,128)(2,1)}, bf16[16,16,2048]{2,1,0:T(8,128)(2,1)S(1)}, u32[]{:S(2)}, u32[]{:S(2)}) %collective-permute-start.7) | collective-permute-done | bytes 1048608 | tf_op jit(solution)/shard_map/cond/branch_2_fun/ppermute | solution.py:304
  258.9 1.8 gather_fusion.7
  260.8 0.0 all-to-all-done.12.in_ref
  260.8 3.6 %all-to-all-start.13 = ((bf16[4,6,16,2048]{3,2,1,0:T(8,128)(2,1)}), bf16[4,6,16,2048]{3,2,1,0:T(8,128)(2,1)S(1)}, u32[]{:S(2)}, u32[]{:S(2)}) async-start(bf16[4,6,16,2048]{3,2,1,0:T(8,128)(2,1)} %bitcast.130), calls=%async_computation.13 | async-start | bytes 3145728 | tf_op jit(solution)/shard_map/cond/branch_2_fun/all_to_all | solution.py:292
  264.4 0.1 collective-permute-start.6
  264.4 25.8 %collective-permute-done.6 = bf16[16,16,2048]{2,1,0:T(8,128)(2,1)} collective-permute-done((bf16[16,16,2048]{2,1,0:T(8,128)(2,1)}, bf16[16,16,2048]{2,1,0:T(8,128)(2,1)}, u32[]{:S(2)}, u32[]{:S(2)}) %collective-permute-start.6) | collective-permute-done | bytes 1048608 | tf_op jit(solution)/shard_map/cond/branch_2_fun/ppermute | solution.py:304
  290.2 3.1 gather_fusion.6
  293.3 0.0 all-to-all-done.13.in_ref
  293.3 4.4 %all-to-all-start.14 = ((bf16[4,6,16,2048]{3,2,1,0:T(8,128)(2,1)}), bf16[4,6,16,2048]{3,2,1,0:T(8,128)(2,1)}, u32[]{:S(2)}, u32[]{:S(2)}) async-start(bf16[4,6,16,2048]{3,2,1,0:T(8,128)(2,1)} %bitcast.123), calls=%async_computation.14 | async-start | bytes 3145728 | tf_op jit(solution)/shard_map/cond/branch_2_fun/all_to_all | solution.py:292
  297.8 0.7 reduce_sum.49
  298.4 1.4 copy-done.5
  299.8 2.4 place.36.rest_0_
  302.3 1.1 copy.108
  303.4 0.8 reshape.261
  304.2 2.4 place.37.rest_0_
  306.7 2.4 place.38.rest_0_
  309.1 8.7 %all-to-all-done.14.in_ref = bf16[4,6,16,2048]{3,2,1,0:T(8,128)(2,1)} async-done(((bf16[4,6,16,2048]{3,2,1,0:T(8,128)(2,1)}), bf16[4,6,16,2048]{3,2,1,0:T(8,128)(2,1)}, u32[]{:S(2)}, u32[]{:S(2)}) %all-to-all-start.14) | async-done | bytes 1572896 | tf_op jit(solution)/shard_map/cond/branch_2_fun/all_to_all | solution.py:292
  317.8 4.1 %place.39 = bf16[6,256,2048]{2,1,0:T(8,128)(2,1)} custom-call(s32[1]{0:T(128)} %bitcast.26.filled_ref, s32[1]{0:T(128)} %bitcast.27.quarter_ref, bf16[4,6,16,2048]{3,2,1,0:T(8,128)(2,1)} %all-to-all-done.14.in_ref, bf16[6,256,2048]{2,1,0:T(8,128)(2,1)} %place.38.rest_0_), custom_call_target="tpu_custom_call", output_to_operand_aliasing={{}: (3, {})} | custom-call | tf_op jit(solution)/shard_map/cond/branch_2_fun/place/pallas_call | solution.py:233
  (10 shorter events, 0.1 us)
Async XLA Ops:
  15.0 7.6 %copy-start.47 = (s32[48,1]{0,1:T(1,128)S(1)}, s32[48,1]{0,1:T(1,128)}, u32[]{:S(2)}) copy-start(s32[48,1]{0,1:T(1,128)} %param.22) | copy-start | bytes 580
  15.0 121.8 %copy-start.45 = (s32[8,2]{0,1:T(2,128)S(1)}, s32[8,2]{0,1:T(2,128)}, u32[]{:S(2)}) copy-start(s32[8,2]{0,1:T(2,128)} %param.19) | copy-start | bytes 196
  15.0 121.8 %copy-start.46 = (s32[16]{0:T(128)S(1)}, s32[16]{0:T(128)}, u32[]{:S(2)}) copy-start(s32[16]{0:T(128)} %param.20) | copy-start | bytes 196
  15.0 121.8 %all-to-all-start.35 = ((bf16[16,2,48,2048]{3,2,1,0:T(8,128)(2,1)}), bf16[16,2,48,2048]{3,2,1,0:T(8,128)(2,1)}, u32[]{:S(2)}, u32[]{:S(2)}) async-start(bf16[16,2,48,2048]{3,2,1,0:T(8,128)(2,1)} %prepare.1), calls=%async_computation.35 | async-start | bytes 12582912 | tf_op jit(solution)/shard_map/all_to_all | solution.py:286
  24.1 3.6 %collective-permute-start.21 = (s32[]{:T(128)}, s32[]{:T(128)}, u32[]{:S(2)}, u32[]{:S(2)}) collective-permute-start(s32[]{:T(128)} %add.293), channel_id=1, source_target_pairs={{0,16},{16,0},{1,17},{17,1},{2,18},{18,2},{3,19},{19,3},{4,20},{20... | collective-permute-start | bytes 20 | tf_op jit(solution)/shard_map/ppermute | solution.py:278
  136.8 11.5 %copy-start.23 = (s32[48]{0:T(128)}, s32[48]{0:T(128)S(1)}, u32[]{:S(2)}) copy-start(s32[48]{0:T(128)S(1)} %get-tuple-element.370) | copy-start | bytes 580 | tf_op jit(solution)/shard_map/cond
  136.8 11.5 %copy-start.35 = (s32[48]{0:T(128)}, s32[48]{0:T(128)S(1)}, u32[]{:S(2)}) copy-start(s32[48]{0:T(128)S(1)} %get-tuple-element.405) | copy-start | bytes 580 | tf_op jit(solution)/shard_map/cond
  148.3 30.0 %copy-start.19 = (f32[8,48,1]{2,1,0:T(8,128)S(1)}, f32[8,48,1]{2,1,0:T(8,128)}, u32[]{:S(2)}) copy-start(f32[8,48,1]{2,1,0:T(8,128)} %get-tuple-element.165) | copy-start | bytes 4612 | tf_op jit(solution)/shard_map/cond
  148.4 30.2 %copy-start.24 = (s32[48]{0:T(128)S(1)}, s32[48]{0:T(128)}, u32[]{:S(2)}) copy-start(s32[48]{0:T(128)} %copy-done.23) | copy-start | bytes 580 | tf_op jit(solution)/shard_map/cond
  148.4 30.2 %copy-start.36 = (s32[48]{0:T(128)S(1)}, s32[48]{0:T(128)}, u32[]{:S(2)}) copy-start(s32[48]{0:T(128)} %copy-done.35) | copy-start | bytes 580 | tf_op jit(solution)/shard_map/cond
  148.4 31.4 %all-to-all-start.10 = ((bf16[4,6,16,2048]{3,2,1,0:T(8,128)(2,1)}), bf16[4,6,16,2048]{3,2,1,0:T(8,128)(2,1)S(1)}, u32[]{:S(2)}, u32[]{:S(2)}) async-start(bf16[4,6,16,2048]{3,2,1,0:T(8,128)(2,1)} %bitcast.142), calls=%async_computation.10 | async-start | bytes 3145728 | tf_op jit(solution)/shard_map/cond/branch_2_fun/all_to_all | solution.py:292
  159.1 66.0 %collective-permute-start.8 = (bf16[16,16,2048]{2,1,0:T(8,128)(2,1)}, bf16[16,16,2048]{2,1,0:T(8,128)(2,1)S(1)}, u32[]{:S(2)}, u32[]{:S(2)}) collective-permute-start(bf16[16,16,2048]{2,1,0:T(8,128)(2,1)} %get-tuple-element.164), channel_id=1, source_target_pairs={{0,8},{1,9},{2,10},{3,11},{4,12},{5,13},{6,14},{7,15},{8,0},{9,1},... | collective-permute-start | bytes 3145736 | tf_op jit(solution)/shard_map/cond/branch_2_fun/ppermute | solution.py:304
  179.7 47.3 %copy-start.4 = (bf16[4,6,16,2048]{3,2,1,0:T(8,128)(2,1)}, bf16[4,6,16,2048]{3,2,1,0:T(8,128)(2,1)S(1)}, u32[]{:S(2)}) copy-start(bf16[4,6,16,2048]{3,2,1,0:T(8,128)(2,1)S(1)} %all-to-all-done.10.in_ref) | copy-start | bytes 4718596 | tf_op jit(solution)/shard_map/cond
  180.4 46.6 %all-to-all-start.11 = ((f32[16,1,384]{2,1,0:T(1,128)}), f32[16,1,384]{2,1,0:T(1,128)S(1)}, u32[]{:S(2)}, u32[]{:S(2)}) async-start(f32[16,1,384]{2,1,0:T(1,128)} %broadcast_in_dim.163), calls=%async_computation.11 | async-start | bytes 49152 | tf_op jit(solution)/shard_map/cond/branch_2_fun/all_to_all | solution.py:310
  227.8 33.0 %all-to-all-start.12 = ((bf16[4,6,16,2048]{3,2,1,0:T(8,128)(2,1)}), bf16[4,6,16,2048]{3,2,1,0:T(8,128)(2,1)S(1)}, u32[]{:S(2)}, u32[]{:S(2)}) async-start(bf16[4,6,16,2048]{3,2,1,0:T(8,128)(2,1)} %bitcast.30), calls=%async_computation.12 | async-start | bytes 3145728 | tf_op jit(solution)/shard_map/cond/branch_2_fun/all_to_all | solution.py:292
  231.4 27.6 %collective-permute-start.7 = (bf16[16,16,2048]{2,1,0:T(8,128)(2,1)}, bf16[16,16,2048]{2,1,0:T(8,128)(2,1)S(1)}, u32[]{:S(2)}, u32[]{:S(2)}) collective-permute-start(bf16[16,16,2048]{2,1,0:T(8,128)(2,1)} %get-tuple-element.163), channel_id=1, source_target_pairs={{0,4},{1,5},{2,6},{3,7},{4,8},{5,9},{6,10},{7,11},{8,12},{9,13},{1... | collective-permute-start | bytes 3145736 | tf_op jit(solution)/shard_map/cond/branch_2_fun/ppermute | solution.py:304
  260.8 32.5 %all-to-all-start.13 = ((bf16[4,6,16,2048]{3,2,1,0:T(8,128)(2,1)}), bf16[4,6,16,2048]{3,2,1,0:T(8,128)(2,1)S(1)}, u32[]{:S(2)}, u32[]{:S(2)}) async-start(bf16[4,6,16,2048]{3,2,1,0:T(8,128)(2,1)} %bitcast.130), calls=%async_computation.13 | async-start | bytes 3145728 | tf_op jit(solution)/shard_map/cond/branch_2_fun/all_to_all | solution.py:292
  264.4 25.9 %collective-permute-start.6 = (bf16[16,16,2048]{2,1,0:T(8,128)(2,1)}, bf16[16,16,2048]{2,1,0:T(8,128)(2,1)}, u32[]{:S(2)}, u32[]{:S(2)}) collective-permute-start(bf16[16,16,2048]{2,1,0:T(8,128)(2,1)} %get-tuple-element.161), channel_id=1, source_target_pairs={{0,12},{1,13},{2,14},{3,15},{4,0},{5,1},{6,2},{7,3},{8,4},{9,5},{1... | collective-permute-start | bytes 3145736 | tf_op jit(solution)/shard_map/cond/branch_2_fun/ppermute | solution.py:304
  293.3 24.5 %all-to-all-start.14 = ((bf16[4,6,16,2048]{3,2,1,0:T(8,128)(2,1)}), bf16[4,6,16,2048]{3,2,1,0:T(8,128)(2,1)}, u32[]{:S(2)}, u32[]{:S(2)}) async-start(bf16[4,6,16,2048]{3,2,1,0:T(8,128)(2,1)} %bitcast.123), calls=%async_computation.14 | async-start | bytes 3145728 | tf_op jit(solution)/shard_map/cond/branch_2_fun/all_to_all | solution.py:292
  298.4 1.4 copy-start.5

commit v6 on v5

--- a/solution.py
+++ b/solution.py
@@ -34,16 +34,21 @@
                 pairs_ref[2 * pair + 1] == me_ref[0], order_ref[pair : pair + 1, :], order
             )
         share = U // devices
-        row = lax.broadcasted_iota(jnp.int32, (units, 1), 0)
-        device = lax.div(row, per_device)
-        within = row - device * per_device
-        piece = lax.div(within, share)
-        unit = piece * U + device * share + within - piece * share
-        columns = lax.broadcasted_iota(jnp.int32, (units, units), 1)
-        source = jnp.sum(
-            jnp.where(unit == columns, order.astype(jnp.float32), 0.0), axis=1, keepdims=True
-        ).astype(jnp.int32)
-        select_ref[...] = (source == columns).astype(jnp.float32).astype(jnp.bfloat16)
+        columns = lax.broadcasted_iota(jnp.int32, (1, units), 1)
+        matched = order.astype(jnp.float32)
+        group = 16
+        for first in range(0, units, group):
+            row = first + lax.broadcasted_iota(jnp.int32, (group, 1), 0)
+            device = lax.div(row, per_device)
+            within = row - device * per_device
+            piece = lax.div(within, share)
+            unit = piece * U + device * share + within - piece * share
+            source = jnp.sum(
+                jnp.where(unit == columns, matched, 0.0), axis=1, keepdims=True
+            ).astype(jnp.int32)
+            select_ref[first : first + group] = (
+                (source == columns).astype(jnp.float32).astype(jnp.bfloat16)
+            )
         for kind, scales in enumerate((gate_scale_ref, up_scale_ref)):
             value = scales[...].astype(jnp.float32)
             block = lax.div(lax.broadcasted_iota(jnp.int32, (value.shape[0], units), 1), BLK)
@@ -95,13 +100,34 @@
 
 
 def merge_kernel(
-    pairs_ref, counts_ref, where_ref, place_ref, left_ref, right_ref, similarity_ref, *rest
+    pairs_ref, counts_ref, where_ref, place_ref, rows_ref, similarity_ref, *rest
 ):
-    outs, (woven, ready, sems) = rest[:-3], rest[-3:]
+    outs, (held, woven, ready, arrive, sems) = rest[:-5], rest[-5:]
     pair = pl.program_id(0)
     pair_count = pl.num_programs(0)
-    per_device, depth = left_ref.shape[2], left_ref.shape[3]
+    per_device, depth = held.shape[3], held.shape[4]
     pieces, piece_rows = ready.shape[1], ready.shape[2]
+
+    def fetches(which_pair):
+        return [
+            pltpu.make_async_copy(
+                rows_ref.at[pairs_ref[2 * which_pair + who], kind],
+                held.at[which_pair, who, kind],
+                arrive.at[which_pair, who, kind],
+            )
+            for who in (0, 1)
+            for kind in (0, 1)
+        ]
+
+    @pl.when(pair == 0)
+    def _():
+        @pl.loop(0, held.shape[0])
+        def _(which_pair):
+            for copy in fetches(which_pair):
+                copy.start()
+
+    for copy in fetches(pair):
+        copy.wait()
     left_freq = counts_ref[pairs_ref[2 * pair]].astype(jnp.float32)
     right_freq = counts_ref[pairs_ref[2 * pair + 1]].astype(jnp.float32)
     group = 16 if per_device % 16 == 0 else per_device
@@ -109,8 +135,8 @@
     def values_of(first, block):
         rows, columns = slice(first, first + group), slice(block * LANES, (block + 1) * LANES)
         return [
-            ref[0, kind, rows, columns].astype(jnp.float32)
-            for ref in (left_ref, right_ref)
+            held[pair, who, kind, rows, columns].astype(jnp.float32)
+            for who in (0, 1)
             for kind in (0, 1)
         ]
 
@@ -184,17 +210,14 @@
     grid_spec = pltpu.PrefetchScalarGridSpec(
         num_scalar_prefetch=4,
         grid=(pair_count,),
-        in_specs=[
-            pl.BlockSpec((1, 2, per_device, depth), lambda p, pairs, *_: (pairs[2 * p], 0, 0, 0)),
-            pl.BlockSpec(
-                (1, 2, per_device, depth), lambda p, pairs, *_: (pairs[2 * p + 1], 0, 0, 0)
-            ),
-        ],
+        in_specs=[pl.BlockSpec(memory_space=pltpu.HBM)],
         out_specs=[pl.BlockSpec((1, per_device, 1), lambda p, *_: (p, 0, 0))]
         + [pl.BlockSpec(memory_space=pltpu.HBM)] * len(lengths),
         scratch_shapes=[
+            pltpu.VMEM((pair_count, 2, 2, per_device, depth), jnp.bfloat16),
             pltpu.VMEM((depth // LANES, 2 * per_device, LANES), jnp.float32),
             pltpu.VMEM((2, pieces, piece_rows, depth), jnp.bfloat16),
+            pltpu.SemaphoreType.DMA((pair_count, 2, 2)),
             pltpu.SemaphoreType.DMA((2, pieces)),
         ],
     )
@@ -205,7 +228,7 @@
         + [jax.ShapeDtypeStruct((length, piece_rows, depth), jnp.bfloat16) for length in lengths],
         compiler_params=pltpu.CompilerParams(vmem_limit_bytes=VMEM),
         name="merge",
-    )(pairs.reshape(-1), counts, where, places, rows, rows)
+    )(pairs.reshape(-1), counts, where, places, rows)
 
 
 def place_kernel(filled_ref, quarter_ref, in_ref, *rest):
@@ -278,6 +301,7 @@
         longest = jnp.maximum(longest, lax.ppermute(here, "layers", ring))
     least = all_pieces // QUARTERS
     lengths = sorted({min(size * CAP, -(-least * part // 12)) for part in LIST_PARTS})
+    any_piece = longest > 0
     level = sum((longest > length).astype(jnp.int32) for length in lengths[:-1])
 
     outgoing = prepare(
@@ -293,27 +317,41 @@
             value, "expert", split_axis=0, concat_axis=0, tiled=True, axis_index_groups=groups
         )
 
-    def deal(listed, rows, where, places, from_list):
+    def deal(listed, rows, where, places, from_list, any_piece):
         similarity_part, slots, *lists = merge(
             pairs, counts, where, places, rows, size * CAP, listed
         )
-        arrived = [within_quarter(slots)]
         shifts = (2, 1, 3)
-        for step, shift in enumerate(shifts):
+
+        def permuted(shift, after):
+            chunk, _ = lax.optimization_barrier((lists[shift - 1], after))
             ring = [(device, (device + shift * size) % devices) for device in range(devices)]
-            chunk = lax.ppermute(lists[shift - 1], "expert", ring)
-            spread = jnp.take(chunk, from_list, axis=0, mode="clip")
-            if step == 0:
-                part, arrived[0] = lax.optimization_barrier(
-                    (similarity_part.reshape(1, -1), arrived[0])
-                )
-                similarity = lax.all_to_all(
-                    jnp.broadcast_to(part, (devices, part.shape[1])), "expert", 0, 0, tiled=True
-                )
-                spread, similarity = lax.optimization_barrier((spread, similarity))
-            else:
-                spread, arrived[-1] = lax.optimization_barrier((spread, arrived[-1]))
-            arrived.append(within_quarter(spread))
+            return lax.ppermute(chunk, "expert", ring)
+
+        def unless_empty(exchange, *values):
+            shapes = jax.eval_shape(exchange, *values)
+            zeros = lambda *_: jax.tree.map(lambda v: jnp.zeros(v.shape, v.dtype), shapes)
+            return lax.cond(any_piece, exchange, zeros, *values)
+
+        def spread(chunk, from_list):
+            return within_quarter(jnp.take(chunk, from_list, axis=0, mode="clip"))
+
+        def first_exchange(slots, part):
+            served = within_quarter(slots)
+            part, served = lax.optimization_barrier((part, served))
+            spread_part = jnp.broadcast_to(part, (devices, part.shape[1]))
+            return served, lax.all_to_all(spread_part, "expert", 0, 0, tiled=True)
+
+        chunk = permuted(shifts[0], slots)
+        served, similarity = unless_empty(first_exchange, slots, similarity_part.reshape(1, -1))
+        arrived = [served]
+        for shift in shifts[1:]:
+            chunk, arrived[-1] = lax.optimization_barrier((chunk, arrived[-1]))
+            following = permuted(shift, chunk)
+            arrived.append(unless_empty(spread, chunk, from_list))
+            chunk = following
+        chunk, arrived[-1] = lax.optimization_barrier((chunk, arrived[-1]))
+        arrived.append(spread(chunk, from_list))
         merged = None
         for shift, value in zip((0,) + shifts, arrived):
             origin = ((quarter - shift + QUARTERS) % QUARTERS).astype(jnp.int32)[None]
@@ -329,6 +367,7 @@
         where,
         places,
         from_list,
+        any_piece,
     )
 
 

time: 326 us -> 300 us (0.920)
  blocking collectives: 0 us -> 64.1 us
  waiting for transfers between devices: 197 us -> 138 us
  starting transfers between devices: 72.1 us -> 46.9 us
    ppermute x3, waiting for transfers between devices: 77.9 us -> 1.84 us  [permuted(): return lax.ppermute(chunk, 'expert', ring)]
    all_to_all x0 -> x3, blocking collectives: none -> 64.1 us  [the longest x2 46.2 us: within_quarter(): lax.all_to_all(value, 'expert', split_axis=0, concat_axis=0, tiled=True,...]
    all_to_all x1 -> x0, starting transfers between devices: 20 us -> none  [deal(): lax.all_to_all(jnp.broadcast_to(part, (devices, part.shape[1])), 'expert'...]
    all_to_all x4 -> x2, waiting for transfers between devices: 9.74 us -> 27.4 us  [within_quarter(): lax.all_to_all(value, 'expert', split_axis=0, concat_axis=0, tiled=True,...]
    all_to_all x4 -> x2, starting transfers between devices: 22.3 us -> 8.06 us  [within_quarter(): lax.all_to_all(value, 'expert', split_axis=0, concat_axis=0, tiled=True,...]
    ppermute x3, starting transfers between devices: 19.3 us -> 28.4 us  [permuted(): return lax.ppermute(chunk, 'expert', ring)]
  transfers between devices with their start and end apart: 10 -> 7, of which waited for: 7 -> 5; matrix products, arithmetic and copies ran while one was open for 4% -> 3% of each run, Pallas kernels for 2% -> 3%
where the time goes in v6:
time: 300 us; the launch traced here: 299 us
  waiting for transfers between devices  138 us (46%)
  blocking collectives  64.1 us (21%)
  starting transfers between devices  46.9 us (16%)
  Pallas kernels  29.9 us (10%)
  local copies, waits for them, and re-layouts  15 us (5%)
    all_to_all x1, waiting for transfers between devices, body(): lax.all_to_all(outgoing, 'expert', split_axis=0, concat_axis=0, tiled=True)  108 us
    all_to_all x2, blocking collectives, within_quarter(): lax.all_to_all(value, 'expert', split_axis=0, concat_axis=0, tiled=True,...  46.2 us
    ppermute x3, starting transfers between devices, permuted(): return lax.ppermute(chunk, 'expert', ring)  28.4 us
    all_to_all x2, waiting for transfers between devices, within_quarter(): lax.all_to_all(value, 'expert', split_axis=0, concat_axis=0, tiled=True,...  27.4 us
    all_to_all x1, blocking collectives, first_exchange(): return (served, lax.all_to_all(spread_part, 'expert', 0, 0, tiled=True))  17.8 us
    pallas_call x4, Pallas kernels, place(): pl.pallas_call(place_kernel, grid_spec=grid_spec, out_shape=jax.ShapeDtyp...  11.6 us
    pallas_call x1, Pallas kernels, prepare(): pl.pallas_call(prepare_kernel, grid_spec=grid_spec, out_shape=jax.ShapeDt...  10.3 us
    all_to_all x2, starting transfers between devices, within_quarter(): lax.all_to_all(value, 'expert', split_axis=0, concat_axis=0, tiled=True,...  8.06 us
  transfers between devices with their start and end apart: 7, of which 5 were waited for; matrix products, arithmetic and copies ran while one was open for 3% of the time, Pallas kernels for 3%

profile of v6, /device:TPU:0, one launch (start us, length us, event | category | flops | bytes accessed | tf_op | source)
XLA Modules:
  0.0 298.8 jit_solution(7290392244821881325)
XLA Ops:
  0.6 1.4 copy.160.gate_scale_ref
  2.0 1.4 copy.161.up_scale_ref
  3.3 0.8 copy.159
  4.1 0.6 reshape.302.pairs_ref
  4.7 10.3 %prepare.1 = bf16[16,2,48,2048]{3,2,1,0:T(8,128)(2,1)} custom-call(s32[16]{0:T(128)} %reshape.302.pairs_ref, s32[1]{0:T(128)} %bitcast.86.me_ref, s32[8,768]{1,0:T(8,128)} %order_ref.1, bf16[2048,768]{1,0:T(8,128)(2,1)} %bitcast.156, bf16[2048,768]{1,0:T(8,128)(2,1)} %bitcast.157, bf16[16,6]{1,0:T(8,128)(2,1)} %copy.160.gate_scale_ref, ...), custom_call_target="tpu_custom_call" | custom-call | tf_op jit(solution)/shard_map/prepare/pallas_call | solution.py:93
  15.0 0.0 copy-start.40
  15.0 0.0 copy-start.38
  15.0 0.0 copy-start.39
  15.0 7.5 %all-to-all-start.35 = ((bf16[16,2,48,2048]{3,2,1,0:T(8,128)(2,1)}), bf16[16,2,48,2048]{3,2,1,0:T(8,128)(2,1)}, u32[]{:S(2)}, u32[]{:S(2)}) async-start(bf16[16,2,48,2048]{3,2,1,0:T(8,128)(2,1)} %prepare.1), calls=%async_computation.35 | async-start | bytes 12582912 | tf_op jit(solution)/shard_map/all_to_all | solution.py:310
  22.6 0.0 copy-done.40
  22.6 0.2 select_reduce_fusion.8
  22.8 0.6 reduce_max.9
  24.1 2.9 collective-permute-start.21
  27.0 0.2 select_reduce_fusion.7
  27.2 0.5 collective-permute-done.21
  28.3 108.5 %all-to-all-done.35 = bf16[16,2,48,2048]{3,2,1,0:T(8,128)(2,1)} async-done(((bf16[16,2,48,2048]{3,2,1,0:T(8,128)(2,1)}), bf16[16,2,48,2048]{3,2,1,0:T(8,128)(2,1)}, u32[]{:S(2)}, u32[]{:S(2)}) %all-to-all-start.35) | async-done | bytes 6291488 | tf_op jit(solution)/shard_map/all_to_all | solution.py:310
  136.8 0.0 copy-done.38
  136.8 0.0 copy-done.39
  136.8 162.1 %conditional.22 = (bf16[6,256,2048]{2,1,0:T(8,128)(2,1)}, f32[8,768]{1,0:T(8,128)}) conditional(s32[]{:T(128)} %clamp.3, (s32[]{:T(128)}, s32[8,2]{0,1:T(2,128)S(1)}, s32[16]{0:T(128)S(1)}, s32[48]{0:T(128)S(1)}, pred[48]{0:T(512)(128)(4,1)S(1)}, /*index=5*/bf16[16,2,48,2048]{3,2,1,0:T(8,128)(2,1)}, s32[]{:T(128)}, ...), branch_computations={%region_5.12_spmd, %region_12.19_spmd, %region_19.26_spmd, %region... | conditional | flops 7801 | bytes 56927296 | solution.py:363
  136.8 0.0 copy-start.14
  136.8 0.0 copy-start.26
  136.8 0.1 copy.163
  136.9 0.6 reshape.257.pairs_ref
  137.5 0.6 select_n.176.place_ref
  138.1 0.0 copy-done.14
  138.1 0.0 copy-done.26
  138.1 8.1 %merge.8 = (f32[8,48,1]{2,1,0:T(8,128)S(1)}, bf16[24,16,2048]{2,1,0:T(8,128)(2,1)}, bf16[15,16,2048]{2,1,0:T(8,128)(2,1)}, bf16[15,16,2048]{2,1,0:T(8,128)(2,1)}, bf16[15,16,2048]{2,1,0:T(8,128)(2,1)}) custom-call(s32[16]{0:T(128)} %reshape.257.pairs_ref, s32[16]{0:T(128)S(1)} %get-tuple-element.558.counts_ref, s32[48]{0:T(128)S(1)} %get-tuple-element.304.where_ref, ...), custom_call_target="tpu_custom_call" | custom-call | tf_op jit(solution)/shard_map/cond/branch_1_fun/merge/pallas_call | solution.py:224
  146.2 26.3 %collective-permute-start.3 = (bf16[15,16,2048]{2,1,0:T(8,128)(2,1)}, bf16[15,16,2048]{2,1,0:T(8,128)(2,1)S(1)}, u32[]{:S(2)}, u32[]{:S(2)}) collective-permute-start(bf16[15,16,2048]{2,1,0:T(8,128)(2,1)} %get-tuple-element.311), channel_id=1, source_target_pairs={{0,8},{1,9},{2,10},{3,11},{4,12},{5,13},{6,14},{7,15},{8,0},{9,1},... | collective-permute-start | bytes 2949128 | tf_op jit(solution)/shard_map/cond/branch_1_fun/ppermute | solution.py:329
  172.5 0.0 copy-start.15
  172.5 0.0 copy-start.27
  172.5 42.5 %conditional.3 = (bf16[4,6,16,2048]{3,2,1,0:T(8,128)(2,1)}, f32[16,384]{1,0:T(8,128)S(1)}) conditional(s32[]{:T(128)} %convert_element_type.9, () %tuple.124, (f32[8,48,1]{2,1,0:T(8,128)S(1)}, bf16[24,16,2048]{2,1,0:T(8,128)(2,1)}) %tuple.125), branch_computations={%region_13.13_spmd, %region_14.14_spmd} | conditional | bytes 4852280 | solution.py:334
  172.5 4.5 %all-to-all-start.17 = ((bf16[4,6,16,2048]{3,2,1,0:T(8,128)(2,1)}), bf16[4,6,16,2048]{3,2,1,0:T(8,128)(2,1)}, u32[]{:S(2)}, u32[]{:S(2)}) async-start(bf16[4,6,16,2048]{3,2,1,0:T(8,128)(2,1)} %bitcast.12), calls=%async_computation.17 | async-start | bytes 3145728 | tf_op jit(solution)/shard_map/cond/branch_1_fun/cond/branch_1_fun/all_to_all | solution.py:316
  177.0 0.1 reduce.2
  177.1 0.1 reshape.253
  177.2 19.9 %all-to-all-done.17 = bf16[4,6,16,2048]{3,2,1,0:T(8,128)(2,1)} async-done(((bf16[4,6,16,2048]{3,2,1,0:T(8,128)(2,1)}), bf16[4,6,16,2048]{3,2,1,0:T(8,128)(2,1)}, u32[]{:S(2)}, u32[]{:S(2)}) %all-to-all-start.17) | async-done | bytes 1572896 | tf_op jit(solution)/shard_map/cond/branch_1_fun/cond/branch_1_fun/all_to_all | solution.py:316
  197.2 17.8 %all_to_all.169 = f32[16,1,384]{2,1,0:T(1,128)S(1)} all-to-all(f32[16,1,384]{2,1,0:T(1,128)S(1)} %broadcast_in_dim.171), channel_id=1, replica_groups=mesh['layers'=2,'expert'=16] {'expert'}, dimensions={0} | all-to-all | bytes 49152 | tf_op jit(solution)/shard_map/cond/branch_1_fun/cond/branch_1_fun/all_to_all | solution.py:343
  215.0 0.0 collective-permute-done.3
  215.0 0.6 collective-permute-start.4
  215.6 0.0 copy-done.15
  215.6 0.0 copy-done.27
  215.6 0.1 select_reduce_fusion.1
  215.7 23.3 %conditional.4 = (bf16[4,6,16,2048]{3,2,1,0:T(8,128)(2,1)S(1)}) conditional(s32[]{:T(128)} %convert_element_type.9, () %tuple.128, (s32[24]{0:T(128)S(1)}, bf16[15,16,2048]{2,1,0:T(8,128)(2,1)S(1)}) %tuple.129), branch_computations={%region_15.15_spmd, %region_16.16_spmd} | conditional | flops 1024 | bytes 6295752 | solution.py:334
  215.8 0.6 gather_fusion.2
  216.4 22.6 %all_to_all.170 = bf16[4,6,16,2048]{3,2,1,0:T(8,128)(2,1)S(1)} all-to-all(bf16[4,6,16,2048]{3,2,1,0:T(8,128)(2,1)S(1)} %bitcast.144), channel_id=1, replica_groups={{0,1,2,3},{4,5,6,7},{8,9,10,11},{12,13,14,15},{16,17,18,19},{20,21,22,2..., dimensions={0} | all-to-all | bytes 3145728 | tf_op jit(solution)/shard_map/cond/branch_1_fun/cond/branch_1_fun/all_to_all | solution.py:316
  239.1 1.8 collective-permute-done.4
  240.9 1.5 collective-permute-start.5
  242.4 26.7 %conditional.5 = (bf16[4,6,16,2048]{3,2,1,0:T(8,128)(2,1)S(1)}) conditional(s32[]{:T(128)} %convert_element_type.9, () %tuple.132, (s32[24]{0:T(128)S(1)}, bf16[15,16,2048]{2,1,0:T(8,128)(2,1)}) %tuple.133), branch_computations={%region_17.17_spmd, %region_18.18_spmd} | conditional | flops 1024 | bytes 6295752 | solution.py:334
  242.4 3.0 %gather_fusion.3 = bf16[24,16,2048]{2,1,0:T(8,128)(2,1)} fusion(bf16[15,16,2048]{2,1,0:T(8,128)(2,1)} %get-tuple-element.298, s32[1024]{0:T(1024)S(1)} %pad_clamp_fusion.3), kind=kCustom, calls=%fused_computation.4 | custom fusion | bytes 3145824 | tf_op jit(solution)/shard_map/cond/branch_1_fun/cond/branch_1_fun/jit(_take)/gather | solution.py:337
  245.5 23.6 %all_to_all.171 = bf16[4,6,16,2048]{3,2,1,0:T(8,128)(2,1)S(1)} all-to-all(bf16[4,6,16,2048]{3,2,1,0:T(8,128)(2,1)} %bitcast.145), channel_id=1, replica_groups={{0,1,2,3},{4,5,6,7},{8,9,10,11},{12,13,14,15},{16,17,18,19},{20,21,22,2..., dimensions={0} | all-to-all | bytes 3145728 | tf_op jit(solution)/shard_map/cond/branch_1_fun/cond/branch_1_fun/all_to_all | solution.py:316
  269.1 0.0 copy-start.2
  269.1 0.0 collective-permute-done.5
  269.1 3.7 %gather_fusion.15 = bf16[24,16,2048]{2,1,0:T(8,128)(2,1)} fusion(bf16[15,16,2048]{2,1,0:T(8,128)(2,1)} %collective-permute-done.5, s32[1024]{0:T(1024)S(1)} %pad_clamp_fusion.15), kind=kCustom, calls=%fused_computation.15 | custom fusion | bytes 3145824 | tf_op jit(solution)/shard_map/cond/branch_1_fun/jit(_take)/gather | solution.py:337
  272.8 0.0 copy-done.2
  272.8 3.6 %all-to-all-start.19 = ((bf16[4,6,16,2048]{3,2,1,0:T(8,128)(2,1)}), bf16[4,6,16,2048]{3,2,1,0:T(8,128)(2,1)S(1)}, u32[]{:S(2)}, u32[]{:S(2)}) async-start(bf16[4,6,16,2048]{3,2,1,0:T(8,128)(2,1)} %bitcast.136), calls=%async_computation.19 | async-start | bytes 3145728 | tf_op jit(solution)/shard_map/cond/branch_1_fun/all_to_all | solution.py:316
  276.4 0.7 reduce_sum.48
  277.0 0.8 copy.142
  277.8 1.1 copy.143
  279.0 0.8 reshape.260
  279.8 4.1 %place.32.rest_0_ = bf16[6,256,2048]{2,1,0:T(8,128)(2,1)} custom-call(s32[1]{0:T(128)} %bitcast.15.filled_ref, s32[1]{0:T(128)} %bitcast.20.quarter_ref, bf16[4,6,16,2048]{3,2,1,0:T(8,128)(2,1)} %get-tuple-element.323.in_ref), custom_call_target="tpu_custom_call" | custom-call | tf_op jit(solution)/shard_map/cond/branch_1_fun/place/pallas_call | solution.py:256
  283.9 2.6 place.33.rest_0_
  286.5 0.0 copy-done.3
  286.5 2.5 place.34.rest_0_
  288.9 7.4 %all-to-all-done.19.in_ref = bf16[4,6,16,2048]{3,2,1,0:T(8,128)(2,1)S(1)} async-done(((bf16[4,6,16,2048]{3,2,1,0:T(8,128)(2,1)}), bf16[4,6,16,2048]{3,2,1,0:T(8,128)(2,1)S(1)}, u32[]{:S(2)}, u32[]{:S(2)}) %all-to-all-start.19) | async-done | bytes 1572896 | tf_op jit(solution)/shard_map/cond/branch_1_fun/all_to_all | solution.py:316
  296.4 2.5 place.35
  (11 shorter events, 0.1 us)
Async XLA Ops:
  15.0 7.6 %copy-start.40 = (s32[48,1]{0,1:T(1,128)S(1)}, s32[48,1]{0,1:T(1,128)}, u32[]{:S(2)}) copy-start(s32[48,1]{0,1:T(1,128)} %param.64) | copy-start | bytes 580
  15.0 121.8 %copy-start.38 = (s32[8,2]{0,1:T(2,128)S(1)}, s32[8,2]{0,1:T(2,128)}, u32[]{:S(2)}) copy-start(s32[8,2]{0,1:T(2,128)} %param.61) | copy-start | bytes 196
  15.0 121.8 %copy-start.39 = (s32[16]{0:T(128)S(1)}, s32[16]{0:T(128)}, u32[]{:S(2)}) copy-start(s32[16]{0:T(128)} %param.62) | copy-start | bytes 196
  15.0 121.7 %all-to-all-start.35 = ((bf16[16,2,48,2048]{3,2,1,0:T(8,128)(2,1)}), bf16[16,2,48,2048]{3,2,1,0:T(8,128)(2,1)}, u32[]{:S(2)}, u32[]{:S(2)}) async-start(bf16[16,2,48,2048]{3,2,1,0:T(8,128)(2,1)} %prepare.1), calls=%async_computation.35 | async-start | bytes 12582912 | tf_op jit(solution)/shard_map/all_to_all | solution.py:310
  24.1 3.6 %collective-permute-start.21 = (s32[]{:T(128)}, s32[]{:T(128)}, u32[]{:S(2)}, u32[]{:S(2)}) collective-permute-start(s32[]{:T(128)} %add.293), channel_id=1, source_target_pairs={{0,16},{16,0},{1,17},{17,1},{2,18},{18,2},{3,19},{19,3},{4,20},{20... | collective-permute-start | bytes 20 | tf_op jit(solution)/shard_map/ppermute | solution.py:301
  136.8 1.3 copy-start.14
  136.8 1.3 copy-start.26
  146.2 68.9 %collective-permute-start.3 = (bf16[15,16,2048]{2,1,0:T(8,128)(2,1)}, bf16[15,16,2048]{2,1,0:T(8,128)(2,1)S(1)}, u32[]{:S(2)}, u32[]{:S(2)}) collective-permute-start(bf16[15,16,2048]{2,1,0:T(8,128)(2,1)} %get-tuple-element.311), channel_id=1, source_target_pairs={{0,8},{1,9},{2,10},{3,11},{4,12},{5,13},{6,14},{7,15},{8,0},{9,1},... | collective-permute-start | bytes 2949128 | tf_op jit(solution)/shard_map/cond/branch_1_fun/ppermute | solution.py:329
  172.5 43.2 %copy-start.15 = (s32[48]{0:T(128)S(1)}, s32[48]{0:T(128)}, u32[]{:S(2)}) copy-start(s32[48]{0:T(128)} %copy-done.14) | copy-start | bytes 580 | tf_op jit(solution)/shard_map/cond
  172.5 43.2 %copy-start.27 = (s32[48]{0:T(128)S(1)}, s32[48]{0:T(128)}, u32[]{:S(2)}) copy-start(s32[48]{0:T(128)} %copy-done.26) | copy-start | bytes 580 | tf_op jit(solution)/shard_map/cond
  172.5 24.6 %all-to-all-start.17 = ((bf16[4,6,16,2048]{3,2,1,0:T(8,128)(2,1)}), bf16[4,6,16,2048]{3,2,1,0:T(8,128)(2,1)}, u32[]{:S(2)}, u32[]{:S(2)}) async-start(bf16[4,6,16,2048]{3,2,1,0:T(8,128)(2,1)} %bitcast.12), calls=%async_computation.17 | async-start | bytes 3145728 | tf_op jit(solution)/shard_map/cond/branch_1_fun/cond/branch_1_fun/all_to_all | solution.py:316
  215.0 25.9 %collective-permute-start.4 = (bf16[15,16,2048]{2,1,0:T(8,128)(2,1)}, bf16[15,16,2048]{2,1,0:T(8,128)(2,1)}, u32[]{:S(2)}, u32[]{:S(2)}) collective-permute-start(bf16[15,16,2048]{2,1,0:T(8,128)(2,1)} %get-tuple-element.316), channel_id=1, source_target_pairs={{0,4},{1,5},{2,6},{3,7},{4,8},{5,9},{6,10},{7,11},{8,12},{9,13},{1... | collective-permute-start | bytes 2949128 | tf_op jit(solution)/shard_map/cond/branch_1_fun/ppermute | solution.py:329
  240.9 28.2 %collective-permute-start.5 = (bf16[15,16,2048]{2,1,0:T(8,128)(2,1)}, bf16[15,16,2048]{2,1,0:T(8,128)(2,1)}, u32[]{:S(2)}, u32[]{:S(2)}) collective-permute-start(bf16[15,16,2048]{2,1,0:T(8,128)(2,1)} %get-tuple-element.319), channel_id=1, source_target_pairs={{0,12},{1,13},{2,14},{3,15},{4,0},{5,1},{6,2},{7,3},{8,4},{9,5},{1... | collective-permute-start | bytes 2949128 | tf_op jit(solution)/shard_map/cond/branch_1_fun/ppermute | solution.py:329
  269.1 3.7 %copy-start.2 = (bf16[4,6,16,2048]{3,2,1,0:T(8,128)(2,1)}, bf16[4,6,16,2048]{3,2,1,0:T(8,128)(2,1)S(1)}, u32[]{:S(2)}) copy-start(bf16[4,6,16,2048]{3,2,1,0:T(8,128)(2,1)S(1)} %get-tuple-element.1264.in_ref) | copy-start | bytes 4718596 | tf_op jit(solution)/shard_map/cond
  272.8 23.6 %all-to-all-start.19 = ((bf16[4,6,16,2048]{3,2,1,0:T(8,128)(2,1)}), bf16[4,6,16,2048]{3,2,1,0:T(8,128)(2,1)S(1)}, u32[]{:S(2)}, u32[]{:S(2)}) async-start(bf16[4,6,16,2048]{3,2,1,0:T(8,128)(2,1)} %bitcast.136), calls=%async_computation.19 | async-start | bytes 3145728 | tf_op jit(solution)/shard_map/cond/branch_1_fun/all_to_all | solution.py:316
  283.9 2.6 copy-start.3

commit v7 on v6

--- a/solution.py
+++ b/solution.py
@@ -31,7 +31,7 @@
         order = lax.broadcasted_iota(jnp.int32, (1, units), 1)
         for pair in range(order_ref.shape[0]):
             order = jnp.where(
-                pairs_ref[2 * pair + 1] == me_ref[0], order_ref[pair : pair + 1, :], order
+                pairs_ref[1, pair] == me_ref[0], order_ref[pair : pair + 1, :], order
             )
         share = U // devices
         columns = lax.broadcasted_iota(jnp.int32, (1, units), 1)
@@ -50,12 +50,13 @@
                 (source == columns).astype(jnp.float32).astype(jnp.bfloat16)
             )
         for kind, scales in enumerate((gate_scale_ref, up_scale_ref)):
-            value = scales[...].astype(jnp.float32)
-            block = lax.div(lax.broadcasted_iota(jnp.int32, (value.shape[0], units), 1), BLK)
-            spread = jnp.zeros((value.shape[0], units), jnp.float32)
-            for index in range(value.shape[1]):
-                spread = jnp.where(block == index, value[:, index : index + 1], spread)
-            scale_ref[kind] = spread
+            blocks = scales.shape[0]
+            block = lax.broadcasted_iota(jnp.int32, (blocks, units), 0)
+            column = lax.broadcasted_iota(jnp.int32, (blocks, units), 1)
+            covers = (lax.div(column, BLK) == block).astype(jnp.float32).astype(jnp.bfloat16)
+            scale_ref[kind] = lax.dot_general(
+                scales[...], covers, (((0,), (0,)), ((), ())), preferred_element_type=jnp.float32
+            )
 
     for kind, codes_ref in enumerate((gate_ref, up_ref)):
         parts = []
@@ -96,7 +97,7 @@
         out_shape=jax.ShapeDtypeStruct((devices, 2, per_device, depth), jnp.bfloat16),
         compiler_params=pltpu.CompilerParams(vmem_limit_bytes=VMEM),
         name="prepare",
-    )(pairs.reshape(-1), me[None], unit_order, gate_codes, up_codes, gate_scale, up_scale)
+    )(pairs.T, me[None], unit_order, gate_codes, up_codes, gate_scale, up_scale)
 
 
 def merge_kernel(
@@ -107,11 +108,17 @@
     pair_count = pl.num_programs(0)
     per_device, depth = held.shape[3], held.shape[4]
     pieces, piece_rows = ready.shape[1], ready.shape[2]
+    targets = (
+        [(outs[0], 0)],
+        [(outs[1], 0)],
+        [(outs[2], 0), (outs[3], depth // 2)],
+        [(outs[4], 0)],
+    )
 
     def fetches(which_pair):
         return [
             pltpu.make_async_copy(
-                rows_ref.at[pairs_ref[2 * which_pair + who], kind],
+                rows_ref.at[pairs_ref[who, which_pair], kind],
                 held.at[which_pair, who, kind],
                 arrive.at[which_pair, who, kind],
             )
@@ -128,8 +135,8 @@
 
     for copy in fetches(pair):
         copy.wait()
-    left_freq = counts_ref[pairs_ref[2 * pair]].astype(jnp.float32)
-    right_freq = counts_ref[pairs_ref[2 * pair + 1]].astype(jnp.float32)
+    left_freq = counts_ref[pairs_ref[0, pair]].astype(jnp.float32)
+    right_freq = counts_ref[pairs_ref[1, pair]].astype(jnp.float32)
     group = 16 if per_device % 16 == 0 else per_device
 
     def values_of(first, block):
@@ -173,17 +180,18 @@
     def each_copy(which_pair, which_slot, act):
         for piece in range(pieces):
             index = which_pair * pieces + piece
-            for where, out_ref in enumerate(outs):
+            for where, parts in enumerate(targets):
 
                 @pl.when(where_ref[index] == where)
                 def _():
-                    act(
-                        pltpu.make_async_copy(
-                            ready.at[which_slot, piece],
-                            out_ref.at[place_ref[index]],
-                            sems.at[which_slot, piece],
+                    for part, (out_ref, begin) in enumerate(parts):
+                        act(
+                            pltpu.make_async_copy(
+                                ready.at[which_slot, piece, :, pl.ds(begin, out_ref.shape[-1])],
+                                out_ref.at[place_ref[index]],
+                                sems.at[which_slot, piece, part],
+                            )
                         )
-                    )
 
     @pl.when(pair >= 2)
     def _():
@@ -206,33 +214,67 @@
     pair_count = pairs.shape[0]
     pieces = where.shape[0] // pair_count
     piece_rows = 2 * per_device // pieces
-    lengths = (slots,) + (listed,) * (QUARTERS - 1)
+    shapes = [(slots, depth), (listed, depth), (listed, depth // 2), (listed, depth // 2), (listed, depth)]
     grid_spec = pltpu.PrefetchScalarGridSpec(
         num_scalar_prefetch=4,
         grid=(pair_count,),
         in_specs=[pl.BlockSpec(memory_space=pltpu.HBM)],
         out_specs=[pl.BlockSpec((1, per_device, 1), lambda p, *_: (p, 0, 0))]
-        + [pl.BlockSpec(memory_space=pltpu.HBM)] * len(lengths),
+        + [pl.BlockSpec(memory_space=pltpu.HBM)] * len(shapes),
         scratch_shapes=[
             pltpu.VMEM((pair_count, 2, 2, per_device, depth), jnp.bfloat16),
             pltpu.VMEM((depth // LANES, 2 * per_device, LANES), jnp.float32),
             pltpu.VMEM((2, pieces, piece_rows, depth), jnp.bfloat16),
             pltpu.SemaphoreType.DMA((pair_count, 2, 2)),
-            pltpu.SemaphoreType.DMA((2, pieces)),
+            pltpu.SemaphoreType.DMA((2, pieces, 2)),
         ],
     )
     return pl.pallas_call(
         merge_kernel,
         grid_spec=grid_spec,
         out_shape=[jax.ShapeDtypeStruct((pair_count, per_device, 1), jnp.float32)]
-        + [jax.ShapeDtypeStruct((length, piece_rows, depth), jnp.bfloat16) for length in lengths],
+        + [
+            jax.ShapeDtypeStruct((length, piece_rows, width), jnp.bfloat16)
+            for length, width in shapes
+        ],
         compiler_params=pltpu.CompilerParams(vmem_limit_bytes=VMEM),
         name="merge",
-    )(pairs.reshape(-1), counts, where, places, rows)
-
-
-def place_kernel(filled_ref, quarter_ref, in_ref, *rest):
-    out_ref = rest[-1]
+    )(pairs.T, counts, where, places, rows)
+
+
+def place_three_kernel(filled_ref, quarters_ref, *refs):
+    in_refs, out_ref = refs[:-1], refs[-1]
+    slots, rows, _ = out_ref.shape
+    count = rows // QUARTERS
+    for slot in range(slots):
+        keep = pl.program_id(0) * slots + slot < filled_ref[0]
+        for index, in_ref in enumerate(in_refs):
+            value = in_ref[:, slot].reshape(count, out_ref.shape[2])
+            first = pl.multiple_of(quarters_ref[index] * count, count)
+            out_ref[slot, pl.ds(first, count), :] = jnp.where(keep, value, jnp.zeros_like(value))
+
+
+def place_three(filled, quarters, arrived):
+    sources, cap, piece_rows, depth = arrived[0].shape
+    slots = 2
+    rows = QUARTERS * sources * piece_rows
+    grid_spec = pltpu.PrefetchScalarGridSpec(
+        num_scalar_prefetch=2,
+        grid=(cap // slots,),
+        in_specs=[pl.BlockSpec((sources, slots, piece_rows, depth), lambda s, *_: (0, s, 0, 0))]
+        * len(arrived),
+        out_specs=pl.BlockSpec((slots, rows, depth), lambda s, *_: (s, 0, 0)),
+    )
+    return pl.pallas_call(
+        place_three_kernel,
+        grid_spec=grid_spec,
+        out_shape=jax.ShapeDtypeStruct((cap, rows, depth), arrived[0].dtype),
+        compiler_params=pltpu.CompilerParams(vmem_limit_bytes=VMEM // 2),
+        name="place_three",
+    )(filled, quarters, *arrived)
+
+
+def place_kernel(filled_ref, quarter_ref, in_ref, base_ref, out_ref):
     slots = out_ref.shape[0]
     for slot in range(slots):
         value = in_ref[:, slot].reshape(out_ref.shape[1:])
@@ -240,27 +282,28 @@
         out_ref[slot] = jnp.where(keep, value, jnp.zeros_like(value))
 
 
-def place(filled, quarter, arrived, base=None):
-    sources, cap, piece_rows, depth = arrived.shape
+def place(filled, quarter, arrived, part, base):
+    sources, cap, piece_rows, width = arrived.shape
     slots = 2
-    bases = () if base is None else (base,)
     grid_spec = pltpu.PrefetchScalarGridSpec(
         num_scalar_prefetch=2,
         grid=(cap // slots,),
-        in_specs=[pl.BlockSpec((sources, slots, piece_rows, depth), lambda s, *_: (0, s, 0, 0))]
-        + [pl.BlockSpec(memory_space=pltpu.HBM)] * len(bases),
+        in_specs=[
+            pl.BlockSpec((sources, slots, piece_rows, width), lambda s, *_: (0, s, 0, 0)),
+            pl.BlockSpec(memory_space=pltpu.HBM),
+        ],
         out_specs=pl.BlockSpec(
-            (slots, sources * piece_rows, depth), lambda s, filled, quarter: (s, quarter[0], 0)
+            (slots, sources * piece_rows, width), lambda s, filled, quarter: (s, quarter[0], part)
         ),
     )
     return pl.pallas_call(
         place_kernel,
         grid_spec=grid_spec,
-        out_shape=jax.ShapeDtypeStruct((cap, QUARTERS * sources * piece_rows, depth), arrived.dtype),
-        input_output_aliases={3: 0} if bases else {},
+        out_shape=jax.ShapeDtypeStruct(base.shape, base.dtype),
+        input_output_aliases={3: 0},
         compiler_params=pltpu.CompilerParams(vmem_limit_bytes=VMEM // 4),
         name="place",
-    )(filled, quarter, arrived, *bases)
+    )(filled, quarter, arrived, base)
 
 
 def body(gate_codes, up_codes, gate_scale, up_scale, pairs, counts, unit_order, owners):
@@ -305,7 +348,7 @@
     level = sum((longest > length).astype(jnp.int32) for length in lengths[:-1])
 
     outgoing = prepare(
-        pairs, me, unit_order, gate_codes[0], up_codes[0], gate_scale[0], up_scale[0], devices
+        pairs, me, unit_order, gate_codes[0], up_codes[0], gate_scale[0].T, up_scale[0].T, devices
     )
     rows = lax.all_to_all(outgoing, "expert", split_axis=0, concat_axis=0, tiled=True)
 
@@ -318,15 +361,18 @@
         )
 
     def deal(listed, rows, where, places, from_list, any_piece):
-        similarity_part, slots, *lists = merge(
+        similarity_part, slots, next_list, far_first, far_second, last_list = merge(
             pairs, counts, where, places, rows, size * CAP, listed
         )
-        shifts = (2, 1, 3)
-
-        def permuted(shift, after):
-            chunk, _ = lax.optimization_barrier((lists[shift - 1], after))
+        origins = jnp.stack([(quarter - shift + QUARTERS) % QUARTERS for shift in range(QUARTERS)])
+        origins = origins.astype(jnp.int32)
+
+        def permuted(chunk, shift):
             ring = [(device, (device + shift * size) % devices) for device in range(devices)]
             return lax.ppermute(chunk, "expert", ring)
+
+        def in_order(*values):
+            return lax.optimization_barrier(values)
 
         def unless_empty(exchange, *values):
             shapes = jax.eval_shape(exchange, *values)
@@ -336,26 +382,40 @@
         def spread(chunk, from_list):
             return within_quarter(jnp.take(chunk, from_list, axis=0, mode="clip"))
 
-        def first_exchange(slots, part):
-            served = within_quarter(slots)
-            part, served = lax.optimization_barrier((part, served))
-            spread_part = jnp.broadcast_to(part, (devices, part.shape[1]))
-            return served, lax.all_to_all(spread_part, "expert", 0, 0, tiled=True)
-
-        chunk = permuted(shifts[0], slots)
-        served, similarity = unless_empty(first_exchange, slots, similarity_part.reshape(1, -1))
-        arrived = [served]
-        for shift in shifts[1:]:
-            chunk, arrived[-1] = lax.optimization_barrier((chunk, arrived[-1]))
-            following = permuted(shift, chunk)
-            arrived.append(unless_empty(spread, chunk, from_list))
-            chunk = following
-        chunk, arrived[-1] = lax.optimization_barrier((chunk, arrived[-1]))
-        arrived.append(spread(chunk, from_list))
-        merged = None
-        for shift, value in zip((0,) + shifts, arrived):
-            origin = ((quarter - shift + QUARTERS) % QUARTERS).astype(jnp.int32)[None]
-            merged = place(filled, origin, value, merged)
+        def spread_and_place(chunk, from_list, filled, quarters, *arrived):
+            return spread(chunk, from_list), place_three(filled, quarters, arrived)
+
+        one_on = permuted(next_list, 1)
+        own = unless_empty(within_quarter, slots)
+        one_on, own = in_order(one_on, own)
+        last_list, _ = in_order(last_list, one_on)
+        three_on = permuted(last_list, 3)
+        from_one = unless_empty(spread, one_on, from_list)
+        three_on, from_one = in_order(three_on, from_one)
+        far_first, _ = in_order(far_first, three_on)
+        two_on = permuted(far_first, 2)
+        from_three = unless_empty(spread, three_on, from_list)
+        two_on, from_three = in_order(two_on, from_three)
+        far_second, _ = in_order(far_second, two_on)
+        rest_on = permuted(far_second, 2)
+        from_two, merged = unless_empty(
+            spread_and_place,
+            two_on,
+            from_list,
+            filled,
+            origins[jnp.array([0, 1, 3])],
+            own,
+            from_one,
+            from_three,
+        )
+        part, from_two = in_order(similarity_part.reshape(1, -1), from_two)
+        similarity = lax.all_to_all(
+            jnp.broadcast_to(part, (devices, part.shape[1])), "expert", 0, 0, tiled=True
+        )
+        rest_on, similarity = in_order(rest_on, similarity)
+        from_rest = spread(rest_on, from_list)
+        merged = place(filled, origins[2:3], from_two, 0, merged)
+        merged = place(filled, origins[2:3], from_rest, 1, merged)
         similarity = similarity.reshape(devices, pair_count, pieces, share_units)
         similarity = similarity.transpose(1, 2, 0, 3).reshape(pair_count, units)
         return merged, similarity

time: 300 us -> 306 us (1.020); the launches traced: 299 us -> 311 us
  blocking collectives: 64.1 us -> 71 us
  starting transfers between devices: 46.9 us -> 53.8 us
  local copies, waits for them, and re-layouts: 15 us -> 11.7 us
    all_to_all x2 -> x3, blocking collectives: 46.2 us -> 71 us  [within_quarter(): lax.all_to_all(value, 'expert', split_axis=0, concat_axis=0, tiled=True,...]
    all_to_all x1 -> x0, blocking collectives: 17.8 us -> none  [first_exchange(): return (served, lax.all_to_all(spread_part, 'expert', 0, 0, tiled=True))]
    all_to_all x2, waiting for transfers between devices: 27.4 us -> 12.5 us  [within_quarter(): lax.all_to_all(value, 'expert', split_axis=0, concat_axis=0, tiled=True,...]
    all_to_all x0 -> x1, waiting for transfers between devices: none -> 8.67 us  [deal(): lax.all_to_all(jnp.broadcast_to(part, (devices, part.shape[1])), 'expert'...]
    pallas_call x0 -> x1, Pallas kernels: none -> 6.19 us  [place_three(): pl.pallas_call(place_three_kernel, grid_spec=grid_spec, out_shape=jax.Sha...]
    pallas_call x4 -> x2, Pallas kernels: 11.6 us -> 5.67 us  [place(): pl.pallas_call(place_kernel, grid_spec=grid_spec, out_shape=jax.ShapeDtyp...]
    ppermute x3 -> x4, waiting for transfers between devices: 1.84 us -> 7.62 us  [permuted(): return lax.ppermute(chunk, 'expert', ring)]
    all_to_all x0 -> x1, starting transfers between devices: none -> 4.02 us  [deal(): lax.all_to_all(jnp.broadcast_to(part, (devices, part.shape[1])), 'expert'...]
  transfers between devices with their start and end apart: 7 -> 9, of which waited for: 5 -> 8; matrix products, arithmetic and copies ran while one was open for 3% -> 4% of each run, Pallas kernels for 3% -> 3%
where the time goes in v7:
time: 306 us; the launch traced here: 311 us
  waiting for transfers between devices  138 us (45%)
  blocking collectives  71 us (23%)
  starting transfers between devices  53.8 us (18%)
  Pallas kernels  31.3 us (10%)
  local copies, waits for them, and re-layouts  11.7 us (4%)
    all_to_all x1, waiting for transfers between devices, body(): lax.all_to_all(outgoing, 'expert', split_axis=0, concat_axis=0, tiled=True)  108 us
    all_to_all x3, blocking collectives, within_quarter(): lax.all_to_all(value, 'expert', split_axis=0, concat_axis=0, tiled=True,...  71 us
    ppermute x4, starting transfers between devices, permuted(): return lax.ppermute(chunk, 'expert', ring)  30.9 us
    all_to_all x2, waiting for transfers between devices, within_quarter(): lax.all_to_all(value, 'expert', split_axis=0, concat_axis=0, tiled=True,...  12.5 us
    pallas_call x1, Pallas kernels, prepare(): pl.pallas_call(prepare_kernel, grid_spec=grid_spec, out_shape=jax.ShapeDt...  10.3 us
    pallas_call x1, Pallas kernels, merge(): pl.pallas_call(merge_kernel, grid_spec=grid_spec, out_shape=[jax.ShapeDty...  9.17 us
    all_to_all x1, waiting for transfers between devices, deal(): lax.all_to_all(jnp.broadcast_to(part, (devices, part.shape[1])), 'expert'...  8.67 us
    all_to_all x2, starting transfers between devices, within_quarter(): lax.all_to_all(value, 'expert', split_axis=0, concat_axis=0, tiled=True,...  8.46 us
  transfers between devices with their start and end apart: 9, of which 8 were waited for; matrix products, arithmetic and copies ran while one was open for 4% of the time, Pallas kernels for 3%

profile of v7, /device:TPU:0, one launch (start us, length us, event | category | flops | bytes accessed | tf_op | source)
XLA Modules:
  0.0 310.9 jit_solution(16910448218861089697)
XLA Ops:
  0.6 10.3 %prepare.1 = bf16[16,2,48,2048]{3,2,1,0:T(8,128)(2,1)} custom-call(s32[2,8]{1,0:T(2,128)} %bitcast.181, s32[1]{0:T(128)} %bitcast.108.me_ref, s32[8,768]{1,0:T(8,128)} %order_ref.1, bf16[2048,768]{1,0:T(8,128)(2,1)} %bitcast.151, bf16[2048,768]{1,0:T(8,128)(2,1)} %bitcast.152, bf16[6,16]{1,0:T(8,128)(2,1)} %bitcast.189, bf16[6,16]{1,0:T(8,128)(2,1)} %bitcast.190), custom_call_target="tpu_custom_call" | custom-call | tf_op jit(solution)/shard_map/prepare/pallas_call | solution.py:94
  10.9 0.0 copy-start.13
  10.9 0.0 copy-start.14
  10.9 0.0 copy-start.15
  10.9 7.5 %all-to-all-start.42 = ((bf16[16,2,48,2048]{3,2,1,0:T(8,128)(2,1)}), bf16[16,2,48,2048]{3,2,1,0:T(8,128)(2,1)}, u32[]{:S(2)}, u32[]{:S(2)}) async-start(bf16[16,2,48,2048]{3,2,1,0:T(8,128)(2,1)} %prepare.1), calls=%async_computation.42 | async-start | bytes 12582912 | tf_op jit(solution)/shard_map/all_to_all | solution.py:353
  18.5 0.0 copy-done.13
  18.6 0.2 select_reduce_fusion.14
  18.8 0.6 reduce_max.9
  20.0 2.9 collective-permute-start.28
  22.9 0.7 collective-permute-done.28
  24.2 108.5 %all-to-all-done.42 = bf16[16,2,48,2048]{3,2,1,0:T(8,128)(2,1)} async-done(((bf16[16,2,48,2048]{3,2,1,0:T(8,128)(2,1)}), bf16[16,2,48,2048]{3,2,1,0:T(8,128)(2,1)}, u32[]{:S(2)}, u32[]{:S(2)}) %all-to-all-start.42) | async-done | bytes 6291488 | tf_op jit(solution)/shard_map/all_to_all | solution.py:353
  132.7 0.0 copy-done.14
  132.7 0.0 copy-done.15
  132.7 178.0 %conditional.29 = (bf16[6,256,2048]{2,1,0:T(8,128)(2,1)}, f32[8,768]{1,0:T(8,128)}) conditional(s32[]{:T(128)} %clamp.3, (s32[]{:T(128)}, s32[8,2]{0,1:T(2,128)S(1)}, s32[16]{0:T(128)S(1)}, s32[48]{0:T(128)S(1)}, s32[48]{0:T(128)S(1)}, /*index=5*/bf16[16,2,48,2048]{3,2,1,0:T(8,128)(2,1)}, s32[]{:T(128)}, ...), branch_computations={%region_5.14_spmd, %region_14.23_spmd, %region_23.32_spmd, %region... | conditional | flops 19365 | bytes 48015384 | solution.py:423
  133.0 0.2 select_reduce_fusion.10
  133.2 0.5 fusion.14
  133.7 9.2 %merge.12 = (f32[8,48,1]{2,1,0:T(8,128)}, bf16[24,16,2048]{2,1,0:T(8,128)(2,1)}, bf16[20,16,2048]{2,1,0:T(8,128)(2,1)}, bf16[20,16,1024]{2,1,0:T(8,128)(2,1)}, b...) custom-call(s32[2,8]{1,0:T(2,128)S(1)} %bitcast.187, s32[16]{0:T(128)S(1)} %get-tuple-element.835.counts_ref, ...), custom_call_target="tpu_custom_call" | custom-call | tf_op jit(solution)/shard_map/cond/branch_5_fun/merge/pallas_call | solution.py:232
  142.9 23.5 %collective-permute-start.20 = (bf16[20,16,2048]{2,1,0:T(8,128)(2,1)}, bf16[20,16,2048]{2,1,0:T(8,128)(2,1)S(1)}, u32[]{:S(2)}, u32[]{:S(2)}) collective-permute-start(bf16[20,16,2048]{2,1,0:T(8,128)(2,1)} %get-tuple-element.692), channel_id=1, source_target_pairs={{0,4},{1,5},{2,6},{3,7},{4,8},{5,9},{6,10},{7,11},{8,12},{9,13},{1... | collective-permute-start | bytes 3932168 | tf_op jit(solution)/shard_map/cond/branch_5_fun/ppermute | solution.py:372
  166.4 24.4 %conditional.20 = (bf16[4,6,16,2048]{3,2,1,0:T(8,128)(2,1)S(1)}) conditional(s32[]{:T(128)} %convert_element_type.31, () %tuple.231, bf16[24,16,2048]{2,1,0:T(8,128)(2,1)} %get-tuple-element.694), branch_computations={%region_51.51_spmd, %region_52.52_spmd} | conditional | bytes 3145736 | solution.py:380
  166.4 24.4 %all_to_all.209 = bf16[4,6,16,2048]{3,2,1,0:T(8,128)(2,1)S(1)} all-to-all(bf16[4,6,16,2048]{3,2,1,0:T(8,128)(2,1)} %bitcast.158), channel_id=1, replica_groups={{0,1,2,3},{4,5,6,7},{8,9,10,11},{12,13,14,15},{16,17,18,19},{20,21,22,2..., dimensions={0} | all-to-all | bytes 3145728 | tf_op jit(solution)/shard_map/cond/branch_5_fun/cond/branch_1_fun/all_to_all | solution.py:359
  190.8 3.7 %collective-permute-done.20 = bf16[20,16,2048]{2,1,0:T(8,128)(2,1)S(1)} collective-permute-done((bf16[20,16,2048]{2,1,0:T(8,128)(2,1)}, bf16[20,16,2048]{2,1,0:T(8,128)(2,1)S(1)}, u32[]{:S(2)}, u32[]{:S(2)}) %collective-permute-start.20) | collective-permute-done | bytes 1310752 | tf_op jit(solution)/shard_map/cond/branch_5_fun/ppermute | solution.py:372
  194.6 4.9 %collective-permute-start.21 = (bf16[20,16,2048]{2,1,0:T(8,128)(2,1)}, bf16[20,16,2048]{2,1,0:T(8,128)(2,1)}, u32[]{:S(2)}, u32[]{:S(2)}) collective-permute-start(bf16[20,16,2048]{2,1,0:T(8,128)(2,1)} %get-tuple-element.696), channel_id=1, source_target_pairs={{0,12},{1,13},{2,14},{3,15},{4,0},{5,1},{6,2},{7,3},{8,4},{9,5},{1... | collective-permute-start | bytes 3932168 | tf_op jit(solution)/shard_map/cond/branch_5_fun/ppermute | solution.py:372
  199.5 0.1 select_reduce_fusion.11
  199.6 26.3 %conditional.21 = (bf16[4,6,16,2048]{3,2,1,0:T(8,128)(2,1)}) conditional(s32[]{:T(128)} %convert_element_type.31, () %tuple.234, (s32[24]{0:T(128)S(1)}, bf16[20,16,2048]{2,1,0:T(8,128)(2,1)S(1)}) %tuple.235), branch_computations={%region_53.53_spmd, %region_54.54_spmd} | conditional | flops 1024 | bytes 11538660 | solution.py:380
  199.6 0.0 copy-start.5
  199.6 1.0 copy-done.5
  200.7 2.0 gather_fusion.20
  202.6 23.3 %all_to_all.210 = bf16[4,6,16,2048]{3,2,1,0:T(8,128)(2,1)} all-to-all(bf16[4,6,16,2048]{3,2,1,0:T(8,128)(2,1)S(1)} %bitcast.147), channel_id=1, replica_groups={{0,1,2,3},{4,5,6,7},{8,9,10,11},{12,13,14,15},{16,17,18,19},{20,21,22,2..., dimensions={0} | all-to-all | bytes 3145728 | tf_op jit(solution)/shard_map/cond/branch_5_fun/cond/branch_1_fun/all_to_all | solution.py:359
  225.9 1.1 collective-permute-done.21
  227.0 2.4 collective-permute-start.22
  229.5 0.0 copy-start.11
  229.5 25.3 %conditional.22 = (bf16[4,6,16,2048]{3,2,1,0:T(8,128)(2,1)}) conditional(s32[]{:T(128)} %convert_element_type.31, () %tuple.238, (s32[24]{0:T(128)S(1)}, bf16[20,16,2048]{2,1,0:T(8,128)(2,1)}) %tuple.239), branch_computations={%region_55.55_spmd, %region_56.56_spmd} | conditional | flops 1024 | bytes 6295752 | solution.py:380
  229.5 2.0 gather_fusion.21
  231.5 23.3 %all_to_all.211 = bf16[4,6,16,2048]{3,2,1,0:T(8,128)(2,1)} all-to-all(bf16[4,6,16,2048]{3,2,1,0:T(8,128)(2,1)S(1)} %bitcast.148), channel_id=1, replica_groups={{0,1,2,3},{4,5,6,7},{8,9,10,11},{12,13,14,15},{16,17,18,19},{20,21,22,2..., dimensions={0} | all-to-all | bytes 3145728 | tf_op jit(solution)/shard_map/cond/branch_5_fun/cond/branch_1_fun/all_to_all | solution.py:359
  254.8 2.7 collective-permute-done.22
  257.6 0.0 collective-permute-start.23
  257.6 0.7 reduce_sum.52
  258.2 0.0 copy-done.11
  258.2 0.1 reduce.10
  258.4 0.1 reshape.280
  258.5 0.1 pad_add_fusion.5
  258.5 19.9 %conditional.23 = (bf16[4,6,16,1024]{3,2,1,0:T(8,128)(2,1)}, bf16[6,256,2048]{2,1,0:T(8,128)(2,1)}) conditional(s32[]{:T(128)} %convert_element_type.31, () %tuple.242, (s32[24]{0:T(128)S(1)}, bf16[20,16,1024]{2,1,0:T(8,128)(2,1)}, (), s32[4]{0:T(128)S(1)}, s32[1]{0:T(128)}, /*index=5*/bf16[4,6,16,2048]{3,2,1,0:T(8,128)(2,1)S(1)}, ...), branch_computations={%region_57.57_spmd, %region_58.58_spmd} | conditional | flops 2048 | bytes 7077908 | solution.py:380
  258.5 0.0 copy-start.21
  258.5 2.6 gather_fusion.22
  261.2 5.0 %all-to-all-start.24 = ((bf16[4,6,16,1024]{3,2,1,0:T(8,128)(2,1)}), bf16[4,6,16,1024]{3,2,1,0:T(8,128)(2,1)}, u32[]{:S(2)}, u32[]{:S(2)}) async-start(bf16[4,6,16,1024]{3,2,1,0:T(8,128)(2,1)} %bitcast.78), calls=%async_computation.24 | async-start | bytes 1572864 | tf_op jit(solution)/shard_map/cond/branch_5_fun/cond/branch_1_fun/all_to_all | solution.py:359
  266.1 0.0 copy-done.21
  266.2 0.6 gather_fusion.23
  266.8 6.2 %place_three.12 = bf16[6,256,2048]{2,1,0:T(8,128)(2,1)} custom-call(s32[1]{0:T(128)} %get-tuple-element.676.filled_ref, s32[3]{0:T(128)S(1)} %gather_fusion.23, bf16[4,6,16,2048]{3,2,1,0:T(8,128)(2,1)S(1)} %get-tuple-element.679.refs_0_, bf16[4,6,16,2048]{3,2,1,0:T(8,128)(2,1)} %get-tuple-element.680.refs_1_, bf16[4,6,16,2048]{3,2,1,0:T(8,128)(2,1)} %get-tuple-element.681.refs_2_), custom_call_target="tpu_custom_call" | custom-call | tf_op jit(solution)/shard_map/cond/branch_5_fun/cond/branch_1_fun/place_three/pallas_call | solution.py:268
  273.0 5.4 %all-to-all-done.24 = bf16[4,6,16,1024]{3,2,1,0:T(8,128)(2,1)} async-done(((bf16[4,6,16,1024]{3,2,1,0:T(8,128)(2,1)}), bf16[4,6,16,1024]{3,2,1,0:T(8,128)(2,1)}, u32[]{:S(2)}, u32[]{:S(2)}) %all-to-all-start.24) | async-done | bytes 786464 | tf_op jit(solution)/shard_map/cond/branch_5_fun/cond/branch_1_fun/all_to_all | solution.py:359
  278.4 0.6 broadcast_in_dim.183
  279.1 4.0 %all-to-all-start.38 = ((f32[16,1,384]{2,1,0:T(1,128)}), f32[16,1,384]{2,1,0:T(1,128)S(1)}, u32[]{:S(2)}, u32[]{:S(2)}) async-start(f32[16,1,384]{2,1,0:T(1,128)} %broadcast_in_dim.183), calls=%async_computation.38 | async-start | bytes 49152 | tf_op jit(solution)/shard_map/cond/branch_5_fun/all_to_all | solution.py:412
  283.1 8.7 %all-to-all-done.38 = f32[16,1,384]{2,1,0:T(1,128)S(1)} async-done(((f32[16,1,384]{2,1,0:T(1,128)}), f32[16,1,384]{2,1,0:T(1,128)S(1)}, u32[]{:S(2)}, u32[]{:S(2)}) %all-to-all-start.38) | async-done | bytes 24608 | tf_op jit(solution)/shard_map/cond/branch_5_fun/all_to_all | solution.py:412
  291.8 0.1 copy.90
  291.9 0.0 collective-permute-done.23
  291.9 1.5 gather_fusion.33
  293.4 3.5 %all-to-all-start.39 = ((bf16[4,6,16,1024]{3,2,1,0:T(8,128)(2,1)}), bf16[4,6,16,1024]{3,2,1,0:T(8,128)(2,1)S(1)}, u32[]{:S(2)}, u32[]{:S(2)}) async-start(bf16[4,6,16,1024]{3,2,1,0:T(8,128)(2,1)} %bitcast.86), calls=%async_computation.39 | async-start | bytes 1572864 | tf_op jit(solution)/shard_map/cond/branch_5_fun/all_to_all | solution.py:359
  296.9 3.5 %place.24.base_ref = bf16[6,256,2048]{2,1,0:T(8,128)(2,1)} custom-call(s32[1]{0:T(128)} %bitcast.79.filled_ref, s32[1]{0:T(128)} %bitcast.80.quarter_ref, bf16[4,6,16,1024]{3,2,1,0:T(8,128)(2,1)} %get-tuple-element.710.in_ref, bf16[6,256,2048]{2,1,0:T(8,128)(2,1)} %get-tuple-element.711.base_ref), custom_call_target="tpu_custom_call", output_to_operand_aliasing={{}: (3, {})} | custom-call | tf_op jit(solution)/shard_map/cond/branch_5_fun/place/pallas_call | solution.py:299
  300.4 0.2 copy.91
  300.6 0.8 reshape.283
  301.5 7.1 %all-to-all-done.39.in_ref = bf16[4,6,16,1024]{3,2,1,0:T(8,128)(2,1)S(1)} async-done(((bf16[4,6,16,1024]{3,2,1,0:T(8,128)(2,1)}), bf16[4,6,16,1024]{3,2,1,0:T(8,128)(2,1)S(1)}, u32[]{:S(2)}, u32[]{:S(2)}) %all-to-all-start.39) | async-done | bytes 786464 | tf_op jit(solution)/shard_map/cond/branch_5_fun/all_to_all | solution.py:359
  308.6 2.2 place.25
  (15 shorter events, 0.1 us)
Async XLA Ops:
  10.9 7.6 %copy-start.13 = (s32[48,1]{0,1:T(1,128)S(1)}, s32[48,1]{0,1:T(1,128)}, u32[]{:S(2)}) copy-start(s32[48,1]{0,1:T(1,128)} %param.85) | copy-start | bytes 580
  10.9 121.8 %copy-start.14 = (s32[8,2]{0,1:T(2,128)S(1)}, s32[8,2]{0,1:T(2,128)}, u32[]{:S(2)}) copy-start(s32[8,2]{0,1:T(2,128)} %param.82) | copy-start | bytes 196
  10.9 121.8 %copy-start.15 = (s32[16]{0:T(128)S(1)}, s32[16]{0:T(128)}, u32[]{:S(2)}) copy-start(s32[16]{0:T(128)} %param.83) | copy-start | bytes 196
  10.9 121.8 %all-to-all-start.42 = ((bf16[16,2,48,2048]{3,2,1,0:T(8,128)(2,1)}), bf16[16,2,48,2048]{3,2,1,0:T(8,128)(2,1)}, u32[]{:S(2)}, u32[]{:S(2)}) async-start(bf16[16,2,48,2048]{3,2,1,0:T(8,128)(2,1)} %prepare.1), calls=%async_computation.42 | async-start | bytes 12582912 | tf_op jit(solution)/shard_map/all_to_all | solution.py:353
  20.0 3.6 %collective-permute-start.28 = (s32[]{:T(128)}, s32[]{:T(128)}, u32[]{:S(2)}, u32[]{:S(2)}) collective-permute-start(s32[]{:T(128)} %add.321), channel_id=1, source_target_pairs={{0,16},{16,0},{1,17},{17,1},{2,18},{18,2},{3,19},{19,3},{4,20},{20... | collective-permute-start | bytes 20 | tf_op jit(solution)/shard_map/ppermute | solution.py:344
  142.9 51.7 %collective-permute-start.20 = (bf16[20,16,2048]{2,1,0:T(8,128)(2,1)}, bf16[20,16,2048]{2,1,0:T(8,128)(2,1)S(1)}, u32[]{:S(2)}, u32[]{:S(2)}) collective-permute-start(bf16[20,16,2048]{2,1,0:T(8,128)(2,1)} %get-tuple-element.692), channel_id=1, source_target_pairs={{0,4},{1,5},{2,6},{3,7},{4,8},{5,9},{6,10},{7,11},{8,12},{9,13},{1... | collective-permute-start | bytes 3932168 | tf_op jit(solution)/shard_map/cond/branch_5_fun/ppermute | solution.py:372
  194.6 32.5 %collective-permute-start.21 = (bf16[20,16,2048]{2,1,0:T(8,128)(2,1)}, bf16[20,16,2048]{2,1,0:T(8,128)(2,1)}, u32[]{:S(2)}, u32[]{:S(2)}) collective-permute-start(bf16[20,16,2048]{2,1,0:T(8,128)(2,1)} %get-tuple-element.696), channel_id=1, source_target_pairs={{0,12},{1,13},{2,14},{3,15},{4,0},{5,1},{6,2},{7,3},{8,4},{9,5},{1... | collective-permute-start | bytes 3932168 | tf_op jit(solution)/shard_map/cond/branch_5_fun/ppermute | solution.py:372
  199.6 1.1 copy-start.5
  227.0 30.5 %collective-permute-start.22 = (bf16[20,16,1024]{2,1,0:T(8,128)(2,1)}, bf16[20,16,1024]{2,1,0:T(8,128)(2,1)}, u32[]{:S(2)}, u32[]{:S(2)}) collective-permute-start(bf16[20,16,1024]{2,1,0:T(8,128)(2,1)} %get-tuple-element.699), channel_id=1, source_target_pairs={{0,8},{1,9},{2,10},{3,11},{4,12},{5,13},{6,14},{7,15},{8,0},{9,1},... | collective-permute-start | bytes 1966088 | tf_op jit(solution)/shard_map/cond/branch_5_fun/ppermute | solution.py:372
  229.5 28.7 %copy-start.11 = (f32[8,48,1]{2,1,0:T(8,128)S(1)}, f32[8,48,1]{2,1,0:T(8,128)}, u32[]{:S(2)}) copy-start(f32[8,48,1]{2,1,0:T(8,128)} %get-tuple-element.702) | copy-start | bytes 4612 | tf_op jit(solution)/shard_map/cond
  257.6 34.4 %collective-permute-start.23 = (bf16[20,16,1024]{2,1,0:T(8,128)(2,1)}, bf16[20,16,1024]{2,1,0:T(8,128)(2,1)S(1)}, u32[]{:S(2)}, u32[]{:S(2)}) collective-permute-start(bf16[20,16,1024]{2,1,0:T(8,128)(2,1)} %get-tuple-element.701), channel_id=1, source_target_pairs={{0,8},{1,9},{2,10},{3,11},{4,12},{5,13},{6,14},{7,15},{8,0},{9,1},... | collective-permute-start | bytes 1966088 | tf_op jit(solution)/shard_map/cond/branch_5_fun/ppermute | solution.py:372
  258.5 7.6 %copy-start.21 = (s32[3]{0:T(128)S(1)}, s32[3]{0:T(128)}, u32[]{:S(2)}) copy-start(s32[3]{0:T(128)} %constant.414) | copy-start | bytes 40 | tf_op jit(solution)/shard_map/cond/branch_5_fun/cond
  261.2 17.2 %all-to-all-start.24 = ((bf16[4,6,16,1024]{3,2,1,0:T(8,128)(2,1)}), bf16[4,6,16,1024]{3,2,1,0:T(8,128)(2,1)}, u32[]{:S(2)}, u32[]{:S(2)}) async-start(bf16[4,6,16,1024]{3,2,1,0:T(8,128)(2,1)} %bitcast.78), calls=%async_computation.24 | async-start | bytes 1572864 | tf_op jit(solution)/shard_map/cond/branch_5_fun/cond/branch_1_fun/all_to_all | solution.py:359
  279.1 12.7 %all-to-all-start.38 = ((f32[16,1,384]{2,1,0:T(1,128)}), f32[16,1,384]{2,1,0:T(1,128)S(1)}, u32[]{:S(2)}, u32[]{:S(2)}) async-start(f32[16,1,384]{2,1,0:T(1,128)} %broadcast_in_dim.183), calls=%async_computation.38 | async-start | bytes 49152 | tf_op jit(solution)/shard_map/cond/branch_5_fun/all_to_all | solution.py:412
  293.4 15.1 %all-to-all-start.39 = ((bf16[4,6,16,1024]{3,2,1,0:T(8,128)(2,1)}), bf16[4,6,16,1024]{3,2,1,0:T(8,128)(2,1)S(1)}, u32[]{:S(2)}, u32[]{:S(2)}) async-start(bf16[4,6,16,1024]{3,2,1,0:T(8,128)(2,1)} %bitcast.86), calls=%async_computation.39 | async-start | bytes 1572864 | tf_op jit(solution)/shard_map/cond/branch_5_fun/all_to_all | solution.py:359

commit v8 on v7

--- a/solution.py
+++ b/solution.py
@@ -175,9 +175,7 @@
             woven[block, pl.ds(2 * first + 1, group, stride=2), :] = (
                 left_weight * left_up + right_weight * right_up
             )
-    slot = lax.rem(pair, 2)
-
-    def each_copy(which_pair, which_slot, act):
+    def each_copy(which_pair, act):
         for piece in range(pieces):
             index = which_pair * pieces + piece
             for where, parts in enumerate(targets):
@@ -187,26 +185,23 @@
                     for part, (out_ref, begin) in enumerate(parts):
                         act(
                             pltpu.make_async_copy(
-                                ready.at[which_slot, piece, :, pl.ds(begin, out_ref.shape[-1])],
+                                ready.at[which_pair, piece, :, pl.ds(begin, out_ref.shape[-1])],
                                 out_ref.at[place_ref[index]],
-                                sems.at[which_slot, piece, part],
+                                sems.at[which_pair, piece, part],
                             )
                         )
 
-    @pl.when(pair >= 2)
-    def _():
-        each_copy(pair - 2, slot, lambda copy: copy.wait())
-
     for block in range(depth // LANES):
-        ready[slot, :, :, block * LANES : (block + 1) * LANES] = (
+        ready[pair, :, :, block * LANES : (block + 1) * LANES] = (
             woven[block].reshape(pieces, piece_rows, LANES).astype(jnp.bfloat16)
         )
-    each_copy(pair, slot, lambda copy: copy.start())
+    each_copy(pair, lambda copy: copy.start())
 
     @pl.when(pair == pair_count - 1)
     def _():
-        each_copy(pair - 1, 1 - slot, lambda copy: copy.wait())
-        each_copy(pair, slot, lambda copy: copy.wait())
+        @pl.loop(0, ready.shape[0])
+        def _(which_pair):
+            each_copy(which_pair, lambda copy: copy.wait())
 
 
 def merge(pairs, counts, where, places, rows, slots, listed):
@@ -224,9 +219,9 @@
         scratch_shapes=[
             pltpu.VMEM((pair_count, 2, 2, per_device, depth), jnp.bfloat16),
             pltpu.VMEM((depth // LANES, 2 * per_device, LANES), jnp.float32),
-            pltpu.VMEM((2, pieces, piece_rows, depth), jnp.bfloat16),
+            pltpu.VMEM((pair_count, pieces, piece_rows, depth), jnp.bfloat16),
             pltpu.SemaphoreType.DMA((pair_count, 2, 2)),
-            pltpu.SemaphoreType.DMA((2, pieces, 2)),
+            pltpu.SemaphoreType.DMA((pair_count, pieces, 2)),
         ],
     )
     return pl.pallas_call(
@@ -385,6 +380,17 @@
         def spread_and_place(chunk, from_list, filled, quarters, *arrived):
             return spread(chunk, from_list), place_three(filled, quarters, arrived)
 
+        def spread_and_place_part(chunk, from_list, filled, quarter, arrived, merged):
+            return spread(chunk, from_list), place(filled, quarter, arrived, 0, merged)
+
+        similarity = lax.all_to_all(
+            jnp.broadcast_to(similarity_part.reshape(1, -1), (devices, similarity_part.size)),
+            "expert",
+            0,
+            0,
+            tiled=True,
+        )
+        next_list, slots, similarity = in_order(next_list, slots, similarity)
         one_on = permuted(next_list, 1)
         own = unless_empty(within_quarter, slots)
         one_on, own = in_order(one_on, own)
@@ -408,13 +414,9 @@
             from_one,
             from_three,
         )
-        part, from_two = in_order(similarity_part.reshape(1, -1), from_two)
-        similarity = lax.all_to_all(
-            jnp.broadcast_to(part, (devices, part.shape[1])), "expert", 0, 0, tiled=True
-        )
-        rest_on, similarity = in_order(rest_on, similarity)
-        from_rest = spread(rest_on, from_list)
-        merged = place(filled, origins[2:3], from_two, 0, merged)
+        from_rest, merged = unless_empty(
+            spread_and_place_part, rest_on, from_list, filled, origins[2:3], from_two, merged
+        )
         merged = place(filled, origins[2:3], from_rest, 1, merged)
         similarity = similarity.reshape(devices, pair_count, pieces, share_units)
         similarity = similarity.transpose(1, 2, 0, 3).reshape(pair_count, units)

time: 306 us -> 324 us (1.059); the launches traced: 311 us -> 321 us
  starting transfers between devices: 53.8 us -> 19.3 us
  blocking collectives: 71 us -> 105 us
  loops' own time: 0.42 us -> 8.88 us
    all_to_all x0 -> x1, blocking collectives: none -> 34.4 us  [deal(): lax.all_to_all(jnp.broadcast_to(similarity_part.reshape(1, -1), (devices,...]
    ppermute x4, starting transfers between devices: 30.9 us -> 0.46 us  [permuted(): return lax.ppermute(chunk, 'expert', ring)]
    ppermute x4, waiting for transfers between devices: 7.62 us -> 16.7 us  [permuted(): return lax.ppermute(chunk, 'expert', ring)]
    all_to_all x1 -> x0, waiting for transfers between devices: 8.67 us -> none  [deal(): lax.all_to_all(jnp.broadcast_to(part, (devices, part.shape[1])), 'expert'...]
    another operation x1, loops' own time: 0.35 us -> 8.78 us  [body(): lax.switch(level, [functools.partial(deal, length) for length in lengths]...]
    all_to_all x1 -> x0, starting transfers between devices: 4.02 us -> none  [deal(): lax.all_to_all(jnp.broadcast_to(part, (devices, part.shape[1])), 'expert'...]
  transfers between devices with their start and end apart: 9 -> 8, of which waited for: 8 -> 8; matrix products, arithmetic and copies ran while one was open for 4% -> 3% of each run, Pallas kernels for 3% -> 3%
where the time goes in v8:
time: 324 us; the launch traced here: 321 us
  waiting for transfers between devices  139 us (43%)
  blocking collectives  105 us (32%)
  Pallas kernels  32.8 us (10%)
  starting transfers between devices  19.3 us (6%)
  local copies, waits for them, and re-layouts  10.8 us (3%)
  loops' own time  8.88 us (3%)
  other arithmetic  3.48 us (1%)
    all_to_all x1, waiting for transfers between devices, body(): lax.all_to_all(outgoing, 'expert', split_axis=0, concat_axis=0, tiled=True)  108 us
    all_to_all x3, blocking collectives, within_quarter(): lax.all_to_all(value, 'expert', split_axis=0, concat_axis=0, tiled=True,...  70.2 us
    all_to_all x1, blocking collectives, deal(): lax.all_to_all(jnp.broadcast_to(similarity_part.reshape(1, -1), (devices,...  34.4 us
    ppermute x4, waiting for transfers between devices, permuted(): return lax.ppermute(chunk, 'expert', ring)  16.7 us
    all_to_all x2, waiting for transfers between devices, within_quarter(): lax.all_to_all(value, 'expert', split_axis=0, concat_axis=0, tiled=True,...  13 us
    pallas_call x1, Pallas kernels, prepare(): pl.pallas_call(prepare_kernel, grid_spec=grid_spec, out_shape=jax.ShapeDt...  10.3 us
    pallas_call x1, Pallas kernels, merge(): pl.pallas_call(merge_kernel, grid_spec=grid_spec, out_shape=[jax.ShapeDty...  9.28 us
    another operation x1, loops' own time, body(): lax.switch(level, [functools.partial(deal, length) for length in lengths]...  8.78 us
  transfers between devices with their start and end apart: 8, of which 8 were waited for; matrix products, arithmetic and copies ran while one was open for 3% of the time, Pallas kernels for 3%

profile of v8, /device:TPU:0, one launch (start us, length us, event | category | flops | bytes accessed | tf_op | source)
XLA Modules:
  0.0 320.7 jit_solution(3774798158735099080)
XLA Ops:
  0.6 10.3 %prepare.1 = bf16[16,2,48,2048]{3,2,1,0:T(8,128)(2,1)} custom-call(s32[2,8]{1,0:T(2,128)} %bitcast.181, s32[1]{0:T(128)} %bitcast.108.me_ref, s32[8,768]{1,0:T(8,128)} %order_ref.1, bf16[2048,768]{1,0:T(8,128)(2,1)} %bitcast.151, bf16[2048,768]{1,0:T(8,128)(2,1)} %bitcast.152, bf16[6,16]{1,0:T(8,128)(2,1)} %bitcast.189, bf16[6,16]{1,0:T(8,128)(2,1)} %bitcast.190), custom_call_target="tpu_custom_call" | custom-call | tf_op jit(solution)/shard_map/prepare/pallas_call | solution.py:94
  10.9 0.0 copy-start.6
  10.9 0.0 copy-start.7
  10.9 0.0 copy-start.8
  10.9 7.5 %all-to-all-start.42 = ((bf16[16,2,48,2048]{3,2,1,0:T(8,128)(2,1)}), bf16[16,2,48,2048]{3,2,1,0:T(8,128)(2,1)}, u32[]{:S(2)}, u32[]{:S(2)}) async-start(bf16[16,2,48,2048]{3,2,1,0:T(8,128)(2,1)} %prepare.1), calls=%async_computation.42 | async-start | bytes 12582912 | tf_op jit(solution)/shard_map/all_to_all | solution.py:348
  18.5 0.0 copy-done.6
  18.6 0.2 select_reduce_fusion.14
  18.7 0.6 reduce_max.9
  20.0 2.9 collective-permute-start.28
  22.9 0.7 collective-permute-done.28
  24.3 108.4 %all-to-all-done.42 = bf16[16,2,48,2048]{3,2,1,0:T(8,128)(2,1)} async-done(((bf16[16,2,48,2048]{3,2,1,0:T(8,128)(2,1)}), bf16[16,2,48,2048]{3,2,1,0:T(8,128)(2,1)}, u32[]{:S(2)}, u32[]{:S(2)}) %all-to-all-start.42) | async-done | bytes 6291488 | tf_op jit(solution)/shard_map/all_to_all | solution.py:348
  132.7 0.0 copy-done.7
  132.7 0.0 copy-done.8
  132.7 188.0 %conditional.36 = (bf16[6,256,2048]{2,1,0:T(8,128)(2,1)}, f32[8,768]{1,0:T(8,128)}) conditional(s32[]{:T(128)} %clamp.3, (s32[]{:T(128)}, s32[]{:T(128)}, s32[8,2]{0,1:T(2,128)S(1)}, s32[16]{0:T(128)S(1)}, s32[48]{0:T(128)S(1)}, /*index=5*/s32[48]{0:T(128)S(1)}, bf16[16,2,48,2048]{3,2,1,0:T(8,128)(2,1)}, ...), branch_computations={%region_5.16_spmd, %region_16.27_spmd, %region_27.38_spmd, %region... | conditional | flops 19365 | bytes 51123004 | solution.py:425
  141.5 0.2 select_reduce_fusion.8
  141.7 0.5 fusion.13
  142.2 9.3 %merge.11 = (f32[8,48,1]{2,1,0:T(8,128)}, bf16[24,16,2048]{2,1,0:T(8,128)(2,1)}, bf16[18,16,2048]{2,1,0:T(8,128)(2,1)}, bf16[18,16,1024]{2,1,0:T(8,128)(2,1)}, b...) custom-call(s32[2,8]{1,0:T(2,128)S(1)} %bitcast.186, s32[16]{0:T(128)S(1)} %get-tuple-element.967.counts_ref, ...), custom_call_target="tpu_custom_call" | custom-call | tf_op jit(solution)/shard_map/cond/branch_4_fun/merge/pallas_call | solution.py:227
  151.5 1.0 reduce.4
  152.5 0.1 broadcast_in_dim.189
  152.6 34.4 %all_to_all.213 = f32[16,1,384]{2,1,0:T(1,128)S(1)} all-to-all(f32[16,1,384]{2,1,0:T(1,128)S(1)} %broadcast_in_dim.190), channel_id=1, replica_groups=mesh['layers'=2,'expert'=16] {'expert'}, dimensions={0} | all-to-all | bytes 49152 | tf_op jit(solution)/shard_map/cond/branch_4_fun/all_to_all | solution.py:386
  187.0 0.1 copy.88
  187.2 0.5 collective-permute-start.16
  187.6 23.6 %conditional.20 = (bf16[4,6,16,2048]{3,2,1,0:T(8,128)(2,1)S(1)}) conditional(s32[]{:T(128)} %convert_element_type.28, () %tuple.257, bf16[24,16,2048]{2,1,0:T(8,128)(2,1)} %get-tuple-element.773), branch_computations={%region_50.50_spmd, %region_51.51_spmd} | conditional | bytes 3145736 | solution.py:375
  187.6 23.6 %all_to_all.210 = bf16[4,6,16,2048]{3,2,1,0:T(8,128)(2,1)S(1)} all-to-all(bf16[4,6,16,2048]{3,2,1,0:T(8,128)(2,1)} %bitcast.157), channel_id=1, replica_groups={{0,1,2,3},{4,5,6,7},{8,9,10,11},{12,13,14,15},{16,17,18,19},{20,21,22,2..., dimensions={0} | all-to-all | bytes 3145728 | tf_op jit(solution)/shard_map/cond/branch_4_fun/cond/branch_1_fun/all_to_all | solution.py:354
  211.2 5.6 %collective-permute-done.16 = bf16[18,16,2048]{2,1,0:T(8,128)(2,1)S(1)} collective-permute-done((bf16[18,16,2048]{2,1,0:T(8,128)(2,1)}, bf16[18,16,2048]{2,1,0:T(8,128)(2,1)S(1)}, u32[]{:S(2)}, u32[]{:S(2)}) %collective-permute-start.16) | collective-permute-done | bytes 1179680 | tf_op jit(solution)/shard_map/cond/branch_4_fun/ppermute | solution.py:367
  216.8 0.0 collective-permute-start.17
  216.8 0.1 select_reduce_fusion.9
  217.0 26.2 %conditional.21 = (bf16[4,6,16,2048]{3,2,1,0:T(8,128)(2,1)}) conditional(s32[]{:T(128)} %convert_element_type.28, () %tuple.260, (s32[24]{0:T(128)S(1)}, bf16[18,16,2048]{2,1,0:T(8,128)(2,1)S(1)}) %tuple.261), branch_computations={%region_52.52_spmd, %region_53.53_spmd} | conditional | flops 1024 | bytes 11014372 | solution.py:375
  217.0 0.0 copy-start.4
  217.0 1.0 copy-done.4
  218.0 1.9 gather_fusion.20
  219.9 23.3 %all_to_all.211 = bf16[4,6,16,2048]{3,2,1,0:T(8,128)(2,1)} all-to-all(bf16[4,6,16,2048]{3,2,1,0:T(8,128)(2,1)S(1)} %bitcast.145), channel_id=1, replica_groups={{0,1,2,3},{4,5,6,7},{8,9,10,11},{12,13,14,15},{16,17,18,19},{20,21,22,2..., dimensions={0} | all-to-all | bytes 3145728 | tf_op jit(solution)/shard_map/cond/branch_4_fun/cond/branch_1_fun/all_to_all | solution.py:354
  243.2 0.7 collective-permute-done.17
  243.9 0.0 collective-permute-start.18
  243.9 25.3 %conditional.22 = (bf16[4,6,16,2048]{3,2,1,0:T(8,128)(2,1)}) conditional(s32[]{:T(128)} %convert_element_type.28, () %tuple.264, (s32[24]{0:T(128)S(1)}, bf16[18,16,2048]{2,1,0:T(8,128)(2,1)}) %tuple.265), branch_computations={%region_54.54_spmd, %region_55.55_spmd} | conditional | flops 1024 | bytes 6295752 | solution.py:375
  243.9 1.9 gather_fusion.21
  245.8 23.3 %all_to_all.212 = bf16[4,6,16,2048]{3,2,1,0:T(8,128)(2,1)} all-to-all(bf16[4,6,16,2048]{3,2,1,0:T(8,128)(2,1)S(1)} %bitcast.146), channel_id=1, replica_groups={{0,1,2,3},{4,5,6,7},{8,9,10,11},{12,13,14,15},{16,17,18,19},{20,21,22,2..., dimensions={0} | all-to-all | bytes 3145728 | tf_op jit(solution)/shard_map/cond/branch_4_fun/cond/branch_1_fun/all_to_all | solution.py:354
  269.1 2.9 collective-permute-done.18
  272.0 0.0 collective-permute-start.19
  272.0 0.6 reduce_sum.51
  272.7 0.1 pad_add_fusion.4
  272.8 0.2 copy.89
  272.9 0.8 reshape.277
  273.8 18.5 %conditional.23 = (bf16[4,6,16,1024]{3,2,1,0:T(8,128)(2,1)}, bf16[6,256,2048]{2,1,0:T(8,128)(2,1)}) conditional(s32[]{:T(128)} %convert_element_type.28, () %tuple.268, (s32[24]{0:T(128)S(1)}, bf16[18,16,1024]{2,1,0:T(8,128)(2,1)}, (), s32[4]{0:T(128)S(1)}, s32[1]{0:T(128)}, /*index=5*/bf16[4,6,16,2048]{3,2,1,0:T(8,128)(2,1)S(1)}, ...), branch_computations={%region_56.56_spmd, %region_57.57_spmd} | conditional | flops 2048 | bytes 7077908 | solution.py:375
  273.8 0.0 copy-start.13
  273.8 2.6 gather_fusion.22
  276.4 4.2 %all-to-all-start.25 = ((bf16[4,6,16,1024]{3,2,1,0:T(8,128)(2,1)}), bf16[4,6,16,1024]{3,2,1,0:T(8,128)(2,1)}, u32[]{:S(2)}, u32[]{:S(2)}) async-start(bf16[4,6,16,1024]{3,2,1,0:T(8,128)(2,1)} %bitcast.63), calls=%async_computation.25 | async-start | bytes 1572864 | tf_op jit(solution)/shard_map/cond/branch_4_fun/cond/branch_1_fun/all_to_all | solution.py:354
  280.6 0.0 copy-done.13
  280.6 0.6 gather_fusion.23
  281.2 6.2 %place_three.11 = bf16[6,256,2048]{2,1,0:T(8,128)(2,1)} custom-call(s32[1]{0:T(128)} %get-tuple-element.745.filled_ref, s32[3]{0:T(128)S(1)} %gather_fusion.23, bf16[4,6,16,2048]{3,2,1,0:T(8,128)(2,1)S(1)} %get-tuple-element.748.refs_0_, bf16[4,6,16,2048]{3,2,1,0:T(8,128)(2,1)} %get-tuple-element.749.refs_1_, bf16[4,6,16,2048]{3,2,1,0:T(8,128)(2,1)} %get-tuple-element.750.refs_2_), custom_call_target="tpu_custom_call" | custom-call | tf_op jit(solution)/shard_map/cond/branch_4_fun/cond/branch_1_fun/place_three/pallas_call | solution.py:263
  287.4 4.9 %all-to-all-done.25 = bf16[4,6,16,1024]{3,2,1,0:T(8,128)(2,1)} async-done(((bf16[4,6,16,1024]{3,2,1,0:T(8,128)(2,1)}), bf16[4,6,16,1024]{3,2,1,0:T(8,128)(2,1)}, u32[]{:S(2)}, u32[]{:S(2)}) %all-to-all-start.25) | async-done | bytes 786464 | tf_op jit(solution)/shard_map/cond/branch_4_fun/cond/branch_1_fun/all_to_all | solution.py:354
  292.3 7.5 %collective-permute-done.19 = bf16[18,16,1024]{2,1,0:T(8,128)(2,1)S(1)} collective-permute-done((bf16[18,16,1024]{2,1,0:T(8,128)(2,1)}, bf16[18,16,1024]{2,1,0:T(8,128)(2,1)S(1)}, u32[]{:S(2)}, u32[]{:S(2)}) %collective-permute-start.19) | collective-permute-done | bytes 589856 | tf_op jit(solution)/shard_map/cond/branch_4_fun/ppermute | solution.py:367
  299.7 17.5 %conditional.24 = (bf16[4,6,16,1024]{3,2,1,0:T(8,128)(2,1)}, bf16[6,256,2048]{2,1,0:T(8,128)(2,1)}) conditional(s32[]{:T(128)} %convert_element_type.28, () %tuple.255, (s32[24]{0:T(128)S(1)}, bf16[18,16,1024]{2,1,0:T(8,128)(2,1)S(1)}, s32[1]{0:T(128)}, s32[1]{0:T(128)}, bf16[4,6,16,1024]{3,2,1,0:T(8,128)(2,1)}, ...), branch_computations={%region_58.58_spmd, %region_59.59_spmd} | conditional | flops 1024 | bytes 7077908 | solution.py:375
  299.8 1.5 gather_fusion.24
  301.3 4.2 %all-to-all-start.26 = ((bf16[4,6,16,1024]{3,2,1,0:T(8,128)(2,1)}), bf16[4,6,16,1024]{3,2,1,0:T(8,128)(2,1)}, u32[]{:S(2)}, u32[]{:S(2)}) async-start(bf16[4,6,16,1024]{3,2,1,0:T(8,128)(2,1)} %bitcast.64), calls=%async_computation.26 | async-start | bytes 1572864 | tf_op jit(solution)/shard_map/cond/branch_4_fun/cond/branch_1_fun/all_to_all | solution.py:354
  305.5 3.5 %place.22 = bf16[6,256,2048]{2,1,0:T(8,128)(2,1)} custom-call(s32[1]{0:T(128)} %get-tuple-element.753.filled_ref, s32[1]{0:T(128)} %get-tuple-element.754.quarter_ref, bf16[4,6,16,1024]{3,2,1,0:T(8,128)(2,1)} %get-tuple-element.755.in_ref, bf16[6,256,2048]{2,1,0:T(8,128)(2,1)} %get-tuple-element.756.base_ref), custom_call_target="tpu_custom_call", output_to_operand_aliasing={{}: (3, {})} | custom-call | tf_op jit(solution)/shard_map/cond/branch_4_fun/cond/branch_1_fun/place/pallas_call | solution.py:294
  309.0 8.2 %all-to-all-done.26 = bf16[4,6,16,1024]{3,2,1,0:T(8,128)(2,1)} async-done(((bf16[4,6,16,1024]{3,2,1,0:T(8,128)(2,1)}), bf16[4,6,16,1024]{3,2,1,0:T(8,128)(2,1)}, u32[]{:S(2)}, u32[]{:S(2)}) %all-to-all-start.26) | async-done | bytes 786464 | tf_op jit(solution)/shard_map/cond/branch_4_fun/cond/branch_1_fun/all_to_all | solution.py:354
  317.2 3.5 %place.23 = bf16[6,256,2048]{2,1,0:T(8,128)(2,1)} custom-call(s32[1]{0:T(128)} %bitcast.65.filled_ref, s32[1]{0:T(128)} %bitcast.66.quarter_ref, bf16[4,6,16,1024]{3,2,1,0:T(8,128)(2,1)} %get-tuple-element.786.in_ref, bf16[6,256,2048]{2,1,0:T(8,128)(2,1)} %get-tuple-element.787.base_ref), custom_call_target="tpu_custom_call", output_to_operand_aliasing={{}: (3, {})} | custom-call | tf_op jit(solution)/shard_map/cond/branch_4_fun/place/pallas_call | solution.py:294
  (15 shorter events, 0.1 us)
Async XLA Ops:
  10.9 7.6 %copy-start.6 = (s32[48,1]{0,1:T(1,128)S(1)}, s32[48,1]{0,1:T(1,128)}, u32[]{:S(2)}) copy-start(s32[48,1]{0,1:T(1,128)} %param.99) | copy-start | bytes 580
  10.9 121.8 %copy-start.7 = (s32[8,2]{0,1:T(2,128)S(1)}, s32[8,2]{0,1:T(2,128)}, u32[]{:S(2)}) copy-start(s32[8,2]{0,1:T(2,128)} %param.96) | copy-start | bytes 196
  10.9 121.8 %copy-start.8 = (s32[16]{0:T(128)S(1)}, s32[16]{0:T(128)}, u32[]{:S(2)}) copy-start(s32[16]{0:T(128)} %param.97) | copy-start | bytes 196
  10.9 121.7 %all-to-all-start.42 = ((bf16[16,2,48,2048]{3,2,1,0:T(8,128)(2,1)}), bf16[16,2,48,2048]{3,2,1,0:T(8,128)(2,1)}, u32[]{:S(2)}, u32[]{:S(2)}) async-start(bf16[16,2,48,2048]{3,2,1,0:T(8,128)(2,1)} %prepare.1), calls=%async_computation.42 | async-start | bytes 12582912 | tf_op jit(solution)/shard_map/all_to_all | solution.py:348
  20.0 3.6 %collective-permute-start.28 = (s32[]{:T(128)}, s32[]{:T(128)}, u32[]{:S(2)}, u32[]{:S(2)}) collective-permute-start(s32[]{:T(128)} %add.321), channel_id=1, source_target_pairs={{0,16},{16,0},{1,17},{17,1},{2,18},{18,2},{3,19},{19,3},{4,20},{20... | collective-permute-start | bytes 20 | tf_op jit(solution)/shard_map/ppermute | solution.py:339
  187.2 29.7 %collective-permute-start.16 = (bf16[18,16,2048]{2,1,0:T(8,128)(2,1)}, bf16[18,16,2048]{2,1,0:T(8,128)(2,1)S(1)}, u32[]{:S(2)}, u32[]{:S(2)}) collective-permute-start(bf16[18,16,2048]{2,1,0:T(8,128)(2,1)} %get-tuple-element.772), channel_id=1, source_target_pairs={{0,4},{1,5},{2,6},{3,7},{4,8},{5,9},{6,10},{7,11},{8,12},{9,13},{1... | collective-permute-start | bytes 3538952 | tf_op jit(solution)/shard_map/cond/branch_4_fun/ppermute | solution.py:367
  216.8 27.0 %collective-permute-start.17 = (bf16[18,16,2048]{2,1,0:T(8,128)(2,1)}, bf16[18,16,2048]{2,1,0:T(8,128)(2,1)}, u32[]{:S(2)}, u32[]{:S(2)}) collective-permute-start(bf16[18,16,2048]{2,1,0:T(8,128)(2,1)} %get-tuple-element.775), channel_id=1, source_target_pairs={{0,12},{1,13},{2,14},{3,15},{4,0},{5,1},{6,2},{7,3},{8,4},{9,5},{1... | collective-permute-start | bytes 3538952 | tf_op jit(solution)/shard_map/cond/branch_4_fun/ppermute | solution.py:367
  217.0 1.0 copy-start.4
  243.9 28.2 %collective-permute-start.18 = (bf16[18,16,1024]{2,1,0:T(8,128)(2,1)}, bf16[18,16,1024]{2,1,0:T(8,128)(2,1)}, u32[]{:S(2)}, u32[]{:S(2)}) collective-permute-start(bf16[18,16,1024]{2,1,0:T(8,128)(2,1)} %get-tuple-element.777), channel_id=1, source_target_pairs={{0,8},{1,9},{2,10},{3,11},{4,12},{5,13},{6,14},{7,15},{8,0},{9,1},... | collective-permute-start | bytes 1769480 | tf_op jit(solution)/shard_map/cond/branch_4_fun/ppermute | solution.py:367
  272.0 27.7 %collective-permute-start.19 = (bf16[18,16,1024]{2,1,0:T(8,128)(2,1)}, bf16[18,16,1024]{2,1,0:T(8,128)(2,1)S(1)}, u32[]{:S(2)}, u32[]{:S(2)}) collective-permute-start(bf16[18,16,1024]{2,1,0:T(8,128)(2,1)} %get-tuple-element.779), channel_id=1, source_target_pairs={{0,8},{1,9},{2,10},{3,11},{4,12},{5,13},{6,14},{7,15},{8,0},{9,1},... | collective-permute-start | bytes 1769480 | tf_op jit(solution)/shard_map/cond/branch_4_fun/ppermute | solution.py:367
  273.8 6.8 %copy-start.13 = (s32[3]{0:T(128)S(1)}, s32[3]{0:T(128)}, u32[]{:S(2)}) copy-start(s32[3]{0:T(128)} %constant.438) | copy-start | bytes 40 | tf_op jit(solution)/shard_map/cond/branch_4_fun/cond
  276.4 15.9 %all-to-all-start.25 = ((bf16[4,6,16,1024]{3,2,1,0:T(8,128)(2,1)}), bf16[4,6,16,1024]{3,2,1,0:T(8,128)(2,1)}, u32[]{:S(2)}, u32[]{:S(2)}) async-start(bf16[4,6,16,1024]{3,2,1,0:T(8,128)(2,1)} %bitcast.63), calls=%async_computation.25 | async-start | bytes 1572864 | tf_op jit(solution)/shard_map/cond/branch_4_fun/cond/branch_1_fun/all_to_all | solution.py:354
  301.3 16.0 %all-to-all-start.26 = ((bf16[4,6,16,1024]{3,2,1,0:T(8,128)(2,1)}), bf16[4,6,16,1024]{3,2,1,0:T(8,128)(2,1)}, u32[]{:S(2)}, u32[]{:S(2)}) async-start(bf16[4,6,16,1024]{3,2,1,0:T(8,128)(2,1)} %bitcast.64), calls=%async_computation.26 | async-start | bytes 1572864 | tf_op jit(solution)/shard_map/cond/branch_4_fun/cond/branch_1_fun/all_to_all | solution.py:354

commit v9 on v7

--- a/solution.py
+++ b/solution.py
@@ -15,7 +15,7 @@
 EPSILON = 1e-06
 VMEM = 60 * 1024 * 1024
 QUARTERS = 4
-LIST_PARTS = (14, 15, 16, 17, 18, 20, 24)
+LIST_PARTS = (15, 16, 17, 18, 19, 20, 24)
 
 
 def prepare_kernel(

time: 306 us -> 298 us (0.974); the launches traced: 311 us -> 296 us
  waiting for transfers between devices: 138 us -> 128 us
  starting transfers between devices: 53.8 us -> 49.9 us
    ppermute x4, waiting for transfers between devices: 7.62 us -> 0.01 us  [permuted(): return lax.ppermute(chunk, 'expert', ring)]
  transfers between devices with their start and end apart: 9 -> 9, of which waited for: 8 -> 5; matrix products, arithmetic and copies ran while one was open for 4% -> 4% of each run, Pallas kernels for 3% -> 3%
where the time goes in v9:
time: 298 us; the launch traced here: 296 us
  waiting for transfers between devices  128 us (43%)
  blocking collectives  71 us (24%)
  starting transfers between devices  49.9 us (17%)
  Pallas kernels  31.4 us (11%)
  local copies, waits for them, and re-layouts  11.3 us (4%)
    all_to_all x1, waiting for transfers between devices, body(): lax.all_to_all(outgoing, 'expert', split_axis=0, concat_axis=0, tiled=True)  108 us
    all_to_all x3, blocking collectives, within_quarter(): lax.all_to_all(value, 'expert', split_axis=0, concat_axis=0, tiled=True,...  71 us
    ppermute x4, starting transfers between devices, permuted(): return lax.ppermute(chunk, 'expert', ring)  28 us
    all_to_all x2, waiting for transfers between devices, within_quarter(): lax.all_to_all(value, 'expert', split_axis=0, concat_axis=0, tiled=True,...  11.9 us
    pallas_call x1, Pallas kernels, prepare(): pl.pallas_call(prepare_kernel, grid_spec=grid_spec, out_shape=jax.ShapeDt...  10.3 us
    pallas_call x1, Pallas kernels, merge(): pl.pallas_call(merge_kernel, grid_spec=grid_spec, out_shape=[jax.ShapeDty...  9.19 us
    gather x4, local copies, waits for them, and re-layouts, spread(): return within_quarter(jnp.take(chunk, from_list, axis=0, mode='clip'))  7.81 us
    all_to_all x2, starting transfers between devices, within_quarter(): lax.all_to_all(value, 'expert', split_axis=0, concat_axis=0, tiled=True,...  7.68 us
  transfers between devices with their start and end apart: 9, of which 5 were waited for; matrix products, arithmetic and copies ran while one was open for 4% of the time, Pallas kernels for 3%

profile of v9, /device:TPU:0, one launch (start us, length us, event | category | flops | bytes accessed | tf_op | source)
XLA Modules:
  0.0 296.1 jit_solution(6660884691442562103)
XLA Ops:
  0.6 10.3 %prepare.1 = bf16[16,2,48,2048]{3,2,1,0:T(8,128)(2,1)} custom-call(s32[2,8]{1,0:T(2,128)} %bitcast.181, s32[1]{0:T(128)} %bitcast.108.me_ref, s32[8,768]{1,0:T(8,128)} %order_ref.1, bf16[2048,768]{1,0:T(8,128)(2,1)} %bitcast.151, bf16[2048,768]{1,0:T(8,128)(2,1)} %bitcast.152, bf16[6,16]{1,0:T(8,128)(2,1)} %bitcast.189, bf16[6,16]{1,0:T(8,128)(2,1)} %bitcast.190), custom_call_target="tpu_custom_call" | custom-call | tf_op jit(solution)/shard_map/prepare/pallas_call | solution.py:94
  10.9 0.0 copy-start.13
  10.9 0.0 copy-start.14
  10.9 0.0 copy-start.15
  10.9 7.5 %all-to-all-start.42 = ((bf16[16,2,48,2048]{3,2,1,0:T(8,128)(2,1)}), bf16[16,2,48,2048]{3,2,1,0:T(8,128)(2,1)}, u32[]{:S(2)}, u32[]{:S(2)}) async-start(bf16[16,2,48,2048]{3,2,1,0:T(8,128)(2,1)} %prepare.1), calls=%async_computation.42 | async-start | bytes 12582912 | tf_op jit(solution)/shard_map/all_to_all | solution.py:353
  18.5 0.0 copy-done.13
  18.6 0.2 select_reduce_fusion.14
  18.8 0.6 reduce_max.9
  20.0 2.9 collective-permute-start.28
  22.9 0.7 collective-permute-done.28
  24.2 108.5 %all-to-all-done.42 = bf16[16,2,48,2048]{3,2,1,0:T(8,128)(2,1)} async-done(((bf16[16,2,48,2048]{3,2,1,0:T(8,128)(2,1)}), bf16[16,2,48,2048]{3,2,1,0:T(8,128)(2,1)}, u32[]{:S(2)}, u32[]{:S(2)}) %all-to-all-start.42) | async-done | bytes 6291488 | tf_op jit(solution)/shard_map/all_to_all | solution.py:353
  132.7 0.0 copy-done.14
  132.7 0.0 copy-done.15
  132.7 163.2 %conditional.29 = (bf16[6,256,2048]{2,1,0:T(8,128)(2,1)}, f32[8,768]{1,0:T(8,128)}) conditional(s32[]{:T(128)} %clamp.3, (s32[]{:T(128)}, s32[8,2]{0,1:T(2,128)S(1)}, s32[16]{0:T(128)S(1)}, s32[48]{0:T(128)S(1)}, s32[48]{0:T(128)S(1)}, /*index=5*/bf16[16,2,48,2048]{3,2,1,0:T(8,128)(2,1)}, s32[]{:T(128)}, ...), branch_computations={%region_5.14_spmd, %region_14.23_spmd, %region_23.32_spmd, %region... | conditional | flops 19365 | bytes 48015384 | solution.py:423
  132.8 0.2 select_reduce_fusion
  132.9 0.5 fusion.9
  133.5 9.2 %merge.7 = (f32[8,48,1]{2,1,0:T(8,128)}, bf16[24,16,2048]{2,1,0:T(8,128)(2,1)}, bf16[15,16,2048]{2,1,0:T(8,128)(2,1)}, bf16[15,16,1024]{2,1,0:T(8,128)(2,1)}, bf...) custom-call(s32[2,8]{1,0:T(2,128)S(1)} %bitcast.182, s32[16]{0:T(128)S(1)} %get-tuple-element.830.counts_ref, ...), custom_call_target="tpu_custom_call" | custom-call | tf_op jit(solution)/shard_map/cond/branch_0_fun/merge/pallas_call | solution.py:232
  142.7 23.5 %collective-permute-start = (bf16[15,16,2048]{2,1,0:T(8,128)(2,1)}, bf16[15,16,2048]{2,1,0:T(8,128)(2,1)S(1)}, u32[]{:S(2)}, u32[]{:S(2)}) collective-permute-start(bf16[15,16,2048]{2,1,0:T(8,128)(2,1)} %get-tuple-element.477), channel_id=1, source_target_pairs={{0,4},{1,5},{2,6},{3,7},{4,8},{5,9},{6,10},{7,11},{8,12},{9,13},{1... | collective-permute-start | bytes 2949128 | tf_op jit(solution)/shard_map/cond/branch_0_fun/ppermute | solution.py:372
  166.2 24.4 %conditional = (bf16[4,6,16,2048]{3,2,1,0:T(8,128)(2,1)S(1)}) conditional(s32[]{:T(128)} %convert_element_type.6, () %tuple.141, bf16[24,16,2048]{2,1,0:T(8,128)(2,1)} %get-tuple-element.479), branch_computations={%region_6.6_spmd, %region_7.7_spmd} | conditional | bytes 3145736 | solution.py:380
  166.2 24.4 %all_to_all.194 = bf16[4,6,16,2048]{3,2,1,0:T(8,128)(2,1)S(1)} all-to-all(bf16[4,6,16,2048]{3,2,1,0:T(8,128)(2,1)} %bitcast.153), channel_id=1, replica_groups={{0,1,2,3},{4,5,6,7},{8,9,10,11},{12,13,14,15},{16,17,18,19},{20,21,22,2..., dimensions={0} | all-to-all | bytes 3145728 | tf_op jit(solution)/shard_map/cond/branch_0_fun/cond/branch_1_fun/all_to_all | solution.py:359
  190.6 0.0 collective-permute-done
  190.6 1.6 collective-permute-start.1
  192.2 0.1 select_reduce_fusion.1
  192.3 26.1 %conditional.1 = (bf16[4,6,16,2048]{3,2,1,0:T(8,128)(2,1)}) conditional(s32[]{:T(128)} %convert_element_type.6, () %tuple.144, (s32[24]{0:T(128)S(1)}, bf16[15,16,2048]{2,1,0:T(8,128)(2,1)S(1)}) %tuple.145), branch_computations={%region_8.8_spmd, %region_9.9_spmd} | conditional | flops 1024 | bytes 10227940 | solution.py:380
  192.3 0.0 copy-start
  192.3 0.9 copy-done
  193.2 1.8 gather_fusion
  195.1 23.3 %all_to_all.195 = bf16[4,6,16,2048]{3,2,1,0:T(8,128)(2,1)} all-to-all(bf16[4,6,16,2048]{3,2,1,0:T(8,128)(2,1)S(1)} %bitcast.137), channel_id=1, replica_groups={{0,1,2,3},{4,5,6,7},{8,9,10,11},{12,13,14,15},{16,17,18,19},{20,21,22,2..., dimensions={0} | all-to-all | bytes 3145728 | tf_op jit(solution)/shard_map/cond/branch_0_fun/cond/branch_1_fun/all_to_all | solution.py:359
  218.4 0.0 collective-permute-done.1
  218.4 2.4 collective-permute-start.2
  220.8 0.0 copy-start.6
  220.8 25.2 %conditional.2 = (bf16[4,6,16,2048]{3,2,1,0:T(8,128)(2,1)}) conditional(s32[]{:T(128)} %convert_element_type.6, () %tuple.148, (s32[24]{0:T(128)S(1)}, bf16[15,16,2048]{2,1,0:T(8,128)(2,1)}) %tuple.149), branch_computations={%region_10.10_spmd, %region_11.11_spmd} | conditional | flops 1024 | bytes 6295752 | solution.py:380
  220.8 1.9 gather_fusion.1
  222.7 23.3 %all_to_all.196 = bf16[4,6,16,2048]{3,2,1,0:T(8,128)(2,1)} all-to-all(bf16[4,6,16,2048]{3,2,1,0:T(8,128)(2,1)S(1)} %bitcast.138), channel_id=1, replica_groups={{0,1,2,3},{4,5,6,7},{8,9,10,11},{12,13,14,15},{16,17,18,19},{20,21,22,2..., dimensions={0} | all-to-all | bytes 3145728 | tf_op jit(solution)/shard_map/cond/branch_0_fun/cond/branch_1_fun/all_to_all | solution.py:359
  246.0 0.0 collective-permute-done.2
  246.0 0.5 collective-permute-start.3
  246.5 0.6 reduce_sum.47
  247.1 0.0 copy-done.6
  247.1 0.1 reduce
  247.3 0.1 reshape.240
  247.4 0.1 pad_add_fusion
  247.4 18.5 %conditional.3 = (bf16[4,6,16,1024]{3,2,1,0:T(8,128)(2,1)}, bf16[6,256,2048]{2,1,0:T(8,128)(2,1)}) conditional(s32[]{:T(128)} %convert_element_type.6, () %tuple.152, (s32[24]{0:T(128)S(1)}, bf16[15,16,1024]{2,1,0:T(8,128)(2,1)}, (), s32[4]{0:T(128)S(1)}, s32[1]{0:T(128)}, /*index=5*/bf16[4,6,16,2048]{3,2,1,0:T(8,128)(2,1)S(1)}, ...), branch_computations={%region_12.12_spmd, %region_13.13_spmd} | conditional | flops 2048 | bytes 7077908 | solution.py:380
  247.5 0.0 copy-start.16
  247.5 2.6 gather_fusion.2
  250.0 4.2 %all-to-all-start.9 = ((bf16[4,6,16,1024]{3,2,1,0:T(8,128)(2,1)}), bf16[4,6,16,1024]{3,2,1,0:T(8,128)(2,1)}, u32[]{:S(2)}, u32[]{:S(2)}) async-start(bf16[4,6,16,1024]{3,2,1,0:T(8,128)(2,1)} %bitcast.3), calls=%async_computation.9 | async-start | bytes 1572864 | tf_op jit(solution)/shard_map/cond/branch_0_fun/cond/branch_1_fun/all_to_all | solution.py:359
  254.2 0.0 copy-done.16
  254.3 0.6 gather_fusion.3
  254.9 6.2 %place_three.7 = bf16[6,256,2048]{2,1,0:T(8,128)(2,1)} custom-call(s32[1]{0:T(128)} %get-tuple-element.461.filled_ref, s32[3]{0:T(128)S(1)} %gather_fusion.3, bf16[4,6,16,2048]{3,2,1,0:T(8,128)(2,1)S(1)} %get-tuple-element.464.refs_0_, bf16[4,6,16,2048]{3,2,1,0:T(8,128)(2,1)} %get-tuple-element.465.refs_1_, bf16[4,6,16,2048]{3,2,1,0:T(8,128)(2,1)} %get-tuple-element.466.refs_2_), custom_call_target="tpu_custom_call" | custom-call | tf_op jit(solution)/shard_map/cond/branch_0_fun/cond/branch_1_fun/place_three/pallas_call | solution.py:268
  261.1 4.8 %all-to-all-done.9 = bf16[4,6,16,1024]{3,2,1,0:T(8,128)(2,1)} async-done(((bf16[4,6,16,1024]{3,2,1,0:T(8,128)(2,1)}), bf16[4,6,16,1024]{3,2,1,0:T(8,128)(2,1)}, u32[]{:S(2)}, u32[]{:S(2)}) %all-to-all-start.9) | async-done | bytes 786464 | tf_op jit(solution)/shard_map/cond/branch_0_fun/cond/branch_1_fun/all_to_all | solution.py:359
  266.0 0.6 broadcast_in_dim.153
  266.6 3.8 %all-to-all-start.28 = ((f32[16,1,384]{2,1,0:T(1,128)}), f32[16,1,384]{2,1,0:T(1,128)S(1)}, u32[]{:S(2)}, u32[]{:S(2)}) async-start(f32[16,1,384]{2,1,0:T(1,128)} %broadcast_in_dim.153), calls=%async_computation.28 | async-start | bytes 49152 | tf_op jit(solution)/shard_map/cond/branch_0_fun/all_to_all | solution.py:412
  270.4 6.6 %all-to-all-done.28 = f32[16,1,384]{2,1,0:T(1,128)S(1)} async-done(((f32[16,1,384]{2,1,0:T(1,128)}), f32[16,1,384]{2,1,0:T(1,128)S(1)}, u32[]{:S(2)}, u32[]{:S(2)}) %all-to-all-start.28) | async-done | bytes 24608 | tf_op jit(solution)/shard_map/cond/branch_0_fun/all_to_all | solution.py:412
  277.0 0.1 copy.80
  277.1 0.0 collective-permute-done.3
  277.1 1.5 gather_fusion.28
  278.6 3.5 %all-to-all-start.29 = ((bf16[4,6,16,1024]{3,2,1,0:T(8,128)(2,1)}), bf16[4,6,16,1024]{3,2,1,0:T(8,128)(2,1)S(1)}, u32[]{:S(2)}, u32[]{:S(2)}) async-start(bf16[4,6,16,1024]{3,2,1,0:T(8,128)(2,1)} %bitcast.11), calls=%async_computation.29 | async-start | bytes 1572864 | tf_op jit(solution)/shard_map/cond/branch_0_fun/all_to_all | solution.py:359
  282.1 3.5 %place.14.base_ref = bf16[6,256,2048]{2,1,0:T(8,128)(2,1)} custom-call(s32[1]{0:T(128)} %bitcast.4.filled_ref, s32[1]{0:T(128)} %bitcast.5.quarter_ref, bf16[4,6,16,1024]{3,2,1,0:T(8,128)(2,1)} %get-tuple-element.495.in_ref, bf16[6,256,2048]{2,1,0:T(8,128)(2,1)} %get-tuple-element.496.base_ref), custom_call_target="tpu_custom_call", output_to_operand_aliasing={{}: (3, {})} | custom-call | tf_op jit(solution)/shard_map/cond/branch_0_fun/place/pallas_call | solution.py:299
  285.6 0.2 copy.81
  285.8 0.8 reshape.243
  286.7 7.1 %all-to-all-done.29.in_ref = bf16[4,6,16,1024]{3,2,1,0:T(8,128)(2,1)S(1)} async-done(((bf16[4,6,16,1024]{3,2,1,0:T(8,128)(2,1)}), bf16[4,6,16,1024]{3,2,1,0:T(8,128)(2,1)S(1)}, u32[]{:S(2)}, u32[]{:S(2)}) %all-to-all-start.29) | async-done | bytes 786464 | tf_op jit(solution)/shard_map/cond/branch_0_fun/all_to_all | solution.py:359
  293.7 2.2 place.15
  (15 shorter events, 0.1 us)
Async XLA Ops:
  10.9 7.6 %copy-start.13 = (s32[48,1]{0,1:T(1,128)S(1)}, s32[48,1]{0,1:T(1,128)}, u32[]{:S(2)}) copy-start(s32[48,1]{0,1:T(1,128)} %param.85) | copy-start | bytes 580
  10.9 121.8 %copy-start.14 = (s32[8,2]{0,1:T(2,128)S(1)}, s32[8,2]{0,1:T(2,128)}, u32[]{:S(2)}) copy-start(s32[8,2]{0,1:T(2,128)} %param.82) | copy-start | bytes 196
  10.9 121.8 %copy-start.15 = (s32[16]{0:T(128)S(1)}, s32[16]{0:T(128)}, u32[]{:S(2)}) copy-start(s32[16]{0:T(128)} %param.83) | copy-start | bytes 196
  10.9 121.8 %all-to-all-start.42 = ((bf16[16,2,48,2048]{3,2,1,0:T(8,128)(2,1)}), bf16[16,2,48,2048]{3,2,1,0:T(8,128)(2,1)}, u32[]{:S(2)}, u32[]{:S(2)}) async-start(bf16[16,2,48,2048]{3,2,1,0:T(8,128)(2,1)} %prepare.1), calls=%async_computation.42 | async-start | bytes 12582912 | tf_op jit(solution)/shard_map/all_to_all | solution.py:353
  20.0 3.6 %collective-permute-start.28 = (s32[]{:T(128)}, s32[]{:T(128)}, u32[]{:S(2)}, u32[]{:S(2)}) collective-permute-start(s32[]{:T(128)} %add.321), channel_id=1, source_target_pairs={{0,16},{16,0},{1,17},{17,1},{2,18},{18,2},{3,19},{19,3},{4,20},{20... | collective-permute-start | bytes 20 | tf_op jit(solution)/shard_map/ppermute | solution.py:344
  142.7 47.9 %collective-permute-start = (bf16[15,16,2048]{2,1,0:T(8,128)(2,1)}, bf16[15,16,2048]{2,1,0:T(8,128)(2,1)S(1)}, u32[]{:S(2)}, u32[]{:S(2)}) collective-permute-start(bf16[15,16,2048]{2,1,0:T(8,128)(2,1)} %get-tuple-element.477), channel_id=1, source_target_pairs={{0,4},{1,5},{2,6},{3,7},{4,8},{5,9},{6,10},{7,11},{8,12},{9,13},{1... | collective-permute-start | bytes 2949128 | tf_op jit(solution)/shard_map/cond/branch_0_fun/ppermute | solution.py:372
  190.6 27.8 %collective-permute-start.1 = (bf16[15,16,2048]{2,1,0:T(8,128)(2,1)}, bf16[15,16,2048]{2,1,0:T(8,128)(2,1)}, u32[]{:S(2)}, u32[]{:S(2)}) collective-permute-start(bf16[15,16,2048]{2,1,0:T(8,128)(2,1)} %get-tuple-element.481), channel_id=1, source_target_pairs={{0,12},{1,13},{2,14},{3,15},{4,0},{5,1},{6,2},{7,3},{8,4},{9,5},{1... | collective-permute-start | bytes 2949128 | tf_op jit(solution)/shard_map/cond/branch_0_fun/ppermute | solution.py:372
  192.3 0.9 copy-start
  218.4 27.6 %collective-permute-start.2 = (bf16[15,16,1024]{2,1,0:T(8,128)(2,1)}, bf16[15,16,1024]{2,1,0:T(8,128)(2,1)}, u32[]{:S(2)}, u32[]{:S(2)}) collective-permute-start(bf16[15,16,1024]{2,1,0:T(8,128)(2,1)} %get-tuple-element.484), channel_id=1, source_target_pairs={{0,8},{1,9},{2,10},{3,11},{4,12},{5,13},{6,14},{7,15},{8,0},{9,1},... | collective-permute-start | bytes 1474568 | tf_op jit(solution)/shard_map/cond/branch_0_fun/ppermute | solution.py:372
  220.8 26.4 %copy-start.6 = (f32[8,48,1]{2,1,0:T(8,128)S(1)}, f32[8,48,1]{2,1,0:T(8,128)}, u32[]{:S(2)}) copy-start(f32[8,48,1]{2,1,0:T(8,128)} %get-tuple-element.487) | copy-start | bytes 4612 | tf_op jit(solution)/shard_map/cond
  246.0 31.1 %collective-permute-start.3 = (bf16[15,16,1024]{2,1,0:T(8,128)(2,1)}, bf16[15,16,1024]{2,1,0:T(8,128)(2,1)S(1)}, u32[]{:S(2)}, u32[]{:S(2)}) collective-permute-start(bf16[15,16,1024]{2,1,0:T(8,128)(2,1)} %get-tuple-element.486), channel_id=1, source_target_pairs={{0,8},{1,9},{2,10},{3,11},{4,12},{5,13},{6,14},{7,15},{8,0},{9,1},... | collective-permute-start | bytes 1474568 | tf_op jit(solution)/shard_map/cond/branch_0_fun/ppermute | solution.py:372
  247.5 6.8 %copy-start.16 = (s32[3]{0:T(128)S(1)}, s32[3]{0:T(128)}, u32[]{:S(2)}) copy-start(s32[3]{0:T(128)} %constant.429) | copy-start | bytes 40 | tf_op jit(solution)/shard_map/cond/branch_0_fun/cond
  250.0 15.9 %all-to-all-start.9 = ((bf16[4,6,16,1024]{3,2,1,0:T(8,128)(2,1)}), bf16[4,6,16,1024]{3,2,1,0:T(8,128)(2,1)}, u32[]{:S(2)}, u32[]{:S(2)}) async-start(bf16[4,6,16,1024]{3,2,1,0:T(8,128)(2,1)} %bitcast.3), calls=%async_computation.9 | async-start | bytes 1572864 | tf_op jit(solution)/shard_map/cond/branch_0_fun/cond/branch_1_fun/all_to_all | solution.py:359
  266.6 10.4 %all-to-all-start.28 = ((f32[16,1,384]{2,1,0:T(1,128)}), f32[16,1,384]{2,1,0:T(1,128)S(1)}, u32[]{:S(2)}, u32[]{:S(2)}) async-start(f32[16,1,384]{2,1,0:T(1,128)} %broadcast_in_dim.153), calls=%async_computation.28 | async-start | bytes 49152 | tf_op jit(solution)/shard_map/cond/branch_0_fun/all_to_all | solution.py:412
  278.6 15.1 %all-to-all-start.29 = ((bf16[4,6,16,1024]{3,2,1,0:T(8,128)(2,1)}), bf16[4,6,16,1024]{3,2,1,0:T(8,128)(2,1)S(1)}, u32[]{:S(2)}, u32[]{:S(2)}) async-start(bf16[4,6,16,1024]{3,2,1,0:T(8,128)(2,1)} %bitcast.11), calls=%async_computation.29 | async-start | bytes 1572864 | tf_op jit(solution)/shard_map/cond/branch_0_fun/all_to_all | solution.py:359

commit v10 on v9

--- a/solution.py
+++ b/solution.py
@@ -412,7 +412,6 @@
         similarity = lax.all_to_all(
             jnp.broadcast_to(part, (devices, part.shape[1])), "expert", 0, 0, tiled=True
         )
-        rest_on, similarity = in_order(rest_on, similarity)
         from_rest = spread(rest_on, from_list)
         merged = place(filled, origins[2:3], from_two, 0, merged)
         merged = place(filled, origins[2:3], from_rest, 1, merged)

time: 298 us -> 297 us (level)
    all_to_all x1, waiting for transfers between devices: 6.55 us -> 2.75 us  [deal(): lax.all_to_all(jnp.broadcast_to(part, (devices, part.shape[1])), 'expert'...]
    ppermute x4, waiting for transfers between devices: 0.01 us -> 3.27 us  [permuted(): return lax.ppermute(chunk, 'expert', ring)]
  transfers between devices with their start and end apart: 9 -> 9, of which waited for: 5 -> 7; matrix products, arithmetic and copies ran while one was open for 4% -> 4% of each run, Pallas kernels for 3% -> 3%
where the time goes in v10:
time: 297 us
  waiting for transfers between devices  127 us (43%)
  blocking collectives  71 us (24%)
  starting transfers between devices  51.4 us (17%)
  Pallas kernels  31.2 us (11%)
  local copies, waits for them, and re-layouts  11.4 us (4%)
    all_to_all x1, waiting for transfers between devices, body(): lax.all_to_all(outgoing, 'expert', split_axis=0, concat_axis=0, tiled=True)  108 us
    all_to_all x3, blocking collectives, within_quarter(): lax.all_to_all(value, 'expert', split_axis=0, concat_axis=0, tiled=True,...  71 us
    ppermute x4, starting transfers between devices, permuted(): return lax.ppermute(chunk, 'expert', ring)  29.8 us
    all_to_all x2, waiting for transfers between devices, within_quarter(): lax.all_to_all(value, 'expert', split_axis=0, concat_axis=0, tiled=True,...  11.9 us
    pallas_call x1, Pallas kernels, prepare(): pl.pallas_call(prepare_kernel, grid_spec=grid_spec, out_shape=jax.ShapeDt...  10.3 us
    pallas_call x1, Pallas kernels, merge(): pl.pallas_call(merge_kernel, grid_spec=grid_spec, out_shape=[jax.ShapeDty...  9.19 us
    gather x4, local copies, waits for them, and re-layouts, spread(): return within_quarter(jnp.take(chunk, from_list, axis=0, mode='clip'))  7.92 us
    all_to_all x2, starting transfers between devices, within_quarter(): lax.all_to_all(value, 'expert', split_axis=0, concat_axis=0, tiled=True,...  7.68 us
  transfers between devices with their start and end apart: 9, of which 7 were waited for; matrix products, arithmetic and copies ran while one was open for 4% of the time, Pallas kernels for 3%

profile of v10, /device:TPU:0, one launch (start us, length us, event | category | flops | bytes accessed | tf_op | source)
XLA Modules:
  0.0 297.2 jit_solution(3677989975842001372)
XLA Ops:
  0.6 10.3 %prepare.1 = bf16[16,2,48,2048]{3,2,1,0:T(8,128)(2,1)} custom-call(s32[2,8]{1,0:T(2,128)} %bitcast.174, s32[1]{0:T(128)} %bitcast.101.me_ref, s32[8,768]{1,0:T(8,128)} %order_ref.1, bf16[2048,768]{1,0:T(8,128)(2,1)} %bitcast.144, bf16[2048,768]{1,0:T(8,128)(2,1)} %bitcast.145, bf16[6,16]{1,0:T(8,128)(2,1)} %bitcast.182, bf16[6,16]{1,0:T(8,128)(2,1)} %bitcast.183), custom_call_target="tpu_custom_call" | custom-call | tf_op jit(solution)/shard_map/prepare/pallas_call | solution.py:94
  10.9 0.0 copy-start.13
  10.9 0.0 copy-start.14
  10.9 0.0 copy-start.15
  10.9 7.5 %all-to-all-start.42 = ((bf16[16,2,48,2048]{3,2,1,0:T(8,128)(2,1)}), bf16[16,2,48,2048]{3,2,1,0:T(8,128)(2,1)}, u32[]{:S(2)}, u32[]{:S(2)}) async-start(bf16[16,2,48,2048]{3,2,1,0:T(8,128)(2,1)} %prepare.1), calls=%async_computation.42 | async-start | bytes 12582912 | tf_op jit(solution)/shard_map/all_to_all | solution.py:353
  18.5 0.0 copy-done.13
  18.6 0.2 select_reduce_fusion.14
  18.8 0.6 reduce_max.9
  20.0 2.9 collective-permute-start.28
  22.9 0.7 collective-permute-done.28
  24.2 108.5 %all-to-all-done.42 = bf16[16,2,48,2048]{3,2,1,0:T(8,128)(2,1)} async-done(((bf16[16,2,48,2048]{3,2,1,0:T(8,128)(2,1)}), bf16[16,2,48,2048]{3,2,1,0:T(8,128)(2,1)}, u32[]{:S(2)}, u32[]{:S(2)}) %all-to-all-start.42) | async-done | bytes 6291488 | tf_op jit(solution)/shard_map/all_to_all | solution.py:353
  132.7 0.0 copy-done.14
  132.7 0.0 copy-done.15
  132.7 164.3 %conditional.29 = (bf16[6,256,2048]{2,1,0:T(8,128)(2,1)}, f32[8,768]{1,0:T(8,128)}) conditional(s32[]{:T(128)} %clamp.3, (s32[]{:T(128)}, s32[8,2]{0,1:T(2,128)S(1)}, s32[16]{0:T(128)S(1)}, s32[48]{0:T(128)S(1)}, s32[48]{0:T(128)S(1)}, /*index=5*/bf16[16,2,48,2048]{3,2,1,0:T(8,128)(2,1)}, s32[]{:T(128)}, ...), branch_computations={%region_5.14_spmd, %region_14.23_spmd, %region_23.32_spmd, %region... | conditional | flops 19365 | bytes 48015384 | solution.py:422
  133.0 0.2 select_reduce_fusion.4
  133.1 0.5 fusion.11
  133.7 9.2 %merge.9 = (f32[8,48,1]{2,1,0:T(8,128)}, bf16[24,16,2048]{2,1,0:T(8,128)(2,1)}, bf16[17,16,2048]{2,1,0:T(8,128)(2,1)}, bf16[17,16,1024]{2,1,0:T(8,128)(2,1)}, bf...) custom-call(s32[2,8]{1,0:T(2,128)S(1)} %bitcast.177, s32[16]{0:T(128)S(1)} %get-tuple-element.818.counts_ref, ...), custom_call_target="tpu_custom_call" | custom-call | tf_op jit(solution)/shard_map/cond/branch_2_fun/merge/pallas_call | solution.py:232
  142.9 23.5 %collective-permute-start.8 = (bf16[17,16,2048]{2,1,0:T(8,128)(2,1)}, bf16[17,16,2048]{2,1,0:T(8,128)(2,1)S(1)}, u32[]{:S(2)}, u32[]{:S(2)}) collective-permute-start(bf16[17,16,2048]{2,1,0:T(8,128)(2,1)} %get-tuple-element.559), channel_id=1, source_target_pairs={{0,4},{1,5},{2,6},{3,7},{4,8},{5,9},{6,10},{7,11},{8,12},{9,13},{1... | collective-permute-start | bytes 3342344 | tf_op jit(solution)/shard_map/cond/branch_2_fun/ppermute | solution.py:372
  166.3 24.4 %conditional.8 = (bf16[4,6,16,2048]{3,2,1,0:T(8,128)(2,1)S(1)}) conditional(s32[]{:T(128)} %convert_element_type.9, () %tuple.175, bf16[24,16,2048]{2,1,0:T(8,128)(2,1)} %get-tuple-element.561), branch_computations={%region_24.24_spmd, %region_25.25_spmd} | conditional | bytes 3145736 | solution.py:380
  166.3 24.4 %all_to_all.186 = bf16[4,6,16,2048]{3,2,1,0:T(8,128)(2,1)S(1)} all-to-all(bf16[4,6,16,2048]{3,2,1,0:T(8,128)(2,1)} %bitcast.148), channel_id=1, replica_groups={{0,1,2,3},{4,5,6,7},{8,9,10,11},{12,13,14,15},{16,17,18,19},{20,21,22,2..., dimensions={0} | all-to-all | bytes 3145728 | tf_op jit(solution)/shard_map/cond/branch_2_fun/cond/branch_1_fun/all_to_all | solution.py:359
  190.8 0.0 collective-permute-done.8
  190.8 4.4 %collective-permute-start.9 = (bf16[17,16,2048]{2,1,0:T(8,128)(2,1)}, bf16[17,16,2048]{2,1,0:T(8,128)(2,1)}, u32[]{:S(2)}, u32[]{:S(2)}) collective-permute-start(bf16[17,16,2048]{2,1,0:T(8,128)(2,1)} %get-tuple-element.563), channel_id=1, source_target_pairs={{0,12},{1,13},{2,14},{3,15},{4,0},{5,1},{6,2},{7,3},{8,4},{9,5},{1... | collective-permute-start | bytes 3342344 | tf_op jit(solution)/shard_map/cond/branch_2_fun/ppermute | solution.py:372
  195.2 0.1 select_reduce_fusion.5
  195.3 26.2 %conditional.9 = (bf16[4,6,16,2048]{3,2,1,0:T(8,128)(2,1)}) conditional(s32[]{:T(128)} %convert_element_type.9, () %tuple.178, (s32[24]{0:T(128)S(1)}, bf16[17,16,2048]{2,1,0:T(8,128)(2,1)S(1)}) %tuple.179), branch_computations={%region_26.26_spmd, %region_27.27_spmd} | conditional | flops 1024 | bytes 10752228 | solution.py:380
  195.3 0.0 copy-start.2
  195.4 1.0 copy-done.2
  196.3 1.9 gather_fusion.8
  198.2 23.3 %all_to_all.187 = bf16[4,6,16,2048]{3,2,1,0:T(8,128)(2,1)} all-to-all(bf16[4,6,16,2048]{3,2,1,0:T(8,128)(2,1)S(1)} %bitcast.134), channel_id=1, replica_groups={{0,1,2,3},{4,5,6,7},{8,9,10,11},{12,13,14,15},{16,17,18,19},{20,21,22,2..., dimensions={0} | all-to-all | bytes 3145728 | tf_op jit(solution)/shard_map/cond/branch_2_fun/cond/branch_1_fun/all_to_all | solution.py:359
  221.5 0.0 collective-permute-done.9
  221.5 0.5 collective-permute-start.10
  222.0 0.0 copy-start.8
  222.0 25.3 %conditional.10 = (bf16[4,6,16,2048]{3,2,1,0:T(8,128)(2,1)}) conditional(s32[]{:T(128)} %convert_element_type.9, () %tuple.182, (s32[24]{0:T(128)S(1)}, bf16[17,16,2048]{2,1,0:T(8,128)(2,1)}) %tuple.183), branch_computations={%region_28.28_spmd, %region_29.29_spmd} | conditional | flops 1024 | bytes 6295752 | solution.py:380
  222.0 1.9 gather_fusion.9
  224.0 23.3 %all_to_all.188 = bf16[4,6,16,2048]{3,2,1,0:T(8,128)(2,1)} all-to-all(bf16[4,6,16,2048]{3,2,1,0:T(8,128)(2,1)S(1)} %bitcast.135), channel_id=1, replica_groups={{0,1,2,3},{4,5,6,7},{8,9,10,11},{12,13,14,15},{16,17,18,19},{20,21,22,2..., dimensions={0} | all-to-all | bytes 3145728 | tf_op jit(solution)/shard_map/cond/branch_2_fun/cond/branch_1_fun/all_to_all | solution.py:359
  247.3 1.0 collective-permute-done.10
  248.3 1.4 collective-permute-start.11
  249.7 0.6 reduce_sum.49
  250.3 0.0 copy-done.8
  250.3 0.1 reduce.4
  250.4 0.1 reshape.264
  250.5 0.1 pad_add_fusion.2
  250.6 18.5 %conditional.11 = (bf16[4,6,16,1024]{3,2,1,0:T(8,128)(2,1)}, bf16[6,256,2048]{2,1,0:T(8,128)(2,1)}) conditional(s32[]{:T(128)} %convert_element_type.9, () %tuple.186, (s32[24]{0:T(128)S(1)}, bf16[17,16,1024]{2,1,0:T(8,128)(2,1)}, (), s32[4]{0:T(128)S(1)}, s32[1]{0:T(128)}, /*index=5*/bf16[4,6,16,2048]{3,2,1,0:T(8,128)(2,1)S(1)}, ...), branch_computations={%region_30.30_spmd, %region_31.31_spmd} | conditional | flops 2048 | bytes 7077908 | solution.py:380
  250.6 0.0 copy-start.18
  250.6 2.6 gather_fusion.10
  253.2 4.2 %all-to-all-start.15 = ((bf16[4,6,16,1024]{3,2,1,0:T(8,128)(2,1)}), bf16[4,6,16,1024]{3,2,1,0:T(8,128)(2,1)}, u32[]{:S(2)}, u32[]{:S(2)}) async-start(bf16[4,6,16,1024]{3,2,1,0:T(8,128)(2,1)} %bitcast.31), calls=%async_computation.15 | async-start | bytes 1572864 | tf_op jit(solution)/shard_map/cond/branch_2_fun/cond/branch_1_fun/all_to_all | solution.py:359
  257.4 0.0 copy-done.18
  257.4 0.6 gather_fusion.11
  258.1 6.1 %place_three.9 = bf16[6,256,2048]{2,1,0:T(8,128)(2,1)} custom-call(s32[1]{0:T(128)} %get-tuple-element.543.filled_ref, s32[3]{0:T(128)S(1)} %gather_fusion.11, bf16[4,6,16,2048]{3,2,1,0:T(8,128)(2,1)S(1)} %get-tuple-element.546.refs_0_, bf16[4,6,16,2048]{3,2,1,0:T(8,128)(2,1)} %get-tuple-element.547.refs_1_, bf16[4,6,16,2048]{3,2,1,0:T(8,128)(2,1)} %get-tuple-element.548.refs_2_), custom_call_target="tpu_custom_call" | custom-call | tf_op jit(solution)/shard_map/cond/branch_2_fun/cond/branch_1_fun/place_three/pallas_call | solution.py:268
  264.2 4.9 %all-to-all-done.15 = bf16[4,6,16,1024]{3,2,1,0:T(8,128)(2,1)} async-done(((bf16[4,6,16,1024]{3,2,1,0:T(8,128)(2,1)}), bf16[4,6,16,1024]{3,2,1,0:T(8,128)(2,1)}, u32[]{:S(2)}, u32[]{:S(2)}) %all-to-all-start.15) | async-done | bytes 786464 | tf_op jit(solution)/shard_map/cond/branch_2_fun/cond/branch_1_fun/all_to_all | solution.py:359
  269.2 0.6 broadcast_in_dim.166
  269.8 3.5 %all-to-all-start.33 = ((f32[16,1,384]{2,1,0:T(1,128)}), f32[16,1,384]{2,1,0:T(1,128)S(1)}, u32[]{:S(2)}, u32[]{:S(2)}) async-start(f32[16,1,384]{2,1,0:T(1,128)} %broadcast_in_dim.166), calls=%async_computation.33 | async-start | bytes 49152 | tf_op jit(solution)/shard_map/cond/branch_2_fun/all_to_all | solution.py:412
  273.3 2.3 collective-permute-done.11
  275.6 1.5 gather_fusion.30
  277.1 2.7 all-to-all-done.33
  279.8 3.5 %all-to-all-start.32 = ((bf16[4,6,16,1024]{3,2,1,0:T(8,128)(2,1)}), bf16[4,6,16,1024]{3,2,1,0:T(8,128)(2,1)S(1)}, u32[]{:S(2)}, u32[]{:S(2)}) async-start(bf16[4,6,16,1024]{3,2,1,0:T(8,128)(2,1)} %bitcast.35), calls=%async_computation.32 | async-start | bytes 1572864 | tf_op jit(solution)/shard_map/cond/branch_2_fun/all_to_all | solution.py:359
  283.3 3.5 %place.18.base_ref = bf16[6,256,2048]{2,1,0:T(8,128)(2,1)} custom-call(s32[1]{0:T(128)} %bitcast.32.filled_ref, s32[1]{0:T(128)} %bitcast.33.quarter_ref, bf16[4,6,16,1024]{3,2,1,0:T(8,128)(2,1)} %get-tuple-element.575.in_ref, bf16[6,256,2048]{2,1,0:T(8,128)(2,1)} %get-tuple-element.576.base_ref), custom_call_target="tpu_custom_call", output_to_operand_aliasing={{}: (3, {})} | custom-call | tf_op jit(solution)/shard_map/cond/branch_2_fun/place/pallas_call | solution.py:299
  286.8 0.1 copy.84
  286.9 0.2 copy.85
  287.1 0.8 reshape.266
  288.0 7.0 %all-to-all-done.32.in_ref = bf16[4,6,16,1024]{3,2,1,0:T(8,128)(2,1)S(1)} async-done(((bf16[4,6,16,1024]{3,2,1,0:T(8,128)(2,1)}), bf16[4,6,16,1024]{3,2,1,0:T(8,128)(2,1)S(1)}, u32[]{:S(2)}, u32[]{:S(2)}) %all-to-all-start.32) | async-done | bytes 786464 | tf_op jit(solution)/shard_map/cond/branch_2_fun/all_to_all | solution.py:359
  294.9 2.1 place.19
  (15 shorter events, 0.1 us)
Async XLA Ops:
  10.9 7.6 %copy-start.13 = (s32[48,1]{0,1:T(1,128)S(1)}, s32[48,1]{0,1:T(1,128)}, u32[]{:S(2)}) copy-start(s32[48,1]{0,1:T(1,128)} %param.85) | copy-start | bytes 580
  10.9 121.8 %copy-start.14 = (s32[8,2]{0,1:T(2,128)S(1)}, s32[8,2]{0,1:T(2,128)}, u32[]{:S(2)}) copy-start(s32[8,2]{0,1:T(2,128)} %param.82) | copy-start | bytes 196
  10.9 121.8 %copy-start.15 = (s32[16]{0:T(128)S(1)}, s32[16]{0:T(128)}, u32[]{:S(2)}) copy-start(s32[16]{0:T(128)} %param.83) | copy-start | bytes 196
  10.9 121.8 %all-to-all-start.42 = ((bf16[16,2,48,2048]{3,2,1,0:T(8,128)(2,1)}), bf16[16,2,48,2048]{3,2,1,0:T(8,128)(2,1)}, u32[]{:S(2)}, u32[]{:S(2)}) async-start(bf16[16,2,48,2048]{3,2,1,0:T(8,128)(2,1)} %prepare.1), calls=%async_computation.42 | async-start | bytes 12582912 | tf_op jit(solution)/shard_map/all_to_all | solution.py:353
  20.0 3.6 %collective-permute-start.28 = (s32[]{:T(128)}, s32[]{:T(128)}, u32[]{:S(2)}, u32[]{:S(2)}) collective-permute-start(s32[]{:T(128)} %add.321), channel_id=1, source_target_pairs={{0,16},{16,0},{1,17},{17,1},{2,18},{18,2},{3,19},{19,3},{4,20},{20... | collective-permute-start | bytes 20 | tf_op jit(solution)/shard_map/ppermute | solution.py:344
  142.9 47.9 %collective-permute-start.8 = (bf16[17,16,2048]{2,1,0:T(8,128)(2,1)}, bf16[17,16,2048]{2,1,0:T(8,128)(2,1)S(1)}, u32[]{:S(2)}, u32[]{:S(2)}) collective-permute-start(bf16[17,16,2048]{2,1,0:T(8,128)(2,1)} %get-tuple-element.559), channel_id=1, source_target_pairs={{0,4},{1,5},{2,6},{3,7},{4,8},{5,9},{6,10},{7,11},{8,12},{9,13},{1... | collective-permute-start | bytes 3342344 | tf_op jit(solution)/shard_map/cond/branch_2_fun/ppermute | solution.py:372
  190.8 30.7 %collective-permute-start.9 = (bf16[17,16,2048]{2,1,0:T(8,128)(2,1)}, bf16[17,16,2048]{2,1,0:T(8,128)(2,1)}, u32[]{:S(2)}, u32[]{:S(2)}) collective-permute-start(bf16[17,16,2048]{2,1,0:T(8,128)(2,1)} %get-tuple-element.563), channel_id=1, source_target_pairs={{0,12},{1,13},{2,14},{3,15},{4,0},{5,1},{6,2},{7,3},{8,4},{9,5},{1... | collective-permute-start | bytes 3342344 | tf_op jit(solution)/shard_map/cond/branch_2_fun/ppermute | solution.py:372
  195.3 1.0 copy-start.2
  221.5 26.8 %collective-permute-start.10 = (bf16[17,16,1024]{2,1,0:T(8,128)(2,1)}, bf16[17,16,1024]{2,1,0:T(8,128)(2,1)}, u32[]{:S(2)}, u32[]{:S(2)}) collective-permute-start(bf16[17,16,1024]{2,1,0:T(8,128)(2,1)} %get-tuple-element.566), channel_id=1, source_target_pairs={{0,8},{1,9},{2,10},{3,11},{4,12},{5,13},{6,14},{7,15},{8,0},{9,1},... | collective-permute-start | bytes 1671176 | tf_op jit(solution)/shard_map/cond/branch_2_fun/ppermute | solution.py:372
  222.0 28.3 %copy-start.8 = (f32[8,48,1]{2,1,0:T(8,128)S(1)}, f32[8,48,1]{2,1,0:T(8,128)}, u32[]{:S(2)}) copy-start(f32[8,48,1]{2,1,0:T(8,128)} %get-tuple-element.569) | copy-start | bytes 4612 | tf_op jit(solution)/shard_map/cond
  248.3 27.3 %collective-permute-start.11 = (bf16[17,16,1024]{2,1,0:T(8,128)(2,1)}, bf16[17,16,1024]{2,1,0:T(8,128)(2,1)S(1)}, u32[]{:S(2)}, u32[]{:S(2)}) collective-permute-start(bf16[17,16,1024]{2,1,0:T(8,128)(2,1)} %get-tuple-element.568), channel_id=1, source_target_pairs={{0,8},{1,9},{2,10},{3,11},{4,12},{5,13},{6,14},{7,15},{8,0},{9,1},... | collective-permute-start | bytes 1671176 | tf_op jit(solution)/shard_map/cond/branch_2_fun/ppermute | solution.py:372
  250.6 6.8 %copy-start.18 = (s32[3]{0:T(128)S(1)}, s32[3]{0:T(128)}, u32[]{:S(2)}) copy-start(s32[3]{0:T(128)} %constant.423) | copy-start | bytes 40 | tf_op jit(solution)/shard_map/cond/branch_2_fun/cond
  253.2 15.9 %all-to-all-start.15 = ((bf16[4,6,16,1024]{3,2,1,0:T(8,128)(2,1)}), bf16[4,6,16,1024]{3,2,1,0:T(8,128)(2,1)}, u32[]{:S(2)}, u32[]{:S(2)}) async-start(bf16[4,6,16,1024]{3,2,1,0:T(8,128)(2,1)} %bitcast.31), calls=%async_computation.15 | async-start | bytes 1572864 | tf_op jit(solution)/shard_map/cond/branch_2_fun/cond/branch_1_fun/all_to_all | solution.py:359
  269.8 10.0 %all-to-all-start.33 = ((f32[16,1,384]{2,1,0:T(1,128)}), f32[16,1,384]{2,1,0:T(1,128)S(1)}, u32[]{:S(2)}, u32[]{:S(2)}) async-start(f32[16,1,384]{2,1,0:T(1,128)} %broadcast_in_dim.166), calls=%async_computation.33 | async-start | bytes 49152 | tf_op jit(solution)/shard_map/cond/branch_2_fun/all_to_all | solution.py:412
  279.8 15.1 %all-to-all-start.32 = ((bf16[4,6,16,1024]{3,2,1,0:T(8,128)(2,1)}), bf16[4,6,16,1024]{3,2,1,0:T(8,128)(2,1)S(1)}, u32[]{:S(2)}, u32[]{:S(2)}) async-start(bf16[4,6,16,1024]{3,2,1,0:T(8,128)(2,1)} %bitcast.35), calls=%async_computation.32 | async-start | bytes 1572864 | tf_op jit(solution)/shard_map/cond/branch_2_fun/all_to_all | solution.py:359
